TPU v7x, 32 devices: a whole 2x2x4 slice. The times are simulated.
32 devices in a mesh: seq: 8 (over z, x), row: 4 (over y, core).
Axes of the slice: x: 2, y: 2, z: 4, core: 2. Of those that a mesh axis runs over, the one named last changes fastest.
Arguments:
- tokens: bfloat16 [4, 4096, 2048], P('row', 'seq'), may hold values from -6 to 6
- resets: int32 [4, 4096], P('row', 'seq'), may hold values from 0 to 1, as said below
- cotangent: bfloat16 [4, 4096, 2048], P('row', 'seq'), may hold values from -6 to 6
- weight: bfloat16 [2, 2048, 6144], P(None, ('seq', 'row')), may hold values from -0.125 to 0.125
- norm_gain: bfloat16 [2, 2048], P(None, ('seq', 'row')), may hold values from 0.5 to 1.5
- norm_bias: bfloat16 [2, 2048], P(None, ('seq', 'row')), may hold values from -1 to 1
- forget_peep: bfloat16 [2, 2048], P(None, ('seq', 'row')), may hold values from -1 to 1
- reset_peep: bfloat16 [2, 2048], P(None, ('seq', 'row')), may hold values from -2 to 2
- forget_bias: bfloat16 [2, 2048], P(None, ('seq', 'row')), may hold values from 3.5 to 10.5
- reset_bias: bfloat16 [2, 2048], P(None, ('seq', 'row')), may hold values from -1 to 1
Outputs:
- result: bfloat16 [4, 4096, 2048], P('row', 'seq')
- input_grad: bfloat16 [4, 4096, 2048], P('row', 'seq')
- weight_grad: float32 [2, 2048, 6144], P(None, ('seq', 'row'))
- norm_gain_grad: float32 [2, 2048], P(None, ('seq', 'row'))
- norm_bias_grad: float32 [2, 2048], P(None, ('seq', 'row'))
- forget_peep_grad: float32 [2, 2048], P(None, ('seq', 'row'))
- reset_peep_grad: float32 [2, 2048], P(None, ('seq', 'row'))
- forget_bias_grad: float32 [2, 2048], P(None, ('seq', 'row'))
- reset_bias_grad: float32 [2, 2048], P(None, ('seq', 'row'))
Inputs may be any that keep to these rules, and one draw needn't show every extreme that they name: `resets`: position 0 of every row is 1. In each row one sentence starts within the first 512 positions and runs into the last 512 positions.
All inputs are finite; a program needn't handle non-finite values.
Results may differ from a plain program's by a relative error of at most 0.0045.
Values may be sent and summed in bfloat16 or wider, within the bound.
A program may use at most 256 MiB of HBM per device.

v0:
```python
import jax
import jax.numpy as jnp
from jax import lax
from jax.sharding import PartitionSpec as P

epsilon = 1e-05


def entering(value, axis, join, neutral, backward):
    count, mine = (lax.axis_size(axis), lax.axis_index(axis))
    pieces = jax.tree.map(lambda part: lax.all_gather(part, axis), value)
    if backward:
        pieces = jax.tree.map(lambda part: part[::-1], pieces)
        mine = count - 1 - mine
    subtotal = jax.tree.map(
        lambda part, zero: jnp.full_like(part, 0) + jnp.asarray(zero, part.dtype), value, neutral
    )

    def step(position, subtotal):
        longer = join(subtotal, jax.tree.map(lambda part: part[position], pieces))
        return jax.tree.map(lambda new, old: jnp.where(position < mine, new, old), longer, subtotal)

    return lax.fori_loop(0, count - 1, step, subtotal)


def affine_join(earlier, later_item):
    first_scale, first_shift = earlier
    second_scale, second_shift = later_item
    return (first_scale * second_scale, second_scale * first_shift + second_shift)


def local_norm(values, gain_row, shift_row):
    center = values - jnp.mean(values, axis=-1, keepdims=True)
    variance = jnp.mean(center * center, axis=-1, keepdims=True)
    inverse = lax.rsqrt(variance + epsilon)
    normed = center * inverse
    return (normed, inverse, normed * gain_row + shift_row)


def body(
    tokens,
    resets,
    cotangent,
    weight,
    norm_gain,
    norm_bias,
    forget_peep,
    reset_peep,
    forget_bias,
    reset_bias,
):
    keep_mask = (1 - resets).astype(jnp.float32)[:, :, None]
    model_width = tokens.shape[-1]
    layers = weight.shape[0]
    current = tokens.astype(jnp.float32)
    stored = []
    for depth_index in range(layers):
        vectors = jnp.stack(
            [
                norm_gain[depth_index],
                norm_bias[depth_index],
                forget_peep[depth_index],
                reset_peep[depth_index],
                forget_bias[depth_index],
                reset_bias[depth_index],
            ],
            axis=1,
        )
        full_weight, full_vectors = (
            lax.all_gather(weight[depth_index], ("seq", "row"), axis=0, tiled=True),
            lax.all_gather(vectors, ("seq", "row"), axis=0, tiled=True),
        )
        vector_values = full_vectors.astype(jnp.float32)
        normed, inverse, features = local_norm(current, vector_values[:, 0], vector_values[:, 1])
        features_low = features.astype(jnp.bfloat16)
        projected = jnp.einsum(
            "rtd,de->rte", features_low, full_weight, preferred_element_type=jnp.float32
        )
        candidate = projected[..., :model_width]
        forget_pre = projected[..., model_width : 2 * model_width]
        reset_pre = projected[..., 2 * model_width :]
        forget_logit = forget_pre + vector_values[:, 2] * features + vector_values[:, 4]
        forget = jax.nn.sigmoid(forget_logit)
        complement = jax.nn.sigmoid(-forget_logit)
        decay_rate = forget * keep_mask
        scale_run, state_run = lax.associative_scan(
            affine_join, (decay_rate, complement * candidate), axis=1
        )
        group_ends = (scale_run[:, -1], state_run[:, -1])
        identity = (jnp.ones_like(group_ends[0]), jnp.zeros_like(group_ends[1]))
        incoming = entering(group_ends, "seq", affine_join, identity, False)[1]
        states = state_run + scale_run * incoming[:, None]
        previous = keep_mask * jnp.concatenate([incoming[:, None], states[:, :-1]], axis=1)
        reset_gate = jax.nn.sigmoid(
            reset_pre + vector_values[:, 3] * previous + vector_values[:, 5]
        )
        output = reset_gate * states + (1.0 - reset_gate) * current
        kept_weight = None
        stored.append(
            (
                current,
                normed,
                inverse,
                features,
                features_low,
                candidate,
                forget,
                complement,
                decay_rate,
                states,
                previous,
                reset_gate,
                vector_values,
                kept_weight,
            )
        )
        current = output
    result = current.astype(jnp.bfloat16)
    upstream = cotangent.astype(jnp.float32)
    weight_parts = [None] * layers
    vector_parts = [None] * layers
    for depth_index in reversed(range(layers)):
        (
            inputs,
            normed,
            inverse,
            features,
            features_low,
            candidate,
            forget,
            complement,
            decay_rate,
            states,
            previous,
            reset_gate,
            vector_values,
            kept_weight,
        ) = stored[depth_index]
        full_weight = lax.all_gather(weight[depth_index], ("seq", "row"), axis=0, tiled=True)
        reset_grad = upstream * (states - inputs) * reset_gate * (1.0 - reset_gate)
        direct = upstream * reset_gate
        local_term = keep_mask * vector_values[:, 3] * reset_grad + decay_rate * direct
        suffix_scale, suffix_state = lax.associative_scan(
            affine_join, (decay_rate, local_term), reverse=True, axis=1
        )
        back_ends = (suffix_scale[:, 0], suffix_state[:, 0])
        identity = (jnp.ones_like(back_ends[0]), jnp.zeros_like(back_ends[1]))
        incoming_back = entering(back_ends, "seq", affine_join, identity, True)[1]
        adjoint = suffix_state + suffix_scale * incoming_back[:, None]
        following = jnp.concatenate([adjoint[:, 1:], incoming_back[:, None]], axis=1)
        state_grad = direct + following
        cand_grad = state_grad * complement
        forget_grad = state_grad * (
            previous * forget * (1.0 - forget) - candidate * complement * (1.0 - complement)
        )
        projected_grad = jnp.concatenate([cand_grad, forget_grad, reset_grad], axis=-1).astype(
            jnp.bfloat16
        )
        weight_term = jnp.einsum(
            "rtd,rte->de", features_low, projected_grad, preferred_element_type=jnp.float32
        )
        feature_grad = (
            jnp.einsum(
                "rte,de->rtd", projected_grad, full_weight, preferred_element_type=jnp.float32
            )
            + forget_grad * vector_values[:, 2]
        )
        vector_sums = jnp.stack(
            [
                jnp.sum(feature_grad * normed, axis=(0, 1)),
                jnp.sum(feature_grad, axis=(0, 1)),
                jnp.sum(forget_grad * features, axis=(0, 1)),
                jnp.sum(reset_grad * previous, axis=(0, 1)),
                jnp.sum(forget_grad, axis=(0, 1)),
                jnp.sum(reset_grad, axis=(0, 1)),
            ],
            axis=1,
        )
        weight_part, vector_part = (
            lax.psum_scatter(weight_term, ("seq", "row"), scatter_dimension=0, tiled=True),
            lax.psum_scatter(vector_sums, ("seq", "row"), scatter_dimension=0, tiled=True),
        )
        weight_parts[depth_index] = weight_part
        vector_parts[depth_index] = vector_part
        scaled = feature_grad * vector_values[:, 0]
        norm_grad = inverse * (
            scaled
            - jnp.mean(scaled, axis=-1, keepdims=True)
            - normed * jnp.mean(scaled * normed, axis=-1, keepdims=True)
        )
        upstream = upstream * (1.0 - reset_gate) + norm_grad
    input_grad = upstream.astype(jnp.bfloat16)
    weight_out = jnp.stack(weight_parts, axis=0)
    vector_out = jnp.stack(vector_parts, axis=0)
    return (
        result,
        input_grad,
        weight_out,
        vector_out[:, :, 0],
        vector_out[:, :, 1],
        vector_out[:, :, 2],
        vector_out[:, :, 3],
        vector_out[:, :, 4],
        vector_out[:, :, 5],
    )


def solution(mesh):
    return jax.shard_map(
        body,
        mesh=mesh,
        in_specs=(
            P("row", "seq", None),
            P("row", "seq"),
            P("row", "seq", None),
            P(None, ("seq", "row"), None),
            P(None, ("seq", "row")),
            P(None, ("seq", "row")),
            P(None, ("seq", "row")),
            P(None, ("seq", "row")),
            P(None, ("seq", "row")),
            P(None, ("seq", "row")),
        ),
        out_specs=(
            P("row", "seq", None),
            P("row", "seq", None),
            P(None, ("seq", "row"), None),
            P(None, ("seq", "row")),
            P(None, ("seq", "row")),
            P(None, ("seq", "row")),
            P(None, ("seq", "row")),
            P(None, ("seq", "row")),
            P(None, ("seq", "row")),
        ),
        check_vma=False,
    )
```

profile of v0, /device:TPU:0, one launch (start us, length us, event | category | flops | bytes accessed | tf_op | source)
XLA Modules:
  0.0 3001.2 jit_solution(17624649867894252370)
XLA Ops:
  11.1 44.1 %all-gather.2 = bf16[32,64,6]{1,2,0:T(8,128)(2,1)S(1)} all-gather(bf16[1,64,6]{1,2,0:T(8,128)(2,1)S(1)} %bitcast.246), channel_id=1, replica_groups=mesh['seq'=8,'row'=4] {'seq','row'}, dimensions={0}, use_global_device_ids=true | all-gather | bytes 25344 | tf_op jit(solution)/shard_map/all_gather | solution.py:71
  55.3 37.6 %all-gather.3 = bf16[32,64,6]{1,2,0:T(8,128)(2,1)S(1)} all-gather(bf16[1,64,6]{1,2,0:T(8,128)(2,1)S(1)} %bitcast.247), channel_id=1, replica_groups=mesh['seq'=8,'row'=4] {'seq','row'}, dimensions={0}, use_global_device_ids=true | all-gather | bytes 25344 | tf_op jit(solution)/shard_map/all_gather | solution.py:71
  94.8 74.6 %all-gather.7.cloned.1.call-done = bf16[1,2048,6144]{2,1,0:T(8,128)(2,1)} async-done(((bf16[1,64,6144]{2,1,0:T(8,128)(2,1)}), bf16[1,2048,6144]{2,1,0:T(8,128)(2,1)}) %all-gather.7.cloned.1.call-update) | async-done | bytes 25165840 | tf_op jit(solution)/shard_map/all_gather | solution.py:70
  169.4 20.8 fusion.8
  527.0 30.5 %all_gather.40 = f32[8,1,2048]{2,1,0:T(1,128)S(1)} all-gather(f32[1,1,2048]{2,1,0:T(1,128)S(1)} %slice_add_fusion.20), channel_id=1, replica_groups=mesh['seq'=8,'row'=4] {'seq'}, dimensions={0}, use_global_device_ids=true | all-gather | bytes 73728 | tf_op jit(solution)/shard_map/all_gather | solution.py:11
  558.4 30.5 %all_gather.41 = f32[8,1,2048]{2,1,0:T(1,128)S(1)} all-gather(f32[1,1,2048]{2,1,0:T(1,128)S(1)} %slice_add_fusion.17), channel_id=1, replica_groups=mesh['seq'=8,'row'=4] {'seq'}, dimensions={0}, use_global_device_ids=true | all-gather | bytes 73728 | tf_op jit(solution)/shard_map/all_gather | solution.py:11
  607.9 22.2 fusion.11
  867.6 30.5 %all_gather.44 = f32[8,1,2048]{2,1,0:T(1,128)S(1)} all-gather(f32[1,1,2048]{2,1,0:T(1,128)S(1)} %slice_add_fusion.16), channel_id=1, replica_groups=mesh['seq'=8,'row'=4] {'seq'}, dimensions={0}, use_global_device_ids=true | all-gather | bytes 73728 | tf_op jit(solution)/shard_map/all_gather | solution.py:11
  908.0 30.5 %all_gather.45 = f32[8,1,2048]{2,1,0:T(1,128)S(1)} all-gather(f32[1,1,2048]{2,1,0:T(1,128)S(1)} %slice_add_fusion.13), channel_id=1, replica_groups=mesh['seq'=8,'row'=4] {'seq'}, dimensions={0}, use_global_device_ids=true | all-gather | bytes 73728 | tf_op jit(solution)/shard_map/all_gather | solution.py:11
  1288.6 32.7 %rev.28 = f32[1,512,2048]{2,1,0:T(8,128)} reverse(f32[1,512,2048]{2,1,0:T(8,128)} %add.1110), dimensions={1} | reverse | bytes 8388608 | tf_op jit(solution)/shard_map/rev | solution.py:143
  1321.3 30.5 %all_gather.47 = f32[8,1,2048]{2,1,0:T(1,128)S(1)} all-gather(f32[1,1,2048]{2,1,0:T(1,128)S(1)} %slice_add_fusion.9), channel_id=1, replica_groups=mesh['seq'=8,'row'=4] {'seq'}, dimensions={0}, use_global_device_ids=true | all-gather | bytes 73728 | tf_op jit(solution)/shard_map/all_gather | solution.py:11
  1351.8 32.7 %rev.29 = f32[1,512,2048]{2,1,0:T(8,128)} reverse(f32[1,512,2048]{2,1,0:T(8,128)} %add.1119), dimensions={1} | reverse | bytes 8388608 | tf_op jit(solution)/shard_map/rev | solution.py:143
  1384.5 30.5 %all_gather.46 = f32[8,1,2048]{2,1,0:T(1,128)S(1)} all-gather(f32[1,1,2048]{2,1,0:T(1,128)S(1)} %slice_add_fusion.10), channel_id=1, replica_groups=mesh['seq'=8,'row'=4] {'seq'}, dimensions={0}, use_global_device_ids=true | all-gather | bytes 73728 | tf_op jit(solution)/shard_map/all_gather | solution.py:11
  1432.4 26.1 multiply_reduce_fusion.2
  1817.3 32.6 %rev.32 = f32[1,512,2048]{2,1,0:T(8,128)} reverse(f32[1,512,2048]{2,1,0:T(8,128)} %add.1150), dimensions={1} | reverse | bytes 8388608 | tf_op jit(solution)/shard_map/rev | solution.py:143
  1850.0 30.5 %all_gather.49 = f32[8,1,2048]{2,1,0:T(1,128)S(1)} all-gather(f32[1,1,2048]{2,1,0:T(1,128)S(1)} %slice_add_fusion.5), channel_id=1, replica_groups=mesh['seq'=8,'row'=4] {'seq'}, dimensions={0}, use_global_device_ids=true | all-gather | bytes 73728 | tf_op jit(solution)/shard_map/all_gather | solution.py:11
  1880.5 32.7 %rev.33 = f32[1,512,2048]{2,1,0:T(8,128)} reverse(f32[1,512,2048]{2,1,0:T(8,128)} %add.1159), dimensions={1} | reverse | bytes 8388608 | tf_op jit(solution)/shard_map/rev | solution.py:143
  1913.2 30.5 %all_gather.48 = f32[8,1,2048]{2,1,0:T(1,128)S(1)} all-gather(f32[1,1,2048]{2,1,0:T(1,128)S(1)} %slice_add_fusion.6), channel_id=1, replica_groups=mesh['seq'=8,'row'=4] {'seq'}, dimensions={0}, use_global_device_ids=true | all-gather | bytes 73728 | tf_op jit(solution)/shard_map/all_gather | solution.py:11
  1960.8 24.2 fusion.116
  1986.5 25.0 fusion.58
  2011.5 24.5 fusion.57
  2043.6 76.1 %reduce-scatter.13.cloned.1.call-done = f32[64,6]{1,0:T(8,128)} async-done(((f32[2048,6]{1,0:T(8,128)}), f32[64,6]{1,0:T(8,128)}) %reduce-scatter.13.cloned.1.call-update) | async-done | bytes 1552
  2121.1 432.3 %reduce-scatter.11.cloned.1.call-done = f32[64,6144]{1,0:T(8,128)} async-done(((f32[2048,6144]{1,0:T(8,128)}), f32[64,6144]{1,0:T(8,128)}) %reduce-scatter.11.cloned.1.call-update) | async-done | bytes 1572880 | tf_op jit(solution)/shard_map/reduce_scatter | solution.py:180
  2553.4 436.9 %reduce-scatter.9.cloned.1.call-done = f32[64,6144]{1,0:T(8,128)} async-done(((f32[2048,6144]{1,0:T(8,128)}), f32[64,6144]{1,0:T(8,128)}) %reduce-scatter.9.cloned.1.call-update) | async-done | bytes 1572880 | tf_op jit(solution)/shard_map/reduce_scatter | solution.py:180
  (938 shorter events, 1365.1 us)
Async XLA Ops:
  7.2 85.8 %copy-start.7 = (bf16[1,512,2048]{2,1,0:T(8,128)(2,1)S(1)}, bf16[1,512,2048]{2,1,0:T(8,128)(2,1)}, u32[]{:S(2)}) copy-start(bf16[1,512,2048]{2,1,0:T(8,128)(2,1)} %param.18) | copy-start | bytes 6291460
  7.3 86.1 %copy-start.120 = (s32[1,512]{1,0:T(1,128)S(1)}, s32[1,512]{1,0:T(1,128)}, u32[]{:S(2)}) copy-start(s32[1,512]{1,0:T(1,128)} %param.19) | copy-start | bytes 6148
  7.3 162.2 %all-gather.7.cloned.1.call-start = ((), (), s32[]{:S(2)}) async-start(), calls=%async_computation.6 | async-start | bytes 25952256 | tf_op jit(solution)/shard_map/all_gather | solution.py:70
  10.1 597.7 %all-gather.9.cloned.1.call-start = ((), (), s32[]{:S(2)}) async-start(), calls=%async_computation.7 | async-start | bytes 25952256 | tf_op jit(solution)/shard_map/all_gather | solution.py:70
  10.9 2031.9 %reduce-scatter.15.cloned.1.call-start = ((), (), s32[]{:S(2)}) async-start(), calls=%async_computation.9 | async-start | bytes 1081344
  93.4 96.8 %copy-start.88 = (f32[512]{0:T(512)}, f32[512]{0:T(512)S(1)}, u32[]{:S(2)}) copy-start(f32[512]{0:T(512)S(1)} %broadcast_multiply_fusion.7) | copy-start | bytes 6148
  94.1 96.1 %copy-start.92 = (f32[512]{0:T(512)}, f32[512]{0:T(512)S(1)}, u32[]{:S(2)}) copy-start(f32[512]{0:T(512)S(1)} %add_rsqrt_fusion.1) | copy-start | bytes 6148
  94.2 96.1 %copy-start.82 = (f32[2048,1]{0,1:T(1,128)}, f32[2048,1]{0,1:T(1,128)S(1)}, u32[]{:S(2)}) copy-start(f32[2048,1]{0,1:T(1,128)S(1)} %get-tuple-element.653) | copy-start | bytes 24580
  94.2 96.1 %copy-start.90 = (f32[2048,1]{0,1:T(1,128)}, f32[2048,1]{0,1:T(1,128)S(1)}, u32[]{:S(2)}) copy-start(f32[2048,1]{0,1:T(1,128)S(1)} %get-tuple-element.652) | copy-start | bytes 24580
  94.2 96.1 %copy-start.113 = (f32[2048,1]{0,1:T(1,128)}, f32[2048,1]{0,1:T(1,128)S(1)}, u32[]{:S(2)}) copy-start(f32[2048,1]{0,1:T(1,128)S(1)} %get-tuple-element.651) | copy-start | bytes 24580
  94.2 503.1 %copy-start.105 = (f32[2048,1]{0,1:T(1,128)}, f32[2048,1]{0,1:T(1,128)S(1)}, u32[]{:S(2)}) copy-start(f32[2048,1]{0,1:T(1,128)S(1)} %get-tuple-element.648) | copy-start | bytes 24580
  94.8 535.2 %copy-start.80 = (f32[2048,1]{0,1:T(1,128)}, f32[2048,1]{0,1:T(1,128)S(1)}, u32[]{:S(2)}) copy-start(f32[2048,1]{0,1:T(1,128)S(1)} %get-tuple-element.643) | copy-start | bytes 24580
  94.8 535.2 %copy-start.84 = (f32[2048,1]{0,1:T(1,128)}, f32[2048,1]{0,1:T(1,128)S(1)}, u32[]{:S(2)}) copy-start(f32[2048,1]{0,1:T(1,128)S(1)} %get-tuple-element.642) | copy-start | bytes 24580
  94.8 535.2 %copy-start.110 = (f32[2048,1]{0,1:T(1,128)}, f32[2048,1]{0,1:T(1,128)S(1)}, u32[]{:S(2)}) copy-start(f32[2048,1]{0,1:T(1,128)S(1)} %get-tuple-element.641) | copy-start | bytes 24580
  605.3 24.8 copy-start.86
  850.0 48.1 %copy-start.52 = (f32[1,256,2048]{2,1,0:T(8,128)S(1)}, f32[1,256,2048]{2,1,0:T(8,128)}, u32[]{:S(2)}) copy-start(f32[1,256,2048]{2,1,0:T(8,128)} %add.1074) | copy-start | bytes 6291460
  866.7 71.8 %copy-start.98 = (f32[1,2048]{1,0:T(1,128)S(1)}, f32[1,2048]{1,0:T(1,128)}, u32[]{:S(2)}) copy-start(f32[1,2048]{1,0:T(1,128)} %custom-call.1) | copy-start | bytes 24580
  1351.8 63.2 %copy-start.104 = (f32[1,2048]{1,0:T(1,128)S(1)}, f32[1,2048]{1,0:T(1,128)}, u32[]{:S(2)}) copy-start(f32[1,2048]{1,0:T(1,128)} %custom-call.2) | copy-start | bytes 24580
  1432.4 26.2 copy-start.8
  1432.4 26.2 copy-start.97
  1817.3 302.4 %reduce-scatter.13.cloned.1.call-start = ((), (), s32[]{:S(2)}) async-start(), calls=%async_computation.8 | async-start | bytes 1081344
  1880.4 63.2 %copy-start.103 = (f32[1,2048]{1,0:T(1,128)S(1)}, f32[1,2048]{1,0:T(1,128)}, u32[]{:S(2)}) copy-start(f32[1,2048]{1,0:T(1,128)} %custom-call.3) | copy-start | bytes 24580
  1986.4 567.0 %reduce-scatter.11.cloned.1.call-start = ((), (), s32[]{:S(2)}) async-start(), calls=%async_computation.5 | async-start | bytes 51904512 | tf_op jit(solution)/shard_map/reduce_scatter | solution.py:180
  2011.5 978.9 %reduce-scatter.9.cloned.1.call-start = ((), (), s32[]{:S(2)}) async-start(), calls=%async_computation.4 | async-start | bytes 51904512 | tf_op jit(solution)/shard_map/reduce_scatter | solution.py:180
  (109 other events, 716.0 us)
Sparse Core Ops, SparseCore 0:
  11.6 157.8 all-gather.6
  172.3 152.8 all-gather.8
  1817.4 132.8 reduce-scatter.14
  1986.5 133.1 reduce-scatter.12
  2126.0 427.4 reduce-scatter.10
  2559.7 430.5 reduce-scatter.8
where the time goes:
time: 3050 us; the launch traced here: 3000 us
  local copies, waits for them, and re-layouts  1170 us (38%)
  waiting for transfers between devices  1020 us (33%)
  blocking collectives  326 us (11%)
  other arithmetic  323 us (11%)
  matrix products  143 us (5%)
    reduce_scatter x2, waiting for transfers between devices, body(): lax.psum_scatter(weight_term, ('seq', 'row'), scatter_dimension=0, tiled=...  869 us
    slice x128, local copies, waits for them, and re-layouts, body(): lax.associative_scan(affine_join, (decay_rate, local_term), reverse=True,...  381 us
    all_gather x8, blocking collectives, entering(): pieces = jax.tree.map(lambda part: lax.all_gather(part, axis), value)  244 us
    pad x64, local copies, waits for them, and re-layouts, body(): lax.associative_scan(affine_join, (decay_rate, local_term), reverse=True,...  229 us
    slice x118, local copies, waits for them, and re-layouts, body(): lax.associative_scan(affine_join, (decay_rate, complement * candidate), a...  199 us
    pad x64, local copies, waits for them, and re-layouts, body(): lax.associative_scan(affine_join, (decay_rate, complement * candidate), a...  188 us
    rev x4, local copies, waits for them, and re-layouts, body(): lax.associative_scan(affine_join, (decay_rate, local_term), reverse=True,...  131 us
    all_gather x2, blocking collectives, body(): lax.all_gather(vectors, ('seq', 'row'), axis=0, tiled=True)  81.7 us
  transfers between devices with their start and end apart: 6, of which 4 were waited for; matrix products, arithmetic and copies ran while one was open for 18% of the time, Pallas kernels for 0%

commit v1 on v0

v1 whole, which is shorter than its diff:
```python
import jax
import jax.numpy as jnp
from jax import lax
from jax.experimental import pallas as pl
from jax.experimental.pallas import tpu as pltpu
from jax.sharding import PartitionSpec as P

epsilon = 1e-05
SUB = 8
WIDE = 256
F32 = jnp.float32
BF16 = jnp.bfloat16
GAIN, SHIFT, FPEEP, RPEEP, FBIAS, RBIAS = range(6)


def params(limit=60 << 20):
    return pltpu.CompilerParams(
        dimension_semantics=("arbitrary",), vmem_limit_bytes=limit
    )


def both_sigmoids(z):
    tail = jnp.exp(-jnp.abs(z))
    big = 1.0 / (1.0 + tail)
    small = tail * big
    up = z >= 0
    return jnp.where(up, big, small), jnp.where(up, small, big)


def lanes(value, width):
    return jnp.concatenate([value] * (width // value.shape[-1]), axis=-1)


def row_of(vec, k):
    return jnp.broadcast_to(vec[k : k + 1, :], (SUB, vec.shape[-1]))


def norm_rows(u, vec, n, low, mean, inv):
    steps, _, d = u.shape
    gain, shift = vec[GAIN : GAIN + 1, :], vec[SHIFT : SHIFT + 1, :]
    piece = 8

    def one(k, _):
        at = pl.ds(k * piece, piece)
        x = u[at].reshape(piece * SUB, d)
        mu = jnp.mean(x, axis=-1, keepdims=True)
        x = x - mu
        rstd = lax.rsqrt(jnp.mean(x * x, axis=-1, keepdims=True) + epsilon)
        y = x * rstd * gain + shift
        n[at] = y.reshape(piece, SUB, d)
        low[pl.ds(pl.multiple_of(k * piece * SUB, piece * SUB), piece * SUB), :] = y.astype(BF16)
        mean[at] = jnp.broadcast_to(mu, (piece * SUB, 128)).reshape(piece, SUB, 128)
        inv[at] = jnp.broadcast_to(rstd, (piece * SUB, 128)).reshape(piece, SUB, 128)
        return 0

    lax.fori_loop(0, steps // piece, one, 0)


def forward_gates(u, keep, vec, w, low, mean, inv, f, g, cand, rpre, ends, n, proj):
    j = pl.program_id(0)
    steps, width = f.shape[0], f.shape[-1]

    @pl.when(j == 0)
    def _():
        norm_rows(u, vec, n, low, mean, inv)

    at = pl.ds(pl.multiple_of(j * width, width), width)
    proj[...] = jnp.dot(low[...], w[0], preferred_element_type=F32).reshape(steps, SUB, 3 * width)
    peep, bias, rbias = (row_of(vec[:, at], k) for k in (FPEEP, FBIAS, RBIAS))

    def one(i, carry):
        scale, state = carry
        c = proj[i, :, :width]
        z = proj[i, :, width : 2 * width] + peep * n[i, :, at] + bias
        up, down = both_sigmoids(z)
        f[i] = up
        g[i] = down
        cand[i] = c
        rpre[i] = proj[i, :, 2 * width :] + rbias
        a = up * lanes(keep[i], width)
        return scale * a, a * state + down * c

    start = jnp.ones((SUB, width), F32), jnp.zeros((SUB, width), F32)
    scale, state = lax.fori_loop(0, steps, one, start, unroll=8)
    ends[0] = scale
    ends[1] = state


def forward_states(f, g, cand, rpre, u, keep, vec, first, p, r, out):
    steps, width = f.shape[0], f.shape[-1]
    peep = row_of(vec, RPEEP)

    def one(i, c):
        before = lanes(keep[i], width) * c
        c = f[i] * before + g[i] * cand[i]
        gate = jax.nn.sigmoid(rpre[i] + peep * before)
        p[i] = before
        r[i] = gate
        out[i] = gate * c + (1.0 - gate) * u[i]
        return c

    lax.fori_loop(0, steps, one, first[...], unroll=8)


def step_terms(i, dh, f, g, cand, p, r, u, keep, peep):
    width = f.shape[-1]
    before, gate, up = p[i], r[i], f[i]
    c = up * before + g[i] * cand[i]
    top = dh[i]
    dz_r = top * (c - u[i]) * gate * (1.0 - gate)
    direct = top * gate
    kept = lanes(keep[i], width)
    decay = up * kept
    return before, up, dz_r, direct, decay, kept * peep * dz_r + decay * direct


def backward_ends(dh, f, g, cand, p, r, u, keep, vec, ends):
    steps, width = f.shape[0], f.shape[-1]
    peep = row_of(vec, RPEEP)

    def one(t, carry):
        scale, q = carry
        i = steps - 1 - t
        _, _, _, _, decay, term = step_terms(i, dh, f, g, cand, p, r, u, keep, peep)
        return scale * decay, decay * q + term

    start = jnp.ones((SUB, width), F32), jnp.zeros((SUB, width), F32)
    scale, q = lax.fori_loop(0, steps, one, start, unroll=8)
    ends[0] = scale
    ends[1] = q


def backward_states(
    dh, f, g, cand, p, r, u, keep, vec, mean, inv, first, du, dzf, sums, low
):
    steps, width = f.shape[0], f.shape[-1]
    peep, gain, shift = (row_of(vec, k) for k in (RPEEP, GAIN, SHIFT))

    def one(t, carry):
        q, s0, s1, s2, s3 = carry
        i = steps - 1 - t
        before, up, dz_r, direct, decay, term = step_terms(
            i, dh, f, g, cand, p, r, u, keep, peep
        )
        e = direct + q
        down = g[i]
        dz_f = e * (up * down) * (before - cand[i])
        n = (u[i] - lanes(mean[i], width)) * lanes(inv[i], width) * gain + shift
        low[0, i] = e * down
        low[1, i] = dz_f
        low[2, i] = dz_r
        dzf[i] = dz_f
        return (
            decay * q + term,
            s0 + dz_f * n,
            s1 + dz_r * before,
            s2 + dz_f,
            s3 + dz_r,
        )

    zero = jnp.zeros((SUB, width), F32)
    carry = lax.fori_loop(0, steps, one, (first[...], zero, zero, zero, zero), unroll=4)
    for k in range(4):
        sums[k] = carry[k + 1]
    for k in range(3):
        du[0, :, k * width : (k + 1) * width] = low[k].reshape(steps * SUB, width).astype(BF16)


def input_side(du, w, dzf, u, dh, r, mean, inv, vec, out, sums, acc):
    j = pl.program_id(0)
    steps, _, d = u.shape
    part = lax.dot_general(du[0], w[0], (((1,), (1,)), ((), ())), preferred_element_type=F32)

    @pl.when(j == 0)
    def _():
        acc[...] = part.reshape(steps, SUB, d)

    @pl.when(j > 0)
    def _():
        acc[...] += part.reshape(steps, SUB, d)

    @pl.when(j == pl.num_programs(0) - 1)
    def _():
        sums[...] = jnp.zeros_like(sums)
        peep, gain = row_of(vec, FPEEP), row_of(vec, GAIN)

        def one(i, _):
            dn = acc[i] + dzf[i] * peep
            rstd = lanes(inv[i], d)
            xhat = (u[i] - lanes(mean[i], d)) * rstd
            sums[0] += dn * xhat
            sums[1] += dn
            scaled = dn * gain
            m0 = jnp.mean(scaled, axis=-1, keepdims=True)
            m1 = jnp.mean(scaled * xhat, axis=-1, keepdims=True)
            out[i] = dh[i] * (1.0 - r[i]) + rstd * (scaled - m0 - xhat * m1)
            return 0

        lax.fori_loop(0, steps, one, 0, unroll=2)


def weight_side(low_t, du, out):
    out[0] = jnp.dot(low_t[...], du[0], preferred_element_type=F32)


def columns(steps, width):
    return pl.BlockSpec((steps, SUB, width), lambda j: (0, 0, j))


def whole(*shape):
    return pl.BlockSpec(shape, lambda j: (0,) * len(shape))


def vectors(width):
    return pl.BlockSpec((8, width), lambda j: (0, j))


def arr(*shape, dtype=F32):
    return jax.ShapeDtypeStruct(shape, dtype)


def chain(ends, axis, backward):
    everyone = lax.all_gather(ends, axis)
    count, mine = lax.axis_size(axis), lax.axis_index(axis)
    segments, d = ends.shape[1:]
    total = count * segments
    scale = everyone[:, 0].reshape(total, d)
    state = everyone[:, 1].reshape(total, d)
    if backward:
        scale, state = scale[::-1], state[::-1]
    value = jnp.zeros((d,), F32)
    entering = []
    for k in range(total):
        entering.append(value)
        value = scale[k] * value + state[k]
    entering = jnp.stack(entering)
    if backward:
        entering = entering[::-1]
    return lax.dynamic_slice_in_dim(entering, mine * segments, segments, 0)


def body(tokens, resets, cotangent, weight, *rows):
    _, t, d = tokens.shape
    layers = weight.shape[0]
    steps = t // SUB
    parts = d // WIDE
    axes = ("seq", "row")

    def permuted(x):
        return x.reshape(SUB, steps, -1).transpose(1, 0, 2)

    def restored(x):
        return x.reshape(steps, SUB, d).transpose(1, 0, 2).reshape(1, t, d)

    keep = permuted((1 - resets[0]).astype(F32)[:, None])
    keep = jnp.broadcast_to(keep, (steps, SUB, 128))
    packed = jnp.stack(rows + (jnp.zeros_like(rows[0]),) * 2, axis=1)
    every = lax.all_gather(packed, axes, axis=2, tiled=True).astype(F32)
    local = weight.reshape(layers, -1, 3, parts, WIDE).transpose(0, 3, 1, 2, 4)
    local = local.reshape(layers, parts, -1, 3 * WIDE)
    full = [lax.all_gather(local[l], axes, axis=1, tiled=True) for l in range(layers)]

    u = permuted(tokens).astype(F32)
    stored = []
    col = columns(steps, WIDE)
    keep_spec = whole(steps, SUB, 128)
    w_spec = pl.BlockSpec((1, d, 3 * WIDE), lambda j: (j, 0, 0))
    du_spec = pl.BlockSpec((1, t, 3 * WIDE), lambda j: (j, 0, 0))
    act = arr(steps, SUB, d)
    stat = arr(steps, SUB, 128)
    for l in range(layers):
        vec = every[l]
        low, mean, inv, f, g, cand, rpre, ends = pl.pallas_call(
            forward_gates,
            grid=(parts,),
            in_specs=[whole(steps, SUB, d), keep_spec, whole(8, d), w_spec],
            out_specs=[
                whole(t, d), keep_spec, keep_spec, col, col, col, col,
                pl.BlockSpec((2, SUB, WIDE), lambda j: (0, 0, j)),
            ],
            out_shape=[arr(t, d, dtype=BF16), stat, stat, act, act, act, act, arr(2, SUB, d)],
            scratch_shapes=[
                pltpu.VMEM((steps, SUB, d), F32), pltpu.VMEM((steps, SUB, 3 * WIDE), F32)
            ],
            compiler_params=params(),
            name="forward_gates",
        )(u, keep, vec, full[l])
        first = chain(ends, "seq", False)
        p, r, out = pl.pallas_call(
            forward_states,
            grid=(parts,),
            in_specs=[col] * 5 + [keep_spec, vectors(WIDE), vectors(WIDE)],
            out_specs=[col] * 3,
            out_shape=[act] * 3,
            compiler_params=params(),
            name="forward_states",
        )(f, g, cand, rpre, u, keep, vec, first)
        stored.append((u, low, mean, inv, f, g, cand, p, r))
        u = out
    result = restored(u.astype(BF16))

    dh = permuted(cotangent).astype(F32)
    weight_grads, vector_grads = [None] * layers, [None] * layers
    for l in reversed(range(layers)):
        vec = every[l]
        u, low, mean, inv, f, g, cand, p, r = stored[l]
        ends = pl.pallas_call(
            backward_ends,
            grid=(parts,),
            in_specs=[col] * 7 + [keep_spec, vectors(WIDE)],
            out_specs=pl.BlockSpec((2, SUB, WIDE), lambda j: (0, 0, j)),
            out_shape=arr(2, SUB, d),
            compiler_params=params(),
            name="backward_ends",
        )(dh, f, g, cand, p, r, u, keep, vec)
        first = chain(ends, "seq", True)
        du, dzf, sums = pl.pallas_call(
            backward_states,
            grid=(parts,),
            in_specs=[col] * 7 + [keep_spec, vectors(WIDE), keep_spec, keep_spec, vectors(WIDE)],
            out_specs=[du_spec, col, pl.BlockSpec((4, SUB, WIDE), lambda j: (0, 0, j))],
            out_shape=[arr(parts, t, 3 * WIDE, dtype=BF16), act, arr(4, SUB, d)],
            scratch_shapes=[pltpu.VMEM((3, steps, SUB, WIDE), F32)],
            compiler_params=params(),
            name="backward_states",
        )(dh, f, g, cand, p, r, u, keep, vec, mean, inv, first)
        grad = pl.pallas_call(
            weight_side,
            grid=(parts,),
            in_specs=[whole(d, t), du_spec],
            out_specs=w_spec,
            out_shape=arr(parts, d, 3 * WIDE),
            compiler_params=params(),
            name="weight_side",
        )(low.T, du)
        dh, more = pl.pallas_call(
            input_side,
            grid=(parts,),
            in_specs=[du_spec, w_spec]
            + [whole(steps, SUB, d)] * 4
            + [keep_spec, keep_spec, whole(8, d)],
            out_specs=[whole(steps, SUB, d), whole(2, SUB, d)],
            out_shape=[act, arr(2, SUB, d)],
            scratch_shapes=[pltpu.VMEM((steps, SUB, d), F32)],
            compiler_params=params(),
            name="input_side",
        )(du, full[l], dzf, u, dh, r, mean, inv, vec)
        grad = lax.psum_scatter(grad, axes, scatter_dimension=1, tiled=True)
        weight_grads[l] = (
            grad.reshape(parts, -1, 3, WIDE).transpose(1, 2, 0, 3).reshape(-1, 3 * d)
        )
        vector_grads[l] = jnp.concatenate([more.sum(1), sums.sum(1)])
    input_grad = restored(dh.astype(BF16))
    vector_out = lax.psum_scatter(
        jnp.stack(vector_grads), axes, scatter_dimension=2, tiled=True
    )
    return (result, input_grad, jnp.stack(weight_grads)) + tuple(
        vector_out[:, k] for k in range(6)
    )


def solution(mesh):
    tokens = P("row", "seq", None)
    rows = P(None, ("seq", "row"))
    weight = P(None, ("seq", "row"), None)
    return jax.shard_map(
        body,
        mesh=mesh,
        in_specs=(tokens, P("row", "seq"), tokens, weight) + (rows,) * 6,
        out_specs=(tokens, tokens, weight) + (rows,) * 6,
        check_vma=False,
    )
```

time: 3050 us -> 1730 us (0.57); the launches traced: 3000 us -> 1720 us
  local copies, waits for them, and re-layouts: 1170 us -> 71.5 us
  other arithmetic: 323 us -> 9.44 us
  waiting for transfers between devices: 1020 us -> 1330 us
  blocking collectives: 326 us -> 49.7 us
  Pallas kernels: 0 us -> 250 us
  matrix products: 143 us -> 0 us
    slice x249 -> x2, local copies, waits for them, and re-layouts: 583 us -> 0.91 us  [the longest x1 0.77 us: body(): local[l]]
    pad x128 -> x0, local copies, waits for them, and re-layouts: 417 us -> none  [the longest x64 229 us: body(): lax.associative_scan(affine_join, (decay_rate, local_term), reverse=True,...]
    all_gather x2 -> x6, waiting for transfers between devices: 74.6 us -> 391 us  [the longest x2 242 us: body(): lax.all_gather(local[l], axes, axis=1, tiled=True)]
    all_gather x10 -> x1, blocking collectives: 326 us -> 49.7 us  [body(): every = lax.all_gather(packed, axes, axis=2, tiled=True).astype(F32)]
    pallas_call x0 -> x12, Pallas kernels: none -> 250 us  [the longest x2 63.4 us: body(): pl.pallas_call(input_side, grid=(parts,), in_specs=[du_spec, w_spec] + [w...]
    add x111 -> x4, other arithmetic: 165 us -> 3.44 us  [chain(): value = scale[k] * value + state[k]]
    dot_general x6 -> x0, matrix products: 143 us -> none  [the longest x2 50.3 us: body(): jnp.einsum('rte,de->rtd', projected_grad, full_weight, preferred_element_...]
    rev x8 -> x2, local copies, waits for them, and re-layouts: 131 us -> 0.7 us  [chain(): entering = entering[::-1]]
  transfers between devices with their start and end apart: 6 -> 9, of which waited for: 4 -> 9; matrix products, arithmetic and copies ran while one was open for 18% -> 2% of each run, Pallas kernels for 0% -> 3%
where the time goes in v1:
time: 1730 us; the launch traced here: 1720 us
  waiting for transfers between devices  1330 us (77%)
  Pallas kernels  250 us (14%)
  local copies, waits for them, and re-layouts  71.5 us (4%)
  blocking collectives  49.7 us (3%)
    reduce_scatter x2, waiting for transfers between devices, body(): grad = lax.psum_scatter(grad, axes, scatter_dimension=1, tiled=True)  861 us
    all_gather x2, waiting for transfers between devices, body(): lax.all_gather(local[l], axes, axis=1, tiled=True)  242 us
    all_gather x4, waiting for transfers between devices, chain(): everyone = lax.all_gather(ends, axis)  149 us
    unnamed x10, waiting for transfers between devices  76.3 us
    pallas_call x2, Pallas kernels, body(): pl.pallas_call(input_side, grid=(parts,), in_specs=[du_spec, w_spec] + [w...  63.4 us
    pallas_call x2, Pallas kernels, body(): pl.pallas_call(forward_gates, grid=(parts,), in_specs=[whole(steps, SUB,...  54.4 us
    all_gather x1, blocking collectives, body(): every = lax.all_gather(packed, axes, axis=2, tiled=True).astype(F32)  49.7 us
    pallas_call x2, Pallas kernels, body(): pl.pallas_call(weight_side, grid=(parts,), in_specs=[whole(d, t), du_spec...  43.1 us
  transfers between devices with their start and end apart: 9, of which 9 were waited for; matrix products, arithmetic and copies ran while one was open for 2% of the time, Pallas kernels for 3%

profile of v1, /device:TPU:0, one launch (start us, length us, event | category | flops | bytes accessed | tf_op | source)
XLA Modules:
  0.0 1724.7 jit_solution(4204061143785083243)
XLA Ops:
  14.3 49.7 %all_gather.33 = bf16[2,8,2048]{1,0,2:T(2,128)(2,1)S(1)} all-gather(bf16[2,8,64]{1,0,2:T(2,128)(2,1)S(1)} %stack.39), channel_id=1, replica_groups=mesh['seq'=8,'row'=4] {'seq','row'}, dimensions={2}, use_global_device_ids=true | all-gather | bytes 67584 | tf_op jit(solution)/shard_map/all_gather | solution.py:258
  64.7 4.8 copy.182
  70.1 103.2 %all-gather.11.cloned.1.call-done.w = bf16[8,2048,768]{2,1,0:T(8,128)(2,1)} async-done(((bf16[8,64,768]{2,1,0:T(8,128)(2,1)}), bf16[8,2048,768]{2,1,0:T(8,128)(2,1)}) %all-gather.11.cloned.1.call-update) | async-done | bytes 25165840 | tf_op jit(solution)/shard_map/all_gather | solution.py:261
  174.1 27.1 %forward_gates.2 = (bf16[512,2048]{1,0:T(8,128)(2,1)}, f32[64,8,128]{2,1,0:T(8,128)}, f32[64,8,128]{2,1,0:T(8,128)}, f32[64,8,2048]{2,1,0:T(8,128)}, f32[64,8,20...) custom-call(f32[64,8,2048]{2,1,0:T(8,128)} %bitcast.89, ...), custom_call_target="tpu_custom_call" | custom-call | tf_op jit(solution)/shard_map/forward_gates/pallas_call | solution.py:273
  203.1 36.7 %all-gather.15.cloned.1.call-done = f32[16,8,2048]{2,1,0:T(8,128)} async-done(((f32[2,8,2048]{2,1,0:T(8,128)}), f32[16,8,2048]{2,1,0:T(8,128)}) %all-gather.15.cloned.1.call-update) | async-done | bytes 1048592 | tf_op jit(solution)/shard_map/all_gather | solution.py:223
  243.4 14.6 forward_states.2
  258.0 138.8 %all-gather.13.cloned.1.call-done.w = bf16[8,2048,768]{2,1,0:T(8,128)(2,1)} async-done(((bf16[8,64,768]{2,1,0:T(8,128)(2,1)}), bf16[8,2048,768]{2,1,0:T(8,128)(2,1)}) %all-gather.13.cloned.1.call-update) | async-done | bytes 25165840 | tf_op jit(solution)/shard_map/all_gather | solution.py:261
  396.7 27.3 %forward_gates.3 = (bf16[512,2048]{1,0:T(8,128)(2,1)}, f32[64,8,128]{2,1,0:T(8,128)}, f32[64,8,128]{2,1,0:T(8,128)}, f32[64,8,2048]{2,1,0:T(8,128)}, f32[64,8,20...) custom-call(f32[64,8,2048]{2,1,0:T(8,128)} %get-tuple-element.46.u, ...), custom_call_target="tpu_custom_call" | custom-call | tf_op jit(solution)/shard_map/forward_gates/pallas_call | solution.py:273
  427.5 35.0 %all-gather.17.cloned.1.call-done = f32[16,8,2048]{2,1,0:T(8,128)} async-done(((f32[2,8,2048]{2,1,0:T(8,128)}), f32[16,8,2048]{2,1,0:T(8,128)}) %all-gather.17.cloned.1.call-update) | async-done | bytes 1048592 | tf_op jit(solution)/shard_map/all_gather | solution.py:223
  466.2 14.3 forward_states.3
  480.5 12.4 backward_ends.2
  493.0 39.0 %all-gather.19.cloned.1.call-done = f32[16,8,2048]{2,1,0:T(8,128)} async-done(((f32[2,8,2048]{2,1,0:T(8,128)}), f32[16,8,2048]{2,1,0:T(8,128)}) %all-gather.19.cloned.1.call-update) | async-done | bytes 1048592 | tf_op jit(solution)/shard_map/all_gather | solution.py:223
  536.0 17.4 %backward_states.2 = (bf16[8,512,768]{2,1,0:T(8,128)(2,1)}, f32[64,8,2048]{2,1,0:T(8,128)}, f32[4,8,2048]{2,1,0:T(8,128)}) custom-call(f32[64,8,2048]{2,1,0:T(8,128)} %bitcast.95, f32[64,8,2048]{2,1,0:T(8,128)} %get-tuple-element.47.f, f32[64,8,2048]{2,1,0:T(8,128)} %get-tuple-element.48.g, f32[64,8,2048]{2,1,0:T(8,128)} %get-tuple-element.49.cand, ...), custom_call_target="tpu_custom_call" | custom-call | tf_op jit(solution)/shard_map/backward_states/pallas_call | solution.py:317
  553.4 31.7 %input_side.2 = (f32[64,8,2048]{2,1,0:T(8,128)}, f32[2,8,2048]{2,1,0:T(8,128)}) custom-call(bf16[8,512,768]{2,1,0:T(8,128)(2,1)} %get-tuple-element.57.du, bf16[8,2048,768]{2,1,0:T(8,128)(2,1)} %all-gather.13.cloned.1.call-done.w, f32[64,8,2048]{2,1,0:T(8,128)} %get-tuple-element.58.dzf, f32[64,8,2048]{2,1,0:T(8,128)} %get-tuple-element.46.u, ...), custom_call_target="tpu_custom_call" | custom-call | tf_op jit(solution)/shard_map/input_side/pallas_call | solution.py:336
  585.1 12.5 backward_ends.3
  598.1 38.6 %all-gather.21.cloned.1.call-done = f32[16,8,2048]{2,1,0:T(8,128)} async-done(((f32[2,8,2048]{2,1,0:T(8,128)}), f32[16,8,2048]{2,1,0:T(8,128)}) %all-gather.21.cloned.1.call-update) | async-done | bytes 1048592 | tf_op jit(solution)/shard_map/all_gather | solution.py:223
  640.7 17.4 %backward_states.3 = (bf16[8,512,768]{2,1,0:T(8,128)(2,1)}, f32[64,8,2048]{2,1,0:T(8,128)}, f32[4,8,2048]{2,1,0:T(8,128)}) custom-call(f32[64,8,2048]{2,1,0:T(8,128)} %get-tuple-element.59.dh, f32[64,8,2048]{2,1,0:T(8,128)} %get-tuple-element.41.f, f32[64,8,2048]{2,1,0:T(8,128)} %get-tuple-element.42.g, f32[64,8,2048]{2,1,0:T(8,128)} %get-tuple-element.43.cand, ...), custom_call_target="tpu_custom_call" | custom-call | tf_op jit(solution)/shard_map/backward_states/pallas_call | solution.py:317
  658.1 31.7 %input_side.3 = (f32[64,8,2048]{2,1,0:T(8,128)}, f32[2,8,2048]{2,1,0:T(8,128)}) custom-call(bf16[8,512,768]{2,1,0:T(8,128)(2,1)} %get-tuple-element.64.du, bf16[8,2048,768]{2,1,0:T(8,128)(2,1)} %all-gather.11.cloned.1.call-done.w, f32[64,8,2048]{2,1,0:T(8,128)} %get-tuple-element.65.dzf, f32[64,8,2048]{2,1,0:T(8,128)} %bitcast.93, ...), custom_call_target="tpu_custom_call" | custom-call | tf_op jit(solution)/shard_map/input_side/pallas_call | solution.py:336
  695.8 6.4 reshape.71
  704.8 21.6 %weight_side.3 = f32[8,2048,768]{2,1,0:T(8,128)} custom-call(bf16[2048,512]{1,0:T(8,128)(2,1)} %bitcast.98, bf16[8,512,768]{2,1,0:T(8,128)(2,1)} %get-tuple-element.57.du), custom_call_target="tpu_custom_call" | custom-call | tf_op jit(solution)/shard_map/weight_side/pallas_call | solution.py:327
  730.4 21.6 %weight_side.2 = f32[8,2048,768]{2,1,0:T(8,128)} custom-call(bf16[2048,512]{1,0:T(8,128)(2,1)} %bitcast.99, bf16[8,512,768]{2,1,0:T(8,128)(2,1)} %get-tuple-element.64.du), custom_call_target="tpu_custom_call" | custom-call | tf_op jit(solution)/shard_map/weight_side/pallas_call | solution.py:327
  759.8 76.1 %reduce-scatter.10.cloned.1.call-done = f32[64,12]{1,0:T(8,128)} async-done(((f32[2048,12]{1,0:T(8,128)}), f32[64,12]{1,0:T(8,128)}) %reduce-scatter.10.cloned.1.call-update) | async-done | bytes 3088
  840.7 430.3 %reduce-scatter.8.cloned.1.call-done = f32[8,64,768]{2,1,0:T(8,128)} async-done(((f32[8,2048,768]{2,1,0:T(8,128)}), f32[8,64,768]{2,1,0:T(8,128)}) %reduce-scatter.8.cloned.1.call-update) | async-done | bytes 1572880 | tf_op jit(solution)/shard_map/reduce_scatter | solution.py:348
  1278.3 430.9 %reduce-scatter.6.cloned.1.call-done = f32[8,64,768]{2,1,0:T(8,128)} async-done(((f32[8,2048,768]{2,1,0:T(8,128)}), f32[8,64,768]{2,1,0:T(8,128)}) %reduce-scatter.6.cloned.1.call-update) | async-done | bytes 1572880 | tf_op jit(solution)/shard_map/reduce_scatter | solution.py:348
  (119 shorter events, 71.0 us)
Async XLA Ops:
  7.2 166.1 %all-gather.11.cloned.1.call-start = ((), (), s32[]{:S(2)}) async-start(), calls=%async_computation.3 | async-start | bytes 25952256 | tf_op jit(solution)/shard_map/all_gather | solution.py:261
  10.0 2.6 copy-start.8
  10.1 2.8 copy-start.9
  10.1 2.9 copy-start.10
  10.1 3.0 copy-start.11
  10.1 3.2 copy-start.12
  10.1 3.3 copy-start.13
  10.1 3.4 copy-start.14
  12.6 227.1 %all-gather.15.cloned.1.call-start = ((), (), s32[]{:S(2)}) async-start(), calls=%async_computation.7 | async-start | bytes 1179648 | tf_op jit(solution)/shard_map/all_gather | solution.py:223
  201.3 195.5 %all-gather.13.cloned.1.call-start = ((), (), s32[]{:S(2)}) async-start(), calls=%async_computation.4 | async-start | bytes 25952256 | tf_op jit(solution)/shard_map/all_gather | solution.py:261
  203.0 259.5 %all-gather.17.cloned.1.call-start = ((), (), s32[]{:S(2)}) async-start(), calls=%async_computation.8 | async-start | bytes 1179648 | tf_op jit(solution)/shard_map/all_gather | solution.py:223
  396.7 27.6 %copy-start.2 = (bf16[1,512,2048]{2,1,0:T(8,128)(2,1)S(1)}, bf16[1,512,2048]{2,1,0:T(8,128)(2,1)}, u32[]{:S(2)}) copy-start(bf16[1,512,2048]{2,1,0:T(8,128)(2,1)} %param.12) | copy-start | bytes 6291460
  424.1 108.0 %all-gather.19.cloned.1.call-start = ((), (), s32[]{:S(2)}) async-start(), calls=%async_computation.9 | async-start | bytes 1179648 | tf_op jit(solution)/shard_map/all_gather | solution.py:223
  492.9 143.8 %all-gather.21.cloned.1.call-start = ((), (), s32[]{:S(2)}) async-start(), calls=%async_computation.10 | async-start | bytes 1179648 | tf_op jit(solution)/shard_map/all_gather | solution.py:223
  585.1 12.8 copy-start.7
  585.1 12.9 copy-start.5
  597.7 238.2 %reduce-scatter.10.cloned.1.call-start = ((), (), s32[]{:S(2)}) async-start(), calls=%async_computation.11 | async-start | bytes 1081344
  658.1 32.7 %copy-start.6 = (f32[4,8,2048]{2,1,0:T(8,128)S(1)}, f32[4,8,2048]{2,1,0:T(8,128)}, u32[]{:S(2)}) copy-start(f32[4,8,2048]{2,1,0:T(8,128)} %get-tuple-element.70) | copy-start | bytes 786436
  695.8 6.4 copy-start.4
  702.2 568.8 %reduce-scatter.8.cloned.1.call-start = ((), (), s32[]{:S(2)}) async-start(), calls=%async_computation.6 | async-start | bytes 51904512 | tf_op jit(solution)/shard_map/reduce_scatter | solution.py:348
  726.3 1.6 copy-start.3
  726.4 982.9 %reduce-scatter.6.cloned.1.call-start = ((), (), s32[]{:S(2)}) async-start(), calls=%async_computation.5 | async-start | bytes 51904512 | tf_op jit(solution)/shard_map/reduce_scatter | solution.py:348
  754.5 2.5 copy-start.1
  1713.9 1.9 copy-start
Sparse Core Ops, SparseCore 0:
  12.7 160.5 all-gather.10
  201.4 38.3 all-gather.14
  243.2 153.4 all-gather.12
  424.2 38.3 all-gather.16
  493.1 38.8 all-gather.18
  597.8 38.8 all-gather.20
  702.3 133.5 reduce-scatter.9
  843.5 427.4 reduce-scatter.7
  1278.6 430.6 reduce-scatter.5

commit v2 on v1

--- a/solution.py
+++ b/solution.py
@@ -54,36 +54,6 @@
         return 0
 
     lax.fori_loop(0, steps // piece, one, 0)
-
-
-def forward_gates(u, keep, vec, w, low, mean, inv, f, g, cand, rpre, ends, n, proj):
-    j = pl.program_id(0)
-    steps, width = f.shape[0], f.shape[-1]
-
-    @pl.when(j == 0)
-    def _():
-        norm_rows(u, vec, n, low, mean, inv)
-
-    at = pl.ds(pl.multiple_of(j * width, width), width)
-    proj[...] = jnp.dot(low[...], w[0], preferred_element_type=F32).reshape(steps, SUB, 3 * width)
-    peep, bias, rbias = (row_of(vec[:, at], k) for k in (FPEEP, FBIAS, RBIAS))
-
-    def one(i, carry):
-        scale, state = carry
-        c = proj[i, :, :width]
-        z = proj[i, :, width : 2 * width] + peep * n[i, :, at] + bias
-        up, down = both_sigmoids(z)
-        f[i] = up
-        g[i] = down
-        cand[i] = c
-        rpre[i] = proj[i, :, 2 * width :] + rbias
-        a = up * lanes(keep[i], width)
-        return scale * a, a * state + down * c
-
-    start = jnp.ones((SUB, width), F32), jnp.zeros((SUB, width), F32)
-    scale, state = lax.fori_loop(0, steps, one, start, unroll=8)
-    ends[0] = scale
-    ends[1] = state
 
 
 def forward_states(f, g, cand, rpre, u, keep, vec, first, p, r, out):
@@ -162,14 +132,18 @@
     carry = lax.fori_loop(0, steps, one, (first[...], zero, zero, zero, zero), unroll=4)
     for k in range(4):
         sums[k] = carry[k + 1]
-    for k in range(3):
-        du[0, :, k * width : (k + 1) * width] = low[k].reshape(steps * SUB, width).astype(BF16)
+    for h in range(2):
+        for k in range(3):
+            v = low[k, :, :, h * LANE : (h + 1) * LANE].reshape(steps * SUB, LANE)
+            du[0, h, :, k * LANE : (k + 1) * LANE] = v.astype(BF16)
 
 
 def input_side(du, w, dzf, u, dh, r, mean, inv, vec, out, sums, acc):
     j = pl.program_id(0)
     steps, _, d = u.shape
-    part = lax.dot_general(du[0], w[0], (((1,), (1,)), ((), ())), preferred_element_type=F32)
+    across = (((1,), (1,)), ((), ()))
+    part = lax.dot_general(du[0, 0], w[0, 0], across, preferred_element_type=F32)
+    part = part + lax.dot_general(du[0, 1], w[0, 1], across, preferred_element_type=F32)
 
     @pl.when(j == 0)
     def _():
@@ -199,8 +173,521 @@
         lax.fori_loop(0, steps, one, 0, unroll=2)
 
 
-def weight_side(low_t, du, out):
-    out[0] = jnp.dot(low_t[...], du[0], preferred_element_type=F32)
+MESH = pl.DeviceIdType.MESH
+HALF = 384
+LANE = 128
+
+
+class Place:
+    def __init__(self, seq, row):
+        self.Y = row // 2
+        self.X = self.Y
+        self.Z = seq // self.X
+        self.C = 2
+        self.sizes = dict(z=self.Z, x=self.X, y=self.Y, c=self.C)
+        s, r = lax.axis_index("seq"), lax.axis_index("row")
+        self.at = dict(z=s // self.X, x=s % self.X, y=r // 2, c=r % 2)
+
+    def moved(self, axis, k):
+        size = self.sizes[axis]
+        return dict(self.at, **{axis: lax.rem(self.at[axis] + k, size)})
+
+    def device(self, at):
+        return {"seq": at["z"] * self.X + at["x"], "row": at["y"] * 2 + at["c"]}
+
+    def others(self, axis):
+        return range(1, self.sizes[axis])
+
+    def barrier(self, seq):
+        sem = pltpu.get_barrier_semaphore()
+        count = 0
+        s, r = lax.axis_index("seq"), lax.axis_index("row")
+        for k in range(1, seq):
+            pl.semaphore_signal(
+                sem, inc=1, device_id={"seq": lax.rem(s + k, seq), "row": r}, device_id_type=MESH
+            )
+            count += 1
+        for axis in ("y", "c"):
+            for k in self.others(axis):
+                pl.semaphore_signal(
+                    sem, inc=1, device_id=self.device(self.moved(axis, k)), device_id_type=MESH
+                )
+                count += 1
+        pl.semaphore_wait(sem, count)
+
+
+def remote(src, dst, send, recv, to):
+    return pltpu.make_async_remote_copy(
+        src_ref=src, dst_ref=dst, send_sem=send, recv_sem=recv, device_id=to, device_id_type=MESH
+    )
+
+
+def share_ends(table, own, send, recv, seq):
+    s, r = lax.axis_index("seq"), lax.axis_index("row")
+    table[s] = own
+
+    def copy(k, where, to):
+        return remote(table.at[where], table.at[where], send.at[k], recv.at[k], {"seq": to, "row": r})
+
+    for k in range(1, seq):
+        copy(k, s, lax.rem(s + k, seq)).start()
+    for k in range(1, seq):
+        back = lax.rem(s + seq - k, seq)
+        copy(k, back, back).wait_recv()
+    for k in range(1, seq):
+        copy(k, s, lax.rem(s + k, seq)).wait_send()
+
+
+def total_of(scale, state, backward):
+    order = range(SUB - 1, -1, -1) if backward else range(SUB)
+    whole_scale, whole_state = None, None
+    for k in order:
+        a, b = scale[k : k + 1], state[k : k + 1]
+        if whole_scale is None:
+            whole_scale, whole_state = a, b
+        else:
+            whole_scale, whole_state = a * whole_scale, a * whole_state + b
+    return jnp.concatenate([whole_scale, whole_state], axis=0)
+
+
+def entering(table, scale, state, seq, backward):
+    s = lax.axis_index("seq")
+    value = jnp.zeros_like(scale[:1])
+    for k in range(seq - 1):
+        if backward:
+            k = seq - 1 - k
+        longer = table[k, 0:1] * value + table[k, 1:2]
+        value = jnp.where(k > s if backward else k < s, longer, value)
+    out = [None] * SUB
+    for k in range(SUB - 1, -1, -1) if backward else range(SUB):
+        out[k] = value
+        value = scale[k : k + 1] * value + state[k : k + 1]
+    return jnp.concatenate(out, axis=0)
+
+
+def gather_gates(
+    seq, row, tag, u, keep, vin, w_own, *refs
+):
+    if tag == 0:
+        (w_all, vec_out, low, mean, inv, f_out, g_out, cand_out, rpre_out, first,
+         table, ends, n, proj, wbuf, f, g, cand, rpre, vall,
+         snd, rcv, loc, outs, xsnd, xrcv, vsnd, vrcv) = refs
+    else:
+        (w_all, low, mean, inv, f_out, g_out, cand_out, rpre_out, first,
+         table, ends, n, proj, wbuf, f, g, cand, rpre,
+         snd, rcv, loc, outs, xsnd, xrcv) = refs
+    pos = Place(seq, row)
+    at = pos.at
+    z, x, y, c = (at[k] for k in "zxyc")
+    steps, _, d = u.shape
+    parts = w_own.shape[0]
+    pos.barrier(seq)
+    every = slice(None)
+
+    def region(ref, head, stage, h, who):
+        first_axis = ("y", "x")[h]
+        spot = [who["z"], who["x"], who["y"], who["c"]]
+        if stage >= 1:
+            spot[0] = every
+        if stage >= 2:
+            spot[2 if first_axis == "y" else 1] = every
+        if stage >= 3:
+            spot[1] = spot[2] = every
+        return ref.at[head + tuple(spot)]
+
+    def axis_of(stage, h):
+        return ("z", ("y", "x")[h], ("x", "y")[h], "c")[stage]
+
+    base = (0, pos.Z - 1, pos.Z - 1 + pos.X - 1, pos.Z - 1 + pos.X - 1 + pos.Y - 1)
+
+    def copies(m, stage, h, arriving):
+        axis = axis_of(stage, h)
+        size = pos.sizes[axis]
+        for k in pos.others(axis):
+            k_sem = base[stage] + k - 1
+            to = pos.moved(axis, k)
+            who = pos.moved(axis, size - k) if arriving else at
+            mine = region(w_all, (m, h), stage, h, who)
+            src = w_own.at[m, h] if stage == 0 and not arriving else mine
+            yield remote(src, mine, snd.at[h, m, k_sem], rcv.at[h, m, k_sem], pos.device(to))
+
+    def local(m, h):
+        return pltpu.make_async_copy(
+            w_own.at[m, h], w_all.at[m, h, z, x, y, c], loc.at[h, m]
+        )
+
+    def begin(m):
+        for h in range(2):
+            local(m, h).start()
+            for copy in copies(m, 0, h, False):
+                copy.start()
+
+    def advance(m, stage):
+        for h in range(2):
+            if stage == 1:
+                local(m, h).wait()
+            for copy in copies(m, stage - 1, h, True):
+                copy.wait_recv()
+            if stage < 4:
+                for copy in copies(m, stage, h, False):
+                    copy.start()
+
+    def load(m, h):
+        return pltpu.make_async_copy(
+            w_all.at[m, h],
+            wbuf.at[lax.rem(m, 2), :, :, :, :, :, pl.ds(h * HALF, HALF)],
+            loc.at[h, parts + lax.rem(m, 2)],
+        )
+
+    def vcopies(stage, arriving):
+        axis = axis_of(stage, 0)
+        size = pos.sizes[axis]
+        for k in pos.others(axis):
+            k_sem = base[stage] + k - 1
+            to = pos.moved(axis, k)
+            who = pos.moved(axis, size - k) if arriving else at
+            mine = region(vall, (), stage, 0, who)
+            yield remote(mine, mine, vsnd.at[k_sem], vrcv.at[k_sem], pos.device(to))
+
+    if tag == 0:
+        vall[z, x, y, c] = vin[...]
+        for copy in vcopies(0, False):
+            copy.start()
+    begin(0)
+    begin(1)
+    if tag == 0:
+        for stage in range(1, 5):
+            for copy in vcopies(stage - 1, True):
+                copy.wait_recv()
+            if stage < 4:
+                for copy in vcopies(stage, False):
+                    copy.start()
+        per = d // (seq * row)
+        rows = []
+        for q in range(d // LANE):
+            pieces = []
+            for e in range(LANE // per):
+                i = q * (LANE // per) + e
+                spot = (i // (2 * pos.Y * pos.X), i // (2 * pos.Y) % pos.X, i // 2 % pos.Y, i % 2)
+                pieces.append(vall[spot][:, :per].astype(F32))
+            rows.append(jnp.concatenate(pieces, axis=-1))
+        for q, value in enumerate(rows):
+            for l in range(2):
+                vec_out[l, :, q * LANE : (q + 1) * LANE] = value[l * 8 : l * 8 + 8]
+        vec = vec_out.at[0]
+    else:
+        vec = vin
+    norm_rows(u, vec, n, low, mean, inv)
+
+    def gates(m):
+        for h in range(2):
+            load(m, h).wait()
+        w = wbuf[lax.rem(m, 2)].reshape(d, 2 * HALF)
+        proj[...] = jnp.dot(low[...], w, preferred_element_type=F32).reshape(steps, SUB, 2 * HALF)
+        for h in range(2):
+            cols = pl.ds(pl.multiple_of(m * 2 * LANE + h * LANE, LANE), LANE)
+            peep, bias, rbias = (
+                jnp.broadcast_to(vec[k : k + 1, cols], (SUB, LANE)) for k in (FPEEP, FBIAS, RBIAS)
+            )
+            off = h * HALF
+
+            def one(i, carry):
+                scale, state = carry
+                cd = proj[i, :, off : off + LANE]
+                zf = proj[i, :, off + LANE : off + 2 * LANE] + peep * n[i, :, cols] + bias
+                up, down = both_sigmoids(zf)
+                f[i, :, cols] = up
+                g[i, :, cols] = down
+                cand[i, :, cols] = cd
+                rpre[i, :, cols] = proj[i, :, off + 2 * LANE : off + 3 * LANE] + rbias
+                a = up * keep[i]
+                return scale * a, a * state + down * cd
+
+            start = jnp.ones((SUB, LANE), F32), jnp.zeros((SUB, LANE), F32)
+            scale, state = lax.fori_loop(0, steps, one, start, unroll=8)
+            ends[0, :, cols] = scale
+            ends[1, :, cols] = state
+        for copy in stash(m):
+            copy.start()
+
+    def stash(m):
+        cols = pl.ds(pl.multiple_of(m * 2 * LANE, 2 * LANE), 2 * LANE)
+        for k, (src, dst) in enumerate(
+            ((f, f_out), (g, g_out), (cand, cand_out), (rpre, rpre_out))
+        ):
+            yield pltpu.make_async_copy(src.at[:, :, cols], dst.at[:, :, cols], outs.at[k, m])
+
+    def turn(i, _):
+        @pl.when(i + 2 < parts)
+        def _():
+            begin(i + 2)
+
+        for stage in range(1, 5):
+            m = i - (stage - 1)
+
+            @pl.when((m >= 0) & (m < parts))
+            def _():
+                advance(m, stage)
+                if stage == 4:
+                    for h in range(2):
+                        load(m, h).start()
+
+        @pl.when(i >= 4)
+        def _():
+            gates(i - 4)
+
+        return 0
+
+    lax.fori_loop(0, parts + 4, turn, 0)
+
+    scale, state = ends[0], ends[1]
+    share_ends(table, total_of(scale, state, False), xsnd, xrcv, seq)
+    first[...] = entering(table, scale, state, seq, False)
+
+    def finish(m, _):
+        for h in range(2):
+            for stage in range(4):
+                for copy in copies(m, stage, h, False):
+                    copy.wait_send()
+        for copy in stash(m):
+            copy.wait()
+        return 0
+
+    lax.fori_loop(0, parts, finish, 0)
+    if tag == 0:
+        for stage in range(4):
+            for copy in vcopies(stage, False):
+                copy.wait_send()
+
+
+def call_gather(seq, row, tag, u, keep, vin, w_own):
+    steps, _, d = u.shape
+    parts, _, per, _ = w_own.shape
+    Y = row // 2
+    X = Y
+    Z = seq // X
+    act, stat = arr(steps, SUB, d), arr(steps, SUB, LANE)
+    vmem = pl.BlockSpec(memory_space=pltpu.VMEM)
+    hbm = pl.BlockSpec(memory_space=pl.ANY)
+    count = Z + X + Y - 2
+    dma = pltpu.SemaphoreType.DMA
+    big = pltpu.VMEM((steps, SUB, d), F32)
+    return pl.pallas_call(
+        lambda *refs: gather_gates(seq, row, tag, *refs),
+        in_specs=[vmem, vmem, vmem, hbm],
+        out_specs=[hbm] + [vmem] * (tag == 0) + [vmem] * 3 + [hbm] * 4 + [vmem],
+        out_shape=[arr(parts, 2, Z, X, Y, 2, per, HALF, dtype=BF16)]
+        + [arr(2, 8, d)] * (tag == 0)
+        + [arr(steps * SUB, d, dtype=BF16), stat, stat]
+        + [act] * 4
+        + [arr(SUB, d)],
+        scratch_shapes=[
+            pltpu.VMEM((seq, 2, d), F32),
+            pltpu.VMEM((2, SUB, d), F32),
+            big,
+            pltpu.VMEM((steps, SUB, 2 * HALF), F32),
+            pltpu.VMEM((2, Z, X, Y, 2, per, 2 * HALF), BF16),
+            big, big, big, big,
+        ]
+        + [pltpu.VMEM((Z, X, Y, 2, 16, LANE), BF16)] * (tag == 0)
+        + [
+            dma((2, parts, count)),
+            dma((2, parts, count)),
+            dma((2, parts + 2)),
+            dma((4, parts)),
+            dma((seq,)),
+            dma((seq,)),
+        ]
+        + [dma((count,)), dma((count,))] * (tag == 0),
+        compiler_params=pltpu.CompilerParams(
+            collective_id=tag, has_side_effects=True, vmem_limit_bytes=60 << 20
+        ),
+        name="gather_gates" + str(tag),
+    )(u, keep, vin, w_own)
+
+
+SLOTS = 4
+
+
+def scatter_weight(
+    seq, row, low_t, du, out, send0, recv0, keep1, send1, recv1, keep2, send2, recv2, keep3,
+    send3, recv3, done, snd, rcv, outs
+):
+    pos = Place(seq, row)
+    at = pos.at
+    parts = du.shape[0]
+    _, Z, X, Y, per, t = low_t.shape
+    pos.barrier(seq)
+    every = slice(None)
+    base = (0, 1, 1 + max(X, Y) - 1, 1 + 2 * (max(X, Y) - 1))
+
+    def axis_of(stage, h):
+        return ("c", ("x", "y")[h], ("y", "x")[h], "z")[stage]
+
+    bufs = ((send0, recv0), (send1, recv1), (send2, recv2), (send3, recv3))
+
+    def copy(m, stage, h, k):
+        slot = lax.rem(m, SLOTS)
+        send, recv = bufs[stage]
+        sem = base[stage] + k - 1
+        to = pos.device(pos.moved(axis_of(stage, h), k))
+        return remote(
+            send.at[slot, h, k - 1], recv.at[slot, h, k - 1],
+            snd.at[slot, h, sem], rcv.at[slot, h, sem], to,
+        )
+
+    def ready(m, stage, h):
+        for k in pos.others(axis_of(stage, h)):
+            @pl.when(m >= SLOTS)
+            def _():
+                copy(m, stage, h, k).wait_send()
+
+    def start(m, stage, h):
+        for k in pos.others(axis_of(stage, h)):
+            copy(m, stage, h, k).start()
+
+    def arrive(m, stage, h):
+        for k in pos.others(axis_of(stage, h)):
+            copy(m, stage, h, k).wait_recv()
+
+    def stage0(m):
+        slot = lax.rem(m, SLOTS)
+        rows = low_t[1 - at["c"]].reshape(-1, t)
+        for h in range(2):
+            ready(m, 0, h)
+            v = jnp.dot(rows, du[m, h], preferred_element_type=F32).astype(BF16)
+            send0[slot, h, 0] = v.reshape(Z, X, Y, per, HALF)
+            start(m, 0, h)
+
+    def stage1(m):
+        slot = lax.rem(m, SLOTS)
+        for h in range(2):
+            axis = axis_of(1, h)
+            arrive(m, 0, h)
+            ready(m, 1, h)
+            for k in range(pos.sizes[axis]):
+                p = pos.moved(axis, k)[axis]
+                where = (every, p) if h == 0 else (every, every, p)
+                rows = low_t[(at["c"],) + where].reshape(-1, t)
+                v = jnp.dot(rows, du[m, h], preferred_element_type=F32)
+                got = recv0[(slot, h, 0) + where]
+                v = v.reshape(got.shape) + got.astype(F32)
+                if k == 0:
+                    keep1[slot, h] = v
+                else:
+                    send1[slot, h, k - 1] = v.astype(BF16)
+            start(m, 1, h)
+
+    def stage2(m):
+        slot = lax.rem(m, SLOTS)
+        for h in range(2):
+            axis = axis_of(2, h)
+            arrive(m, 1, h)
+            ready(m, 2, h)
+            for k in range(pos.sizes[axis]):
+                p = pos.moved(axis, k)[axis]
+                v = keep1[slot, h, :, p]
+                for e in pos.others(axis_of(1, h)):
+                    v = v + recv1[slot, h, e - 1, :, p].astype(F32)
+                if k == 0:
+                    keep2[slot, h] = v
+                else:
+                    send2[slot, h, k - 1] = v.astype(BF16)
+            start(m, 2, h)
+
+    def stage3(m):
+        slot = lax.rem(m, SLOTS)
+        for h in range(2):
+            arrive(m, 2, h)
+            ready(m, 3, h)
+            for k in range(Z):
+                p = pos.moved("z", k)["z"]
+                v = keep2[slot, h, p]
+                for e in pos.others(axis_of(2, h)):
+                    v = v + recv2[slot, h, e - 1, p].astype(F32)
+                if k == 0:
+                    keep3[slot, h] = v
+                else:
+                    send3[slot, h, k - 1] = v.astype(BF16)
+            start(m, 3, h)
+
+    def result(m, h, e):
+        d = out.shape[-1] // 3
+        cols = pl.ds(pl.multiple_of(e * d + (2 * m + h) * LANE, LANE), LANE)
+        return pltpu.make_async_copy(
+            done.at[m, h, :, e * LANE : (e + 1) * LANE], out.at[:, cols], outs.at[m, h, e]
+        )
+
+    def stage4(m):
+        slot = lax.rem(m, SLOTS)
+        for h in range(2):
+            arrive(m, 3, h)
+            v = keep3[slot, h]
+            for k in range(1, Z):
+                v = v + recv3[slot, h, k - 1].astype(F32)
+            done[m, h] = v
+            for e in range(3):
+                result(m, h, e).start()
+
+    def turn(i, _):
+        for stage, act in enumerate((stage0, stage1, stage2, stage3, stage4)):
+            m = i - stage
+
+            @pl.when((m >= 0) & (m < parts))
+            def _():
+                act(m)
+
+        return 0
+
+    lax.fori_loop(0, parts + 4, turn, 0)
+
+    def finish(m, _):
+        for stage in range(4):
+            for h in range(2):
+                for k in pos.others(axis_of(stage, h)):
+                    copy(m, stage, h, k).wait_send()
+        return 0
+
+    lax.fori_loop(max(parts - SLOTS, 0), parts, finish, 0)
+
+    def written(m, _):
+        for h in range(2):
+            for e in range(3):
+                result(m, h, e).wait()
+        return 0
+
+    lax.fori_loop(0, parts, written, 0)
+
+
+def call_scatter(seq, row, tag, low_t, du, d):
+    parts, _, t, _ = du.shape
+    _, Z, X, Y, per, _ = low_t.shape
+    vmem = pl.BlockSpec(memory_space=pltpu.VMEM)
+    count = 1 + 2 * (X - 1) + Z - 1
+    dma = pltpu.SemaphoreType.DMA
+
+    def buf(*shape, dtype=BF16):
+        return pltpu.VMEM((SLOTS, 2) + shape, dtype)
+
+    one, two, three = (Z, Y, per, HALF), (Z, per, HALF), (per, HALF)
+    return pl.pallas_call(
+        lambda *refs: scatter_weight(seq, row, *refs),
+        in_specs=[vmem, vmem],
+        out_specs=pl.BlockSpec(memory_space=pl.ANY),
+        out_shape=arr(per, 3 * d),
+        scratch_shapes=[
+            buf(1, Z, X, Y, per, HALF), buf(1, Z, X, Y, per, HALF),
+            buf(*one, dtype=F32), buf(X - 1, *one), buf(X - 1, *one),
+            buf(*two, dtype=F32), buf(Y - 1, *two), buf(Y - 1, *two),
+            buf(*three, dtype=F32), buf(Z - 1, *three), buf(Z - 1, *three),
+            pltpu.VMEM((parts, 2, per, HALF), F32),
+            dma((SLOTS, 2, count)), dma((SLOTS, 2, count)), dma((parts, 2, 3)),
+        ],
+        compiler_params=pltpu.CompilerParams(
+            collective_id=tag, has_side_effects=True, vmem_limit_bytes=60 << 20
+        ),
+        name="scatter_weight" + str(tag),
+    )(low_t, du)
 
 
 def columns(steps, width):
@@ -245,6 +732,10 @@
     steps = t // SUB
     parts = d // WIDE
     axes = ("seq", "row")
+    seq, row = lax.axis_size("seq"), lax.axis_size("row")
+    Y = row // 2
+    X = Y
+    Z = seq // X
 
     def permuted(x):
         return x.reshape(SUB, steps, -1).transpose(1, 0, 2)
@@ -253,39 +744,30 @@
         return x.reshape(steps, SUB, d).transpose(1, 0, 2).reshape(1, t, d)
 
     keep = permuted((1 - resets[0]).astype(F32)[:, None])
-    keep = jnp.broadcast_to(keep, (steps, SUB, 128))
-    packed = jnp.stack(rows + (jnp.zeros_like(rows[0]),) * 2, axis=1)
-    every = lax.all_gather(packed, axes, axis=2, tiled=True).astype(F32)
-    local = weight.reshape(layers, -1, 3, parts, WIDE).transpose(0, 3, 1, 2, 4)
-    local = local.reshape(layers, parts, -1, 3 * WIDE)
-    full = [lax.all_gather(local[l], axes, axis=1, tiled=True) for l in range(layers)]
+    keep = jnp.broadcast_to(keep, (steps, SUB, LANE))
+    per = rows[0].shape[-1]
+    packed = jnp.stack(rows + (jnp.zeros_like(rows[0]),) * 2, axis=1).reshape(2 * 8, per)
+    packed = jnp.pad(packed, ((0, 0), (0, LANE - per)))
+    local = weight.reshape(layers, -1, 3, parts, 2, LANE).transpose(0, 3, 4, 1, 2, 5)
+    local = local.reshape(layers, parts, 2, -1, HALF)
 
     u = permuted(tokens).astype(F32)
     stored = []
     col = columns(steps, WIDE)
     keep_spec = whole(steps, SUB, 128)
-    w_spec = pl.BlockSpec((1, d, 3 * WIDE), lambda j: (j, 0, 0))
-    du_spec = pl.BlockSpec((1, t, 3 * WIDE), lambda j: (j, 0, 0))
+    w_spec = pl.BlockSpec((1, 2, d, HALF), lambda j: (j, 0, 0, 0))
+    du_spec = pl.BlockSpec((1, 2, t, HALF), lambda j: (j, 0, 0, 0))
     act = arr(steps, SUB, d)
-    stat = arr(steps, SUB, 128)
     for l in range(layers):
+        if l == 0:
+            full, every, low, mean, inv, f, g, cand, rpre, first = call_gather(
+                seq, row, 0, u, keep, packed, local[0]
+            )
+        else:
+            full, low, mean, inv, f, g, cand, rpre, first = call_gather(
+                seq, row, 1, u, keep, every[1], local[1]
+            )
         vec = every[l]
-        low, mean, inv, f, g, cand, rpre, ends = pl.pallas_call(
-            forward_gates,
-            grid=(parts,),
-            in_specs=[whole(steps, SUB, d), keep_spec, whole(8, d), w_spec],
-            out_specs=[
-                whole(t, d), keep_spec, keep_spec, col, col, col, col,
-                pl.BlockSpec((2, SUB, WIDE), lambda j: (0, 0, j)),
-            ],
-            out_shape=[arr(t, d, dtype=BF16), stat, stat, act, act, act, act, arr(2, SUB, d)],
-            scratch_shapes=[
-                pltpu.VMEM((steps, SUB, d), F32), pltpu.VMEM((steps, SUB, 3 * WIDE), F32)
-            ],
-            compiler_params=params(),
-            name="forward_gates",
-        )(u, keep, vec, full[l])
-        first = chain(ends, "seq", False)
         p, r, out = pl.pallas_call(
             forward_states,
             grid=(parts,),
@@ -295,7 +777,7 @@
             compiler_params=params(),
             name="forward_states",
         )(f, g, cand, rpre, u, keep, vec, first)
-        stored.append((u, low, mean, inv, f, g, cand, p, r))
+        stored.append((u, low, mean, inv, f, g, cand, p, r, full.reshape(parts, 2, d, HALF)))
         u = out
     result = restored(u.astype(BF16))
 
@@ -303,7 +785,7 @@
     weight_grads, vector_grads = [None] * layers, [None] * layers
     for l in reversed(range(layers)):
         vec = every[l]
-        u, low, mean, inv, f, g, cand, p, r = stored[l]
+        u, low, mean, inv, f, g, cand, p, r, full = stored[l]
         ends = pl.pallas_call(
             backward_ends,
             grid=(parts,),
@@ -319,20 +801,13 @@
             grid=(parts,),
             in_specs=[col] * 7 + [keep_spec, vectors(WIDE), keep_spec, keep_spec, vectors(WIDE)],
             out_specs=[du_spec, col, pl.BlockSpec((4, SUB, WIDE), lambda j: (0, 0, j))],
-            out_shape=[arr(parts, t, 3 * WIDE, dtype=BF16), act, arr(4, SUB, d)],
+            out_shape=[arr(parts, 2, t, HALF, dtype=BF16), act, arr(4, SUB, d)],
             scratch_shapes=[pltpu.VMEM((3, steps, SUB, WIDE), F32)],
             compiler_params=params(),
             name="backward_states",
         )(dh, f, g, cand, p, r, u, keep, vec, mean, inv, first)
-        grad = pl.pallas_call(
-            weight_side,
-            grid=(parts,),
-            in_specs=[whole(d, t), du_spec],
-            out_specs=w_spec,
-            out_shape=arr(parts, d, 3 * WIDE),
-            compiler_params=params(),
-            name="weight_side",
-        )(low.T, du)
+        low_t = low.T.reshape(Z, X, Y, 2, per, t).transpose(3, 0, 1, 2, 4, 5)
+        weight_grads[l] = call_scatter(seq, row, 2 + l, low_t, du, d)
         dh, more = pl.pallas_call(
             input_side,
             grid=(parts,),
@@ -344,11 +819,7 @@
             scratch_shapes=[pltpu.VMEM((steps, SUB, d), F32)],
             compiler_params=params(),
             name="input_side",
-        )(du, full[l], dzf, u, dh, r, mean, inv, vec)
-        grad = lax.psum_scatter(grad, axes, scatter_dimension=1, tiled=True)
-        weight_grads[l] = (
-            grad.reshape(parts, -1, 3, WIDE).transpose(1, 2, 0, 3).reshape(-1, 3 * d)
-        )
+        )(du, full, dzf, u, dh, r, mean, inv, vec)
         vector_grads[l] = jnp.concatenate([more.sum(1), sums.sum(1)])
     input_grad = restored(dh.astype(BF16))
     vector_out = lax.psum_scatter(

time: 1730 us -> 969 us (0.56)
  waiting for transfers between devices: 1330 us -> 173 us
  Pallas kernels: 250 us -> 712 us
  blocking collectives: 49.7 us -> 0 us
    reduce_scatter x2 -> x0, waiting for transfers between devices: 861 us -> none  [body(): grad = lax.psum_scatter(grad, axes, scatter_dimension=1, tiled=True)]
    pallas_call x4, Pallas kernels: 97.5 us -> 551 us  [the longest x2 292 us: call_gather(): pl.pallas_call(lambda *refs: gather_gates(seq, row, tag, *refs), in_specs...]
    all_gather x2 -> x0, waiting for transfers between devices: 242 us -> none  [body(): lax.all_gather(local[l], axes, axis=1, tiled=True)]
    all_gather x4 -> x2, waiting for transfers between devices: 149 us -> 44.1 us  [chain(): everyone = lax.all_gather(ends, axis)]
    unnamed x10 -> x4, waiting for transfers between devices: 76.3 us -> 129 us
    all_gather x1 -> x0, blocking collectives: 49.7 us -> none  [body(): every = lax.all_gather(packed, axes, axis=2, tiled=True).astype(F32)]
  transfers between devices with their start and end apart: 9 -> 3, of which waited for: 9 -> 2; matrix products, arithmetic and copies ran while one was open for 2% -> 2% of each run, Pallas kernels for 3% -> 13%
where the time goes in v2:
time: 969 us; the launch traced here: 968 us
  Pallas kernels  712 us (73%)
  waiting for transfers between devices  173 us (18%)
  local copies, waits for them, and re-layouts  63 us (7%)
  between operations  14 us (1%)
    pallas_call x2, Pallas kernels, call_gather(): pl.pallas_call(lambda *refs: gather_gates(seq, row, tag, *refs), in_specs...  292 us
    pallas_call x2, Pallas kernels, call_scatter(): pl.pallas_call(lambda *refs: scatter_weight(seq, row, *refs), in_specs=[v...  260 us
    unnamed x4, waiting for transfers between devices  129 us
    pallas_call x2, Pallas kernels, body(): pl.pallas_call(input_side, grid=(parts,), in_specs=[du_spec, w_spec] + [w...  72.2 us
    all_gather x2, waiting for transfers between devices, chain(): everyone = lax.all_gather(ends, axis)  44.1 us
    pallas_call x2, Pallas kernels, body(): pl.pallas_call(backward_states, grid=(parts,), in_specs=[col] * 7 + [keep...  34.7 us
    pallas_call x2, Pallas kernels, body(): pl.pallas_call(forward_states, grid=(parts,), in_specs=[col] * 5 + [keep_...  28.8 us
    pallas_call x2, Pallas kernels, body(): pl.pallas_call(backward_ends, grid=(parts,), in_specs=[col] * 7 + [keep_s...  24.8 us
  transfers between devices with their start and end apart: 3, of which 2 were waited for; matrix products, arithmetic and copies ran while one was open for 2% of the time, Pallas kernels for 13%

profile of v2, /device:TPU:0, one launch (start us, length us, event | category | flops | bytes accessed | tf_op | source)
XLA Modules:
  0.0 967.9 jit_solution(14048024675721826926)
XLA Ops:
  12.7 4.1 reshape.70
  21.6 4.8 copy.89
  26.4 3.2 copy.88
  30.5 147.0 %gather_gates0.1 = (bf16[8,2,4,2,2,2,64,384]{7,6,5,4,3,2,1,0:T(8,128)(2,1)}, f32[2,8,2048]{2,1,0:T(8,128)}, bf16[512,2048]{1,0:T(8,128)(2,1)}, f32[64,8,128]{2,1...) custom-call(f32[64,8,2048]{2,1,0:T(8,128)} %bitcast.74, ...), custom_call_target="tpu_custom_call" | custom-call | tf_op jit(solution)/shard_map/gather_gates0/pallas_call | solution.py:475
  179.0 14.4 %forward_states.2 = (f32[64,8,2048]{2,1,0:T(8,128)}, f32[64,8,2048]{2,1,0:T(8,128)}, f32[64,8,2048]{2,1,0:T(8,128)}) custom-call(f32[64,8,2048]{2,1,0:T(8,128)} %get-tuple-element.44.f, f32[64,8,2048]{2,1,0:T(8,128)} %get-tuple-element.45.g, f32[64,8,2048]{2,1,0:T(8,128)} %get-tuple-element.46.cand, f32[64,8,2048]{2,1,0:T(8,128)} %get-tuple-element.47.rpre, ...), custom_call_target="tpu_custom_call" | custom-call | tf_op jit(solution)/shard_map/forward_states/pallas_call | solution.py:771
  193.4 144.6 %gather_gates1.1 = (bf16[8,2,4,2,2,2,64,384]{7,6,5,4,3,2,1,0:T(8,128)(2,1)}, bf16[512,2048]{1,0:T(8,128)(2,1)}, f32[64,8,128]{2,1,0:T(8,128)}, f32[64,8,128]{2,1...) custom-call(f32[64,8,2048]{2,1,0:T(8,128)} %get-tuple-element.50.ref, ...), custom_call_target="tpu_custom_call" | custom-call | tf_op jit(solution)/shard_map/gather_gates1/pallas_call | solution.py:475
  338.0 14.4 %forward_states.3 = (f32[64,8,2048]{2,1,0:T(8,128)}, f32[64,8,2048]{2,1,0:T(8,128)}, f32[64,8,2048]{2,1,0:T(8,128)}) custom-call(f32[64,8,2048]{2,1,0:T(8,128)} %get-tuple-element.51.f, f32[64,8,2048]{2,1,0:T(8,128)} %get-tuple-element.52.g, f32[64,8,2048]{2,1,0:T(8,128)} %get-tuple-element.53.cand, f32[64,8,2048]{2,1,0:T(8,128)} %get-tuple-element.54.rpre, ...), custom_call_target="tpu_custom_call" | custom-call | tf_op jit(solution)/shard_map/forward_states/pallas_call | solution.py:771
  352.4 12.4 %backward_ends.2 = f32[2,8,2048]{2,1,0:T(8,128)} custom-call(f32[64,8,2048]{2,1,0:T(8,128)} %bitcast.79, f32[64,8,2048]{2,1,0:T(8,128)} %get-tuple-element.51.f, f32[64,8,2048]{2,1,0:T(8,128)} %get-tuple-element.52.g, f32[64,8,2048]{2,1,0:T(8,128)} %get-tuple-element.53.cand, f32[64,8,2048]{2,1,0:T(8,128)} %get-tuple-element.57.p, ...), custom_call_target="tpu_custom_call" | custom-call | tf_op jit(solution)/shard_map/backward_ends/pallas_call | solution.py:789
  364.9 44.1 %all-gather.5.cloned.1.call-done = f32[16,8,2048]{2,1,0:T(8,128)} async-done(((f32[2,8,2048]{2,1,0:T(8,128)}), f32[16,8,2048]{2,1,0:T(8,128)}) %all-gather.5.cloned.1.call-update) | async-done | bytes 1048592 | tf_op jit(solution)/shard_map/all_gather | solution.py:710
  413.0 17.4 %backward_states.2 = (bf16[8,2,512,384]{3,2,1,0:T(8,128)(2,1)}, f32[64,8,2048]{2,1,0:T(8,128)}, f32[4,8,2048]{2,1,0:T(8,128)}) custom-call(f32[64,8,2048]{2,1,0:T(8,128)} %bitcast.80, f32[64,8,2048]{2,1,0:T(8,128)} %get-tuple-element.51.f, f32[64,8,2048]{2,1,0:T(8,128)} %get-tuple-element.52.g, f32[64,8,2048]{2,1,0:T(8,128)} %get-tuple-element.53.cand, ...), custom_call_target="tpu_custom_call" | custom-call | tf_op jit(solution)/shard_map/backward_states/pallas_call | solution.py:799
  430.4 36.0 %input_side.2 = (f32[64,8,2048]{2,1,0:T(8,128)}, f32[2,8,2048]{2,1,0:T(8,128)}) custom-call(bf16[8,2,512,384]{3,2,1,0:T(8,128)(2,1)} %get-tuple-element.61.du.refs_1_, bf16[8,2,2048,384]{3,2,1,0:T(8,128)(2,1)} %bitcast.84, f32[64,8,2048]{2,1,0:T(8,128)} %get-tuple-element.63.dzf, f32[64,8,2048]{2,1,0:T(8,128)} %get-tuple-element.50.refs_0_.u, ...), custom_call_target="tpu_custom_call" | custom-call | tf_op jit(solution)/shard_map/input_side/pallas_call | solution.py:811
  466.4 12.4 %backward_ends.3 = f32[2,8,2048]{2,1,0:T(8,128)} custom-call(f32[64,8,2048]{2,1,0:T(8,128)} %get-tuple-element.64.dh, f32[64,8,2048]{2,1,0:T(8,128)} %get-tuple-element.44.f, f32[64,8,2048]{2,1,0:T(8,128)} %get-tuple-element.45.g, f32[64,8,2048]{2,1,0:T(8,128)} %get-tuple-element.46.cand, f32[64,8,2048]{2,1,0:T(8,128)} %get-tuple-element.65.p, ...), custom_call_target="tpu_custom_call" | custom-call | tf_op jit(solution)/shard_map/backward_ends/pallas_call | solution.py:789
  478.9 3.1 copy.67
  483.5 2.9 copy.69
  489.6 2.5 copy.60
  492.1 129.7 %scatter_weight3.1 = f32[64,6144]{1,0:T(8,128)} custom-call(bf16[2,4,2,2,64,512]{5,4,3,2,1,0:T(8,128)(2,1)} %bitcast.86, bf16[8,2,512,384]{3,2,1,0:T(8,128)(2,1)} %get-tuple-element.61.du.refs_1_), custom_call_target="tpu_custom_call" | custom-call | tf_op jit(solution)/shard_map/scatter_weight3/pallas_call | solution.py:673
  626.1 17.3 %backward_states.3 = (bf16[8,2,512,384]{3,2,1,0:T(8,128)(2,1)}, f32[64,8,2048]{2,1,0:T(8,128)}, f32[4,8,2048]{2,1,0:T(8,128)}) custom-call(f32[64,8,2048]{2,1,0:T(8,128)} %get-tuple-element.64.dh, f32[64,8,2048]{2,1,0:T(8,128)} %get-tuple-element.44.f, f32[64,8,2048]{2,1,0:T(8,128)} %get-tuple-element.45.g, f32[64,8,2048]{2,1,0:T(8,128)} %get-tuple-element.46.cand, ...), custom_call_target="tpu_custom_call" | custom-call | tf_op jit(solution)/shard_map/backward_states/pallas_call | solution.py:799
  643.4 130.0 %scatter_weight2.1 = f32[64,6144]{1,0:T(8,128)} custom-call(bf16[2,4,2,2,64,512]{5,4,3,2,1,0:T(8,128)(2,1)} %bitcast.85, bf16[8,2,512,384]{3,2,1,0:T(8,128)(2,1)} %get-tuple-element.69.du.refs_1_), custom_call_target="tpu_custom_call" | custom-call | tf_op jit(solution)/shard_map/scatter_weight2/pallas_call | solution.py:673
  773.4 36.2 %input_side.3 = (f32[64,8,2048]{2,1,0:T(8,128)}, f32[2,8,2048]{2,1,0:T(8,128)}) custom-call(bf16[8,2,512,384]{3,2,1,0:T(8,128)(2,1)} %get-tuple-element.69.du.refs_1_, bf16[8,2,2048,384]{3,2,1,0:T(8,128)(2,1)} %bitcast.83, f32[64,8,2048]{2,1,0:T(8,128)} %get-tuple-element.71.dzf, f32[64,8,2048]{2,1,0:T(8,128)} %bitcast.78, ...), custom_call_target="tpu_custom_call" | custom-call | tf_op jit(solution)/shard_map/input_side/pallas_call | solution.py:811
  810.9 4.7 copy.71
  815.5 6.4 reshape.81
  822.0 1.9 pad_maximum_fusion
  825.6 2.5 copy.66
  828.1 128.5 %reduce-scatter.4.cloned.1.call-done = f32[64,12]{1,0:T(8,128)} async-done(((f32[2048,12]{1,0:T(8,128)}), f32[64,12]{1,0:T(8,128)}) %reduce-scatter.4.cloned.1.call-update) | async-done | bytes 3088
  (73 shorter events, 33.5 us)
Async XLA Ops:
  7.2 401.8 %all-gather.5.cloned.1.call-start = ((), (), s32[]{:S(2)}) async-start(), calls=%async_computation.1 | async-start | bytes 1179648 | tf_op jit(solution)/shard_map/all_gather | solution.py:710
  20.2 6.2 copy-start.4
  364.9 257.2 %all-gather.7.cloned.1.call-start = ((), (), s32[]{:S(2)}) async-start(), calls=%async_computation.2 | async-start | bytes 1179648 | tf_op jit(solution)/shard_map/all_gather | solution.py:710
  478.8 477.7 %reduce-scatter.4.cloned.1.call-start = ((), (), s32[]{:S(2)}) async-start(), calls=%async_computation.3 | async-start | bytes 1081344
  486.3 2.9 copy-start.2
  492.1 129.7 %copy-start.7 = (f32[2,8,2048]{2,1,0:T(8,128)S(1)}, f32[2,8,2048]{2,1,0:T(8,128)}, u32[]{:S(2)}) copy-start(f32[2,8,2048]{2,1,0:T(8,128)} %get-tuple-element.77) | copy-start | bytes 393220
  492.1 129.8 %copy-start.5 = (f32[4,8,2048]{2,1,0:T(8,128)S(1)}, f32[4,8,2048]{2,1,0:T(8,128)}, u32[]{:S(2)}) copy-start(f32[4,8,2048]{2,1,0:T(8,128)} %get-tuple-element.78) | copy-start | bytes 786436
  773.4 37.2 %copy-start.6 = (f32[4,8,2048]{2,1,0:T(8,128)S(1)}, f32[4,8,2048]{2,1,0:T(8,128)}, u32[]{:S(2)}) copy-start(f32[4,8,2048]{2,1,0:T(8,128)} %get-tuple-element.76) | copy-start | bytes 786436
  815.5 6.4 copy-start
  815.5 6.4 copy-start.1
  821.9 3.3 copy-start.3
Sparse Core Ops, SparseCore 0:
  365.0 43.9 all-gather.4
  478.9 43.2 all-gather.6
  822.1 134.4 reduce-scatter.3

commit v3 on v0

v3 whole, which is shorter than its diff:
```python
import jax
import jax.numpy as jnp
from jax import lax
from jax.experimental import pallas as pl
from jax.experimental.pallas import tpu as pltpu
from jax.sharding import PartitionSpec as P

epsilon = 1e-05
SUB = 8
WIDE = 256
F32 = jnp.float32
BF16 = jnp.bfloat16
GAIN, SHIFT, FPEEP, RPEEP, FBIAS, RBIAS = range(6)


def both_sigmoids(z):
    tail = jnp.exp(-jnp.abs(z))
    big = 1.0 / (1.0 + tail)
    small = tail * big
    up = z >= 0
    return jnp.where(up, big, small), jnp.where(up, small, big)


def lanes(value, width):
    return jnp.concatenate([value] * (width // value.shape[-1]), axis=-1)


def arr(*shape, dtype=F32):
    return jax.ShapeDtypeStruct(shape, dtype)


MESH = pl.DeviceIdType.MESH
HALF = 384
LANE = 128


class Place:
    def __init__(self, seq, row):
        self.Y = row // 2
        self.X = self.Y
        self.Z = seq // self.X
        self.C = 2
        self.sizes = dict(z=self.Z, x=self.X, y=self.Y, c=self.C)
        s, r = lax.axis_index("seq"), lax.axis_index("row")
        self.at = dict(z=s // self.X, x=s % self.X, y=r // 2, c=r % 2)
        self.zl = lax.rem(self.at["z"], 2)

    def moved(self, axis, k):
        size = self.sizes[axis]
        return dict(self.at, **{axis: lax.rem(self.at[axis] + k, size)})

    def device(self, at):
        return {"seq": at["z"] * self.X + at["x"], "row": at["y"] * 2 + at["c"]}

    def others(self, axis):
        return range(1, self.sizes[axis])

    def barrier(self, seq):
        sem = pltpu.get_barrier_semaphore()
        count = 0
        s, r = lax.axis_index("seq"), lax.axis_index("row")
        for k in range(1, seq):
            pl.semaphore_signal(
                sem, inc=1, device_id={"seq": lax.rem(s + k, seq), "row": r}, device_id_type=MESH
            )
            count += 1
        for axis in ("y", "c"):
            for k in self.others(axis):
                pl.semaphore_signal(
                    sem, inc=1, device_id=self.device(self.moved(axis, k)), device_id_type=MESH
                )
                count += 1
        pl.semaphore_wait(sem, count)


def remote(src, dst, send, recv, to):
    return pltpu.make_async_remote_copy(
        src_ref=src, dst_ref=dst, send_sem=send, recv_sem=recv, device_id=to, device_id_type=MESH
    )


def total_of(scale, state, backward):
    order = range(SUB - 1, -1, -1) if backward else range(SUB)
    whole_scale, whole_state = None, None
    for k in order:
        a, b = scale[k : k + 1], state[k : k + 1]
        if whole_scale is None:
            whole_scale, whole_state = a, b
        else:
            whole_scale, whole_state = a * whole_scale, a * whole_state + b
    return jnp.concatenate([whole_scale, whole_state], axis=0)


class Gather:
    def __init__(self, pos, parts, w_own, w_all, snd, rcv, loc):
        self.pos, self.parts = pos, parts
        self.w_own, self.w_all, self.snd, self.rcv, self.loc = w_own, w_all, snd, rcv, loc
        z, x, y = pos.Z - 1, pos.X - 1, pos.Y - 1
        self.base = (0, z, z + max(x, y), z + 2 * max(x, y))

    def axis(self, stage, h):
        return ("z", ("y", "x")[h], ("x", "y")[h], "c")[stage]

    def region(self, ref, head, stage, h, who):
        every = slice(None)
        spot = [who["z"], who["x"], who["y"], who["c"]]
        if stage >= 1:
            spot[0] = every
        if stage >= 2:
            spot[2 if h == 0 else 1] = every
        if stage >= 3:
            spot[1] = spot[2] = every
        return ref.at[head + tuple(spot)]

    def copies(self, g, stage, h, arriving):
        pos, axis = self.pos, self.axis(stage, h)
        l, m = g // self.parts, lax.rem(g, self.parts)
        size = pos.sizes[axis]
        for k in pos.others(axis):
            sem = self.base[stage] + k - 1
            to = pos.moved(axis, k)
            who = pos.moved(axis, size - k) if arriving else pos.at
            mine = self.region(self.w_all, (l, m, h), stage, h, who)
            src = mine
            if stage == 0 and not arriving:
                src = self.w_own.at[l, lax.rem(to["z"], 2), m, h]
            yield remote(src, mine, self.snd.at[h, g, sem], self.rcv.at[h, g, sem], pos.device(to))

    def local(self, g, h):
        at = self.pos.at
        l, m = g // self.parts, lax.rem(g, self.parts)
        return pltpu.make_async_copy(
            self.w_own.at[l, self.pos.zl, m, h],
            self.w_all.at[l, m, h, at["z"], at["x"], at["y"], at["c"]],
            self.loc.at[h, g],
        )

    def begin(self, g):
        for h in range(2):
            self.local(g, h).start()
            for copy in self.copies(g, 0, h, False):
                copy.start()

    def advance(self, g, stage):
        for h in range(2):
            if stage == 1:
                self.local(g, h).wait()
            for copy in self.copies(g, stage - 1, h, True):
                copy.wait_recv()
            if stage < 4:
                for copy in self.copies(g, stage, h, False):
                    copy.start()

    def turn(self, i):
        total = 2 * self.parts

        @pl.when(i + 2 < total)
        def _():
            self.begin(i + 2)

        for stage in range(1, 5):
            g = i - (stage - 1)

            @pl.when((g >= 0) & (g < total))
            def _():
                self.advance(g, stage)

    def finish(self):
        def one(g, _):
            for h in range(2):
                for stage in range(4):
                    for copy in self.copies(g, stage, h, False):
                        copy.wait_send()
            return 0

        lax.fori_loop(0, 2 * self.parts, one, 0)


class Chain:
    def __init__(self, pos, table, snd, rcv):
        self.pos, self.table, self.snd, self.rcv = pos, table, snd, rcv

    def run(self, ends, first, backward):
        pos, table = self.pos, self.table
        zh, x = pos.at["z"] // 2, pos.at["x"]
        r = lax.axis_index("row")
        for b in range(2):
            table[zh, x, b] = total_of(ends[b, 0], ends[b, 1], backward)
        moves = [(i, j) for i in range(pos.Z // 2) for j in range(pos.X) if i or j]

        def copy(k, sign):
            i, j = moves[k]
            there = lax.rem(zh + i, pos.Z // 2), lax.rem(x + j, pos.X)
            back = lax.rem(zh + pos.Z // 2 - i, pos.Z // 2), lax.rem(x + pos.X - j, pos.X)
            spot = (zh, x) if sign > 0 else back
            to = {"seq": (2 * there[0] + pos.zl) * pos.X + there[1], "row": r}
            return remote(table.at[spot], table.at[spot], self.snd.at[k], self.rcv.at[k], to)

        for k in range(len(moves)):
            copy(k, 1).start()
        for k in range(len(moves)):
            copy(k, -1).wait_recv()
        for k in range(len(moves)):
            copy(k, 1).wait_send()
        blocks = [(i, b, j) for i in range(pos.Z // 2) for b in range(2) for j in range(pos.X)]
        if backward:
            blocks = blocks[::-1]
        value = jnp.zeros_like(table[0, 0, 0, 0:1])
        mine = [value, value]
        for i, b, j in blocks:
            here = (i == zh) & (j == x)
            mine[b] = jnp.where(here, value, mine[b])
            value = table[i, j, b, 0:1] * value + table[i, j, b, 1:2]
        for b in range(2):
            value = mine[b]
            for k in range(SUB - 1, -1, -1) if backward else range(SUB):
                first[b, k : k + 1] = value
                value = ends[b, 0, k : k + 1] * value + ends[b, 1, k : k + 1]


def diagonal():
    return lax.broadcasted_iota(jnp.int32, (LANE, LANE), 0) == lax.broadcasted_iota(
        jnp.int32, (LANE, LANE), 1
    )


def to_row(column):
    spread = jnp.broadcast_to(column, (LANE, LANE))
    return jnp.sum(jnp.where(diagonal(), spread, 0.0), axis=0, keepdims=True)


def to_column(line):
    spread = jnp.broadcast_to(line, (LANE, LANE))
    return jnp.sum(jnp.where(diagonal(), spread, 0.0), axis=1, keepdims=True)


def spread_rows(column):
    return jnp.broadcast_to(column, (LANE, LANE)).reshape(LANE // SUB, SUB, LANE)


def lane_tile(m, width):
    return pl.ds(pl.multiple_of(m * width, width), width)


def forward_all(
    seq, row, tok, cot, keep_in, vin, w_own,
    w_all, vec, keep, stats, f0, g0, cand0, p0, r0, u0, low0, low1, u1, dhr1, dn1, du1, result,
    sums, tokbuf, cotbuf, keepc, vall, u, np_, f, g, cand, rpre, low, wbuf, proj, du, resbuf, top_of, ends,
    first, tables, st_own, st_got, st_fin,
    gsnd, grcv, gloc, vsnd, vrcv, wsem, psnd, prcv, csnd, crcv, outs,
):
    pos = Place(seq, row)
    at, zl = pos.at, pos.zl
    z, x, y, c = (at[k] for k in "zxyc")
    _, t, d = tokbuf.shape
    steps, H = u.shape[1], u.shape[3]
    parts = w_own.shape[2]
    partner = pos.device(dict(at, z=z + 1 - 2 * zl))
    own = pl.ds(pl.multiple_of(zl * H, H), H)
    other = pl.ds(pl.multiple_of((1 - zl) * H, H), H)
    rows_of = lambda b: pl.ds(pl.multiple_of(b * t, t), t)
    pos.barrier(seq)

    gather = Gather(pos, parts, w_own, w_all, gsnd, grcv, gloc)
    chains = [Chain(pos, tables.at[k], csnd.at[k], crcv.at[k]) for k in range(3)]

    def pair(k, src, dst):
        return remote(src, dst, psnd.at[k], prcv.at[k], partner)

    def tokens(b):
        return pair(0, tok, tokbuf.at[b])

    def cotangents(b):
        return pair(1, cot.at[:, other], cotbuf.at[b])

    def keeps(b):
        return pair(2, keepc.at[b], keepc.at[b])

    def statistics(b, to):
        return pair(3 + b, st_own.at[b], to.at[b])

    def lows(b, cols):
        return pair(5 + b, low.at[rows_of(b), cols], low.at[rows_of(b), cols])

    def results(cols):
        return pair(7, resbuf.at[1 - zl], result.at[:, cols])

    def vcopies(stage, arriving):
        axis = gather.axis(stage, 0)
        size = pos.sizes[axis]
        for k in pos.others(axis):
            sem = gather.base[stage] + k - 1
            to = pos.moved(axis, k)
            who = pos.moved(axis, size - k) if arriving else at
            mine = gather.region(vall, (), stage, 0, who)
            yield remote(mine, mine, vsnd.at[sem], vrcv.at[sem], pos.device(to))

    def vadvance(stage):
        for copy in vcopies(stage - 1, True):
            copy.wait_recv()
        if stage < 4:
            for copy in vcopies(stage, False):
                copy.start()

    own_tokens = pltpu.make_async_copy(tok, tokbuf.at[zl], outs.at[0])
    own_cot = pltpu.make_async_copy(cot.at[:, own], cotbuf.at[zl], outs.at[1])
    vall[z, x, y, c] = vin[...]
    keepc[zl] = keep_in[...]
    own_tokens.start()
    own_cot.start()
    for copy in vcopies(0, False):
        copy.start()
    keeps(zl).start()
    gather.begin(0)
    gather.begin(1)
    tokens(zl).start()
    vadvance(1)
    gather.turn(0)
    vadvance(2)
    vadvance(3)
    gather.turn(1)
    vadvance(4)

    per = d // (seq * row)
    for q in range(d // LANE):
        pieces = []
        for e in range(LANE // per):
            i = q * (LANE // per) + e
            spot = (i // (2 * pos.Y * pos.X), i // (2 * pos.Y) % pos.X, i // 2 % pos.Y, i % 2)
            pieces.append(vall[spot][:, :per].astype(F32))
        value = jnp.concatenate(pieces, axis=-1)
        for l in range(2):
            vec[l, :, q * LANE : (q + 1) * LANE] = value[l * 8 : l * 8 + 8]
    keeps(1 - zl).wait_recv()
    for b in range(2):
        for q in range(t // LANE):
            piece = spread_rows(to_column(keepc[b, q : q + 1, :]))
            keep[b, q * (LANE // SUB) : (q + 1) * (LANE // SUB)] = piece

    def norm0(b):
        piece = 8

        def one(k, _):
            rows = pl.ds(pl.multiple_of(k * piece * SUB, piece * SUB), piece * SUB)
            spot = pl.ds(k * piece, piece)
            v = tokbuf[b, rows, :].astype(F32)
            mu = jnp.mean(v, axis=-1, keepdims=True)
            v = v - mu
            rstd = lax.rsqrt(jnp.mean(v * v, axis=-1, keepdims=True) + epsilon)
            v = v * rstd * vec[0, GAIN : GAIN + 1, :] + vec[0, SHIFT : SHIFT + 1, :]
            at_rows = pl.ds(pl.multiple_of(b * t + k * piece * SUB, piece * SUB), piece * SUB)
            low[at_rows, :] = v.astype(BF16)
            v = tokbuf[b, rows, own].astype(F32)
            u[b, spot] = v.reshape(piece, SUB, H)
            v = (v - mu) * rstd * vec[0, GAIN : GAIN + 1, own] + vec[0, SHIFT : SHIFT + 1, own]
            np_[b, spot] = v.reshape(piece, SUB, H)
            stats[0, 0, b, spot] = jnp.broadcast_to(mu, (piece * SUB, LANE)).reshape(piece, SUB, LANE)
            stats[0, 1, b, spot] = jnp.broadcast_to(rstd, (piece * SUB, LANE)).reshape(
                piece, SUB, LANE
            )
            return 0

        lax.fori_loop(0, steps // piece, one, 0)

    def load(l, m, h):
        slot = lax.rem(m, 2)
        return pltpu.make_async_copy(
            w_all.at[l, m, h],
            wbuf.at[slot, :, :, :, :, :, pl.ds(h * HALF, HALF)],
            wsem.at[slot, h],
        )

    def start_load(l, m):
        for h in range(2):
            load(l, m, h).start()

    def gates(l, m, b):
        for h in range(2):
            load(l, m, h).wait()
        w = wbuf[lax.rem(m, 2)].reshape(d, 2 * HALF)
        v = jnp.dot(low[rows_of(b), :], w, preferred_element_type=F32)
        proj[...] = v.reshape(steps, SUB, 2 * HALF)
        cols = lane_tile(m, 2 * LANE)
        wide = pl.ds(pl.multiple_of(zl * H + m * 2 * LANE, 2 * LANE), 2 * LANE)
        peep, bias, rbias = (
            jnp.broadcast_to(vec[l, k : k + 1, wide], (SUB, 2 * LANE)) for k in (FPEEP, FBIAS, RBIAS)
        )

        def both(i, off):
            return jnp.concatenate(
                [proj[i, :, h * HALF + off : h * HALF + off + LANE] for h in range(2)], axis=-1
            )

        def one(i, carry):
            scale, state = carry
            cd = both(i, 0)
            up, down = both_sigmoids(both(i, LANE) + peep * np_[b, i, :, cols] + bias)
            f[b, i, :, cols] = up
            g[b, i, :, cols] = down
            cand[b, i, :, cols] = cd
            rpre[b, i, :, cols] = both(i, 2 * LANE) + rbias
            a = up * lanes(keep[b, i], 2 * LANE)
            return scale * a, a * state + down * cd

        start = jnp.ones((SUB, 2 * LANE), F32), jnp.zeros((SUB, 2 * LANE), F32)
        scale, state = lax.fori_loop(0, steps, one, start, unroll=8)
        ends[b, 0, :, cols] = scale
        ends[b, 1, :, cols] = state

    def pass_gates(l, b):
        start_load(l, 0)

        def one(m, _):
            @pl.when(m + 1 < parts)
            def _():
                start_load(l, m + 1)

            gates(l, m, b)
            return 0

        lax.fori_loop(0, parts, one, 0)

    def stash(k, src, dst):
        return pltpu.make_async_copy(src, dst, outs.at[k])

    own_tokens.wait()
    norm0(zl)

    def turn(i, _):
        gather.turn(i)

        @pl.when((i >= 3) & (i - 3 < parts))
        def _():
            start_load(0, i - 3)

        @pl.when(i >= 4)
        def _():
            gates(0, i - 4, zl)

        return 0

    lax.fori_loop(2, parts + 4, turn, 0)
    tokens(1 - zl).wait_recv()
    cotangents(zl).start()
    gather.turn(parts + 4)
    norm0(1 - zl)
    keep_u0, keep_low0 = stash(2, u, u0), stash(3, low, low0)
    keep_u0.start()
    keep_low0.start()
    pass_gates(0, 1 - zl)
    gates0 = [stash(4, f, f0), stash(5, g, g0), stash(6, cand, cand0)]
    for copy in gates0:
        copy.start()
    gather.turn(parts + 5)
    chains[0].run(ends, first, False)
    keep_u0.wait()
    keep_low0.wait()

    def states0(b):
        def tile(m, _):
            cols = lane_tile(m, 2 * LANE)
            wide = pl.ds(pl.multiple_of(zl * H + m * 2 * LANE, 2 * LANE), 2 * LANE)
            peep = jnp.broadcast_to(vec[0, RPEEP : RPEEP + 1, wide], (SUB, 2 * LANE))

            def one(i, cell):
                before = lanes(keep[b, i], 2 * LANE) * cell
                cell = f[b, i, :, cols] * before + g[b, i, :, cols] * cand[b, i, :, cols]
                gate = jax.nn.sigmoid(rpre[b, i, :, cols] + peep * before)
                np_[b, i, :, cols] = before
                rpre[b, i, :, cols] = gate
                u[b, i, :, cols] = gate * cell + (1.0 - gate) * u[b, i, :, cols]
                return cell

            lax.fori_loop(0, steps, one, first[b, :, cols], unroll=8)
            return 0

        lax.fori_loop(0, parts, tile, 0)

    def local_stats(b):
        def one(q, _):
            v = u[b, pl.ds(q * (LANE // SUB), LANE // SUB)].reshape(LANE, H)
            mu = jnp.mean(v, axis=-1, keepdims=True)
            v = v - mu
            square = jnp.sum(v * v, axis=-1, keepdims=True)
            st_own[b, pl.ds(q, 1), :] = to_row(mu)
            st_own[b, pl.ds(q + t // LANE, 1), :] = to_row(square)
            return 0

        lax.fori_loop(0, t // LANE, one, 0)
        statistics(b, st_got).start()

    def norm1(b):
        half = t // LANE
        statistics(b, st_got).wait_recv()
        m0, m1 = st_own[b, :half], st_got[b, :half]
        gap = m0 - m1
        square = st_own[b, half:] + st_got[b, half:] + gap * gap * (H / 2)
        st_fin[b, :half] = (m0 + m1) * 0.5
        st_fin[b, half:] = lax.rsqrt(square / (2 * H) + epsilon)

        def one(q, _):
            spot = pl.ds(q * (LANE // SUB), LANE // SUB)
            mu = to_column(st_fin[b, pl.ds(q, 1), :])
            rstd = to_column(st_fin[b, pl.ds(q + half, 1), :])
            v = u[b, spot].reshape(LANE, H)
            v = (v - mu) * rstd * vec[1, GAIN : GAIN + 1, own] + vec[1, SHIFT : SHIFT + 1, own]
            np_[b, spot] = v.reshape(LANE // SUB, SUB, H)
            low[pl.ds(pl.multiple_of(b * t + q * LANE, LANE), LANE), own] = v.astype(BF16)
            stats[1, 0, b, spot] = spread_rows(mu)
            stats[1, 1, b, spot] = spread_rows(rstd)
            return 0

        lax.fori_loop(0, half, one, 0)
        lows(b, own).start()

    states0(0)
    local_stats(0)
    gather.turn(parts + 6)
    states0(1)
    local_stats(1)
    later = [stash(7, np_, p0), stash(8, rpre, r0)]
    for copy in later:
        copy.start()
    for copy in later + gates0:
        copy.wait()
    norm1(0)
    norm1(1)
    for b in range(2):
        lows(b, other).wait_recv()
        pass_gates(1, b)
    keep_low1 = stash(2, low, low1)
    keep_low1.start()
    chains[1].run(ends, first, False)
    own_cot.wait()
    cotangents(1 - zl).wait_recv()

    def step_back(b, i, cols, top, peep):
        before, gate, up = np_[b, i, :, cols], rpre[b, i, :, cols], f[b, i, :, cols]
        cell = up * before + g[b, i, :, cols] * cand[b, i, :, cols]
        dz_r = top * (cell - u[b, i, :, cols]) * gate * (1.0 - gate)
        direct = top * gate
        kept = lanes(keep[b, i], 2 * LANE)
        decay = up * kept
        return before, gate, up, dz_r, direct, decay, kept * peep * dz_r + decay * direct

    def turn_round(b):
        def tile(m, _):
            cols = lane_tile(m, 2 * LANE)
            wide = pl.ds(pl.multiple_of(zl * H + m * 2 * LANE, 2 * LANE), 2 * LANE)
            peep = jnp.broadcast_to(vec[1, RPEEP : RPEEP + 1, wide], (SUB, 2 * LANE))
            top = cotbuf[b, :, cols].astype(F32).reshape(steps, SUB, 2 * LANE)
            proj[:, :, 2 * LANE : 4 * LANE] = top

            def one(i, cell):
                before = lanes(keep[b, i], 2 * LANE) * cell
                cell = f[b, i, :, cols] * before + g[b, i, :, cols] * cand[b, i, :, cols]
                gate = jax.nn.sigmoid(rpre[b, i, :, cols] + peep * before)
                np_[b, i, :, cols] = before
                rpre[b, i, :, cols] = gate
                proj[i, :, : 2 * LANE] = gate * cell + (1.0 - gate) * u[b, i, :, cols]
                return cell

            lax.fori_loop(0, steps, one, first[b, :, cols], unroll=8)
            v = proj[:, :, : 2 * LANE].reshape(t, 2 * LANE)
            resbuf[b, :, cols] = v.astype(BF16)

            def back(k, carry):
                scale, q = carry
                i = steps - 1 - k
                _, _, _, _, _, decay, term = step_back(
                    b, i, cols, proj[i, :, 2 * LANE : 4 * LANE], peep
                )
                return scale * decay, decay * q + term

            start = jnp.ones((SUB, 2 * LANE), F32), jnp.zeros((SUB, 2 * LANE), F32)
            scale, q = lax.fori_loop(0, steps, back, start, unroll=8)
            ends[b, 0, :, cols] = scale
            ends[b, 1, :, cols] = q
            return 0

        lax.fori_loop(0, parts, tile, 0)

    turn_round(0)
    turn_round(1)
    results(own).start()
    own_result = stash(9, resbuf.at[zl], result.at[:, own])
    own_result.start()
    chains[2].run(ends, first, True)

    def down(b):
        def tile(m, _):
            cols = lane_tile(m, 2 * LANE)
            wide = pl.ds(pl.multiple_of(zl * H + m * 2 * LANE, 2 * LANE), 2 * LANE)
            fpeep, rpeep, gain, shift = (
                jnp.broadcast_to(vec[1, k : k + 1, wide], (SUB, 2 * LANE))
                for k in (FPEEP, RPEEP, GAIN, SHIFT)
            )

            def one(k, carry):
                q, s0, s1, s2, s3 = carry
                i = steps - 1 - k
                top = top_of[i]
                before, gate, up, dz_r, direct, decay, term = step_back(b, i, cols, top, rpeep)
                e = direct + q
                low_f = g[b, i, :, cols]
                dz_f = e * (up * low_f) * (before - cand[b, i, :, cols])
                n = (u[b, i, :, cols] - lanes(stats[1, 0, b, i], 2 * LANE)) * lanes(
                    stats[1, 1, b, i], 2 * LANE
                ) * gain + shift
                proj[i, :, : 2 * LANE] = e * low_f
                proj[i, :, 2 * LANE : 4 * LANE] = dz_f
                proj[i, :, 4 * LANE :] = dz_r
                cand[b, i, :, cols] = dz_f * fpeep
                rpre[b, i, :, cols] = top * (1.0 - gate)
                return (
                    decay * q + term,
                    s0 + dz_f * n,
                    s1 + dz_r * before,
                    s2 + dz_f,
                    s3 + dz_r,
                )

            top_of[...] = cotbuf[b, :, cols].astype(F32).reshape(steps, SUB, 2 * LANE)
            zero = jnp.zeros((SUB, 2 * LANE), F32)
            carry = lax.fori_loop(0, steps, one, (first[b, :, cols], zero, zero, zero, zero), unroll=4)
            for k in range(4):
                sums[b, k, :, cols] = carry[k + 1]
            for h in range(2):
                for k in range(3):
                    v = proj[:, :, k * 2 * LANE + h * LANE : k * 2 * LANE + (h + 1) * LANE]
                    to = pl.ds(pl.multiple_of((2 * m + h) * HALF + k * LANE, LANE), LANE)
                    du[rows_of(b), to] = v.reshape(t, LANE).astype(BF16)
            return 0

        lax.fori_loop(0, parts, tile, 0)

    down(0)
    down(1)
    last = [
        stash(3, du, du1), stash(4, cand, dn1), stash(5, rpre, dhr1), stash(6, u, u1),
    ]
    for copy in last:
        copy.start()
    for copy in last + [keep_low1, own_result]:
        copy.wait()
    results(other).wait_recv()
    gather.finish()
    for stage in range(4):
        for copy in vcopies(stage, False):
            copy.wait_send()
    tokens(zl).wait_send()
    cotangents(zl).wait_send()
    keeps(zl).wait_send()
    for b in range(2):
        statistics(b, st_got).wait_send()
        lows(b, own).wait_send()
    results(own).wait_send()


def call_forward(seq, row, tok, cot, keep, vin, w_own):
    t, d = tok.shape
    layers, _, parts, _, per, _ = w_own.shape
    Y = row // 2
    X = Y
    Z = seq // X
    H = d // 2
    steps = t // SUB
    act, stat = arr(2, steps, SUB, H), arr(2, steps, SUB, LANE)
    half = arr(2 * t, d, dtype=BF16)
    vmem = pl.BlockSpec(memory_space=pltpu.VMEM)
    hbm = pl.BlockSpec(memory_space=pl.ANY)
    count = Z + 2 * X - 2
    dma = pltpu.SemaphoreType.DMA
    big = pltpu.VMEM((2, steps, SUB, H), F32)
    st = pltpu.VMEM((2, 8, LANE), F32)
    return pl.pallas_call(
        lambda *refs: forward_all(seq, row, *refs),
        in_specs=[hbm, hbm, vmem, vmem, hbm],
        out_specs=[hbm, vmem, vmem, vmem] + [hbm] * 13 + [vmem],
        out_shape=[
            arr(layers, parts, 2, Z, X, Y, 2, per, HALF, dtype=BF16),
            arr(2, 8, d),
            stat,
            arr(2, 2, 2, steps, SUB, LANE),
        ]
        + [act] * 6
        + [half, half, act, act, act, arr(2 * t, 3 * H, dtype=BF16), arr(t, d, dtype=BF16)]
        + [arr(2, 4, SUB, H)],
        scratch_shapes=[
            pltpu.VMEM((2, t, d), BF16),
            pltpu.VMEM((2, t, H), BF16),
            pltpu.VMEM((2, 8, LANE), F32),
            pltpu.VMEM((Z, X, Y, 2, 16, LANE), BF16),
            big, big, big, big, big, big,
            pltpu.VMEM((2 * t, d), BF16),
            pltpu.VMEM((2, Z, X, Y, 2, per, 2 * HALF), BF16),
            pltpu.VMEM((steps, SUB, 2 * HALF), F32),
            pltpu.VMEM((2 * t, 3 * H), BF16),
            pltpu.VMEM((2, t, H), BF16),
            pltpu.VMEM((steps, SUB, 2 * LANE), F32),
            pltpu.VMEM((2, 2, SUB, H), F32),
            pltpu.VMEM((2, SUB, H), F32),
            pltpu.VMEM((3, Z // 2, X, 2, 2, H), F32),
            st, st, st,
            dma((2, 2 * parts, count)),
            dma((2, 2 * parts, count)),
            dma((2, 2 * parts)),
            dma((count,)),
            dma((count,)),
            dma((2, 2)),
            dma((8,)),
            dma((8,)),
            dma((3, Z // 2 * X)),
            dma((3, Z // 2 * X)),
            dma((10,)),
        ],
        compiler_params=pltpu.CompilerParams(
            collective_id=0, has_side_effects=True, vmem_limit_bytes=62 << 20
        ),
        name="forward_all",
    )(tok, cot, keep, vin, w_own)


def wrap(a, b):
    return a % b if isinstance(a, int) else lax.rem(a, b)


class Scatter:
    slots = (2, 4, 4, 4)

    def __init__(self, pos, count, low, du, out, keep, send, recv, done, snd, rcv, outs):
        self.pos, self.count, self.low, self.du, self.out = pos, count, low, du, out
        self.keep, self.send, self.recv, self.done = keep, send, recv, done
        self.snd, self.rcv, self.outs = snd, rcv, outs
        n = pos.X - 1
        self.base = (0, 1, 1 + n, 1 + 2 * n)

    def axis(self, stage, h):
        return ("c", ("x", "y")[h], ("y", "x")[h], "z")[stage]

    def copy(self, g, stage, h, k):
        slot = wrap(g, self.slots[stage])
        sem = self.base[stage] + k - 1
        to = self.pos.device(self.pos.moved(self.axis(stage, h), k))
        return remote(
            self.send[stage].at[slot, k - 1], self.recv[stage].at[slot, k - 1],
            self.snd.at[slot, sem], self.rcv.at[slot, sem], to,
        )

    def each(self, stage, h):
        return self.pos.others(self.axis(stage, h))

    def ready(self, g, stage, h):
        def wait():
            for k in self.each(stage, h):
                self.copy(g, stage, h, k).wait_send()

        if isinstance(g, int):
            if g >= self.slots[stage]:
                wait()
        else:
            pl.when(g >= self.slots[stage])(wait)

    def start(self, g, stage, h):
        for k in self.each(stage, h):
            self.copy(g, stage, h, k).start()

    def arrive(self, g, stage, h):
        for k in self.each(stage, h):
            self.copy(g, stage, h, k).wait_recv()

    def stage0(self, g, h):
        pos, low, t = self.pos, self.low, self.low.shape[0]
        rows = low.shape[1] // pos.Z
        slot = wrap(g, 2)
        q = wrap(g, self.count)
        cols = pl.ds(q * HALF if isinstance(q, int) else pl.multiple_of(q * HALF, LANE), HALF)
        self.ready(g, 0, h)
        first = pos.at["c"] == 0

        def one(z, _):
            lhs = low[:, pl.ds(pl.multiple_of(z * rows, LANE), rows)]
            v = lax.dot_general(
                lhs, self.du[:, cols], (((0,), (0,)), ((), ())), preferred_element_type=F32
            )
            v = v.reshape(pos.X, pos.Y, 2, -1, HALF)
            even, odd = v[:, :, 0], v[:, :, 1]
            self.keep[0][z] = jnp.where(first, even, odd)
            self.send[0][slot, 0, z] = jnp.where(first, odd, even).astype(BF16)
            return 0

        lax.fori_loop(0, pos.Z, one, 0)
        self.start(g, 0, h)

    def stage1(self, g, h):
        pos, axis = self.pos, self.axis(1, h)
        slot = wrap(g, 4)
        got = wrap(g, 2)
        self.arrive(g, 0, h)
        self.ready(g, 1, h)
        for k in range(pos.sizes[axis]):
            p = pos.moved(axis, k)[axis]

            def one(z, _):
                where = (z, p) if h == 0 else (z, slice(None), p)
                v = self.keep[0][where] + self.recv[0][(got, 0) + where].astype(F32)
                if k == 0:
                    self.keep[1][got, z] = v
                else:
                    self.send[1][slot, k - 1, z] = v.astype(BF16)
                return 0

            lax.fori_loop(0, pos.Z, one, 0)
        self.start(g, 1, h)

    def stage2(self, g, h):
        pos, axis = self.pos, self.axis(2, h)
        slot, mine = wrap(g, 4), wrap(g, 2)
        self.arrive(g, 1, h)
        self.ready(g, 2, h)
        for k in range(pos.sizes[axis]):
            p = pos.moved(axis, k)[axis]
            v = self.keep[1][mine, :, p]
            for e in self.each(1, h):
                v = v + self.recv[1][slot, e - 1, :, p].astype(F32)
            if k == 0:
                self.keep[2][mine] = v
            else:
                self.send[2][slot, k - 1] = v.astype(BF16)
        self.start(g, 2, h)

    def stage3(self, g, h):
        pos = self.pos
        slot, mine = wrap(g, 4), wrap(g, 2)
        self.arrive(g, 2, h)
        self.ready(g, 3, h)
        for k in range(pos.Z):
            p = pos.moved("z", k)["z"]
            v = self.keep[2][mine, p]
            for e in self.each(2, h):
                v = v + self.recv[2][slot, e - 1, p].astype(F32)
            if k == 0:
                self.keep[3][mine] = v
            else:
                self.send[3][slot, k - 1] = v.astype(BF16)
        self.start(g, 3, h)

    def result(self, l, q, half, e):
        d = self.out.shape[-1] // 3
        at = e * d + half * (d // 2) + q * LANE
        return pltpu.make_async_copy(
            self.done.at[half, q, :, e * LANE : (e + 1) * LANE],
            self.out.at[l, :, pl.ds(pl.multiple_of(at, LANE), LANE)],
            self.outs.at[half, q, e],
        )

    def stage4(self, g, h, l):
        pos = self.pos
        slot, mine, q = wrap(g, 4), wrap(g, 2), wrap(g, self.count)
        self.arrive(g, 3, h)
        own, other = self.keep[3][mine], None
        for k in range(1, pos.Z):
            v = self.recv[3][slot, k - 1].astype(F32)
            if k % 2 == 0:
                own = own + v
            else:
                other = v if other is None else other + v
        self.done[pos.zl, q] = own
        self.done[1 - pos.zl, q] = other
        for half in (pos.zl, 1 - pos.zl):
            for e in range(3):
                self.result(l, q, half, e).start()

    def turn(self, run, l, pair, e, enters=True):
        first = run * self.count

        def stage(s, f):
            g = first + 2 * pair + e - s
            h = (e - s) % 2
            if isinstance(g, int):
                if first <= g < first + self.count:
                    f(g, h)
            elif s:
                pl.when(g >= first)(lambda: f(g, h))
            else:
                f(g, h)

        stage(1, self.stage1)
        if enters:
            stage(0, self.stage0)
        stage(2, self.stage2)
        stage(3, self.stage3)
        stage(4, lambda g, h: self.stage4(g, h, l))

    def written(self, l):
        def one(q, _):
            for half in (self.pos.zl, 1 - self.pos.zl):
                for e in range(3):
                    self.result(l, q, half, e).wait()
            return 0

        lax.fori_loop(0, self.count, one, 0)

    def finish(self, total):
        for stage in range(4):
            for g in range(total - self.slots[stage], total):
                for k in self.each(stage, g % 2):
                    self.copy(g, stage, g % 2, k).wait_send()


def backward_all(
    seq, row, w_all, vec, keep, stats, f0, g0, cand0, p0, r0, u0, low0, low1, u1, dhr1, dn1, du1,
    sums1,
    grad, input_grad, vout,
    wbuf, du, low, dn, dnsend, dnrecv, u, dhr, stream, proj, top_of,
    keep0, send0, recv0, keep1, send1, recv1, keep2, send2, recv2, keep3, send3, recv3, done,
    ends, first, table, b_own, b_got, b_fin, sums, vbuf, vr0, vr1, vr2, vr3,
    snd, rcv, gouts, psnd, prcv, csnd, crcv, vsnd, vrcv, ins, ssem, wsem,
):
    pos = Place(seq, row)
    at, zl = pos.at, pos.zl
    z, x, y, c = (at[k] for k in "zxyc")
    t2, H3 = du.shape
    t, H = t2 // 2, H3 // 3
    d = 2 * H
    steps = t // SUB
    parts = H // WIDE
    partner = pos.device(dict(at, z=z + 1 - 2 * zl))
    own = pl.ds(pl.multiple_of(zl * H, H), H)
    other = pl.ds(pl.multiple_of((1 - zl) * H, H), H)
    rows_of = lambda b: pl.ds(pl.multiple_of(b * t, t), t)
    pos.barrier(seq)

    def load(k, src, dst):
        return pltpu.make_async_copy(src, dst, ins.at[k])

    def weights(l, half):
        zs = pl.ds(half * (pos.Z // 2), pos.Z // 2)
        for m in range(parts):
            for h in range(2):
                q = 2 * m + h
                yield pltpu.make_async_copy(
                    w_all.at[l, m, h, zs],
                    wbuf.at[:, :, :, :, :, q * HALF : (q + 1) * HALF],
                    wsem.at[q],
                )

    def begin(copies):
        for copy in copies:
            copy.start()

    def end(copies):
        for copy in copies:
            copy.wait()

    get_du, get_low, get_dn = load(0, du1, du), load(1, low1, low), load(2, dn1, dn)
    get_u, get_dhr = load(3, u1, u), load(4, dhr1, dhr)
    begin(weights(1, 1 - zl))
    begin([get_du, get_low, get_dn, get_u, get_dhr])
    scatter = Scatter(
        pos, 2 * parts, low, du, grad, (keep0, keep1, keep2, keep3), (send0, send1, send2, send3),
        (recv0, recv1, recv2, recv3), done, snd, rcv, gouts,
    )
    chain = Chain(pos, table, csnd, crcv)

    def pair(k, src, dst):
        return remote(src, dst, psnd.at[k], prcv.at[k], partner)

    def partial_sums(b):
        return pair(b, dnsend.at[b], dnrecv.at[b])

    def statistics(b):
        return pair(2 + b, b_own.at[b], b_got.at[b])

    def outputs(b, cols):
        return pair(4, dnsend.at[b], input_grad.at[:, cols])

    across = (((1,), (1,)), ((), ()))

    def theirs(b, _):
        v = lax.dot_general(
            du[rows_of(b), :], wbuf[...].reshape(H, H3), across, preferred_element_type=F32
        )
        dnsend[b] = v.astype(BF16)
        partial_sums(b).start()
        return 0

    def ours(k):
        n = t2 // parts
        rows = pl.ds(pl.multiple_of(k * n, n), n)
        v = lax.dot_general(
            du[rows, :], wbuf[...].reshape(H, H3), across, preferred_element_type=F32
        )
        blocks = t // n
        spot = pl.ds(pl.multiple_of(lax.rem(k, blocks) * (n // SUB), n // SUB), n // SUB)
        dn[k // blocks, spot] += v.reshape(n // SUB, SUB, H)

    half = t // LANE

    def norm_sums(l, b):
        partial_sums(b).wait_recv()

        def one(q, _):
            spot = pl.ds(q * (LANE // SUB), LANE // SUB)
            rows = pl.ds(pl.multiple_of(q * LANE, LANE), LANE)
            v = dn[b, spot].reshape(LANE, H) + dnrecv[b, rows, :].astype(F32)
            dn[b, spot] = v.reshape(LANE // SUB, SUB, H)
            xhat = hat(l, b, spot)
            sums[l, 0] += jnp.sum((v * xhat).reshape(LANE // SUB, SUB, H), axis=0)
            sums[l, 1] += jnp.sum(v.reshape(LANE // SUB, SUB, H), axis=0)
            v = v * vec[l, GAIN : GAIN + 1, own]
            b_own[b, pl.ds(q, 1), :] = to_row(jnp.sum(v, axis=-1, keepdims=True))
            b_own[b, pl.ds(q + half, 1), :] = to_row(jnp.sum(v * xhat, axis=-1, keepdims=True))
            return 0

        lax.fori_loop(0, half, one, 0)
        statistics(b).start()

    def hat(l, b, spot):
        mu = stats[l, 0, b, spot].reshape(LANE, LANE)[:, :1]
        rstd = stats[l, 1, b, spot].reshape(LANE, LANE)[:, :1]
        return (u[b, spot].reshape(LANE, H) - mu) * rstd

    def norm_back(l, b):
        statistics(b).wait_recv()
        b_fin[...] = (b_own[b] + b_got[b]) * (1.0 / d)

        def one(q, _):
            spot = pl.ds(q * (LANE // SUB), LANE // SUB)
            xhat = hat(l, b, spot)
            rstd = stats[l, 1, b, spot].reshape(LANE, LANE)[:, :1]
            m0 = to_column(b_fin[pl.ds(q, 1), :])
            m1 = to_column(b_fin[pl.ds(q + half, 1), :])
            v = dn[b, spot].reshape(LANE, H) * vec[l, GAIN : GAIN + 1, own]
            v = dhr[b, spot].reshape(LANE, H) + rstd * (v - m0 - xhat * m1)
            if l == 1:
                dhr[b, spot] = v.reshape(LANE // SUB, SUB, H)
            else:
                dnsend[b, pl.ds(pl.multiple_of(q * LANE, LANE), LANE), :] = v.astype(BF16)
            return 0

        lax.fori_loop(0, half, one, 0)

    units = 2 * parts
    sources = (f0, g0, cand0, p0, r0)

    def fetch(k):
        slot = lax.rem(k, 2)
        b, m = k // parts, lax.rem(k, parts)
        for j, src in enumerate(sources):
            yield pltpu.make_async_copy(
                src.at[b, :, :, lane_tile(m, WIDE)], stream.at[slot, j], ssem.at[slot, j]
            )

    def tiles(work):
        begin(fetch(0))

        def one(k, _):
            @pl.when(k + 1 < units)
            def _():
                begin(fetch(k + 1))

            end(fetch(k))
            b, m = k // parts, lax.rem(k, parts)
            cols = lane_tile(m, WIDE)
            wide = pl.ds(pl.multiple_of(zl * H + m * WIDE, WIDE), WIDE)
            work(lax.rem(k, 2), b, m, cols, wide)
            return 0

        lax.fori_loop(0, units, one, 0)

    def step_back(slot, b, i, cols, peep):
        up, down, cd, before, gate = (stream[slot, j, i] for j in range(5))
        cell = up * before + down * cd
        top = dhr[b, i, :, cols]
        dz_r = top * (cell - u[b, i, :, cols]) * gate * (1.0 - gate)
        direct = top * gate
        kept = lanes(keep[b, i], WIDE)
        decay = up * kept
        term = kept * peep * dz_r + decay * direct
        return up, down, cd, before, gate, top, dz_r, direct, decay, term

    def row_wide(l, k, wide):
        return jnp.broadcast_to(vec[l, k : k + 1, wide], (SUB, WIDE))

    def ends_work(slot, b, m, cols, wide):
        peep = row_wide(0, RPEEP, wide)

        def one(k, carry):
            scale, q = carry
            decay, term = step_back(slot, b, steps - 1 - k, cols, peep)[-2:]
            return scale * decay, decay * q + term

        start = jnp.ones((SUB, WIDE), F32), jnp.zeros((SUB, WIDE), F32)
        scale, q = lax.fori_loop(0, steps, one, start, unroll=8)
        ends[b, 0, :, cols] = scale
        ends[b, 1, :, cols] = q

    def down_work(slot, b, m, cols, wide):
        fpeep, rpeep, gain, shift = (row_wide(0, k, wide) for k in (FPEEP, RPEEP, GAIN, SHIFT))

        def one(k, carry):
            q, s0, s1, s2, s3 = carry
            i = steps - 1 - k
            up, low_f, cd, before, gate, top, dz_r, direct, decay, term = step_back(
                slot, b, i, cols, rpeep
            )
            e = direct + q
            dz_f = e * (up * low_f) * (before - cd)
            n = (u[b, i, :, cols] - lanes(stats[0, 0, b, i], WIDE)) * lanes(
                stats[0, 1, b, i], WIDE
            ) * gain + shift
            proj[i, :, :WIDE] = e * low_f
            proj[i, :, WIDE : 2 * WIDE] = dz_f
            proj[i, :, 2 * WIDE :] = dz_r
            dn[b, i, :, cols] = dz_f * fpeep
            dhr[b, i, :, cols] = top * (1.0 - gate)
            return (
                decay * q + term,
                s0 + dz_f * n,
                s1 + dz_r * before,
                s2 + dz_f,
                s3 + dz_r,
            )

        zero = jnp.zeros((SUB, WIDE), F32)
        carry = lax.fori_loop(0, steps, one, (first[b, :, cols], zero, zero, zero, zero), unroll=4)
        for k in range(4):
            sums[0, 2 + k, :, cols] += carry[k + 1]
        for h in range(2):
            for k in range(3):
                v = proj[:, :, k * WIDE + h * LANE : k * WIDE + (h + 1) * LANE]
                to = pl.ds(pl.multiple_of((2 * m + h) * HALF + k * LANE, LANE), LANE)
                du[rows_of(b), to] = v.reshape(t, LANE).astype(BF16)

    def layer(run, l):
        end(weights(l, 1 - zl))
        lax.fori_loop(0, 2, theirs, 0)
        begin(weights(l, zl))

        def one(k, _):
            scatter.turn(run, l, k, 0)

            @pl.when(k == 0)
            def _():
                end(weights(l, zl))

            ours(k)
            scatter.turn(run, l, k, 1)
            return 0

        lax.fori_loop(0, parts, one, 0)

    sums[...] = jnp.zeros_like(sums)
    sums[1, 2:6] = sums1[0] + sums1[1]
    get_du.wait()
    get_low.wait()
    get_dn.wait()
    layer(0, 1)
    get_low = load(1, low0, low)
    get_low.start()
    get_u.wait()
    get_dhr.wait()
    begin(weights(0, 1 - zl))
    norm_sums(1, 0)
    norm_sums(1, 1)
    scatter.turn(0, 1, parts, 0, False)
    norm_back(1, 0)
    norm_back(1, 1)
    get_u = load(3, u0, u)
    get_u.start()
    scatter.turn(0, 1, parts, 1, False)
    get_u.wait()
    tiles(ends_work)
    scatter.turn(0, 1, parts + 1, 0, False)
    chain.run(ends, first, True)
    scatter.turn(0, 1, parts + 1, 1, False)
    tiles(down_work)
    for b in range(2):
        partial_sums(b).wait_send()
        statistics(b).wait_send()
    scatter.written(1)
    get_low.wait()
    layer(1, 0)
    norm_sums(0, 0)
    norm_sums(0, 1)
    scatter.turn(1, 0, parts, 0, False)
    for b in range(2):
        partial_sums(b).wait_send()
    norm_back(0, 0)
    norm_back(0, 1)
    outputs(1 - zl, own).start()
    own_out = load(0, dnsend.at[zl], input_grad.at[:, own])
    own_out.start()
    scatter.turn(1, 0, parts, 1, False)

    vbuf[...] = jnp.zeros_like(vbuf)
    per = d // (seq * row)
    total = [jnp.sum(sums[l], axis=1) for l in range(2)]
    blank = jnp.zeros((6, LANE - per), F32) if per < LANE else None
    for i in range(H // per):
        spot = (zl * (pos.Z // 2) + i // (2 * pos.Y * pos.X), i // (2 * pos.Y) % pos.X, i // 2 % pos.Y, i % 2)
        for l in range(2):
            piece = total[l][:, i * per : (i + 1) * per]
            vbuf[spot + (slice(l * 8, l * 8 + 6),)] = jnp.concatenate([piece, blank], axis=-1)
    every = slice(None)

    def vspot(stage, who):
        if stage == 0:
            return (every, every, every, who["c"])
        if stage == 1:
            return (every, who["x"], every, c)
        if stage == 2:
            return (every, x, who["y"], c)
        return (who["z"], x, y, c)

    vrecv = (vr0, vr1, vr2, vr3)

    def vcopy(stage, k):
        axis = "cxyz"[stage]
        to = pos.moved(axis, k)
        sem = scatter.base[stage] + k - 1
        return remote(
            vbuf.at[vspot(stage, to)], vrecv[stage].at[k - 1], vsnd.at[sem], vrcv.at[sem],
            pos.device(to),
        )

    def vstart(stage):
        for k in pos.others("cxyz"[stage]):
            vcopy(stage, k).start()

    def vtake(stage):
        for k in pos.others("cxyz"[stage]):
            vcopy(stage, k).wait_recv()
            vbuf[vspot(stage, at)] += vrecv[stage][k - 1]

    vstart(0)
    scatter.turn(1, 0, parts + 1, 0, False)
    vtake(0)
    vstart(1)
    scatter.turn(1, 0, parts + 1, 1, False)
    vtake(1)
    vstart(2)
    vtake(2)
    vstart(3)
    vtake(3)
    vout[...] = vbuf[z, x, y, c]
    for stage in range(4):
        for k in pos.others("cxyz"[stage]):
            vcopy(stage, k).wait_send()
    scatter.written(0)
    scatter.finish(2 * scatter.count)
    for b in range(2):
        statistics(b).wait_send()
    own_out.wait()
    outputs(1 - zl, own).wait_send()
    outputs(1 - zl, other).wait_recv()


def call_backward(seq, row, t, d, given):
    w_all = given[0]
    layers, parts, _, Z, X, Y, _, per, _ = w_all.shape
    H = d // 2
    steps = t // SUB
    vmem = pl.BlockSpec(memory_space=pltpu.VMEM)
    hbm = pl.BlockSpec(memory_space=pl.ANY)
    dma = pltpu.SemaphoreType.DMA
    big = pltpu.VMEM((2, steps, SUB, H), F32)
    half = pltpu.VMEM((2, t, H), BF16)
    st = pltpu.VMEM((2, 8, LANE), F32)
    count = 1 + 2 * (X - 1) + Z - 1
    chunk = (Z, X, Y, per, HALF)

    def buf(*shape, dtype=BF16):
        return pltpu.VMEM(shape, dtype)

    return pl.pallas_call(
        lambda *refs: backward_all(seq, row, *refs),
        in_specs=[hbm, vmem, vmem, vmem] + [hbm] * 12 + [vmem],
        out_specs=[hbm, hbm, vmem],
        out_shape=[arr(layers, per, 3 * d), arr(t, d, dtype=BF16), arr(16, LANE)],
        scratch_shapes=[
            buf(Z // 2, X, Y, 2, per, 3 * H),
            buf(2 * t, 3 * H),
            buf(2 * t, d),
            big, half, half, big, big,
            buf(2, 5, steps, SUB, WIDE, dtype=F32),
            buf(steps, SUB, 3 * WIDE, dtype=F32),
            buf(8, LANE, dtype=F32),
            buf(*chunk, dtype=F32), buf(2, 1, *chunk), buf(2, 1, *chunk),
            buf(2, Z, Y, per, HALF, dtype=F32), buf(4, X - 1, Z, Y, per, HALF),
            buf(4, X - 1, Z, Y, per, HALF),
            buf(2, Z, per, HALF, dtype=F32), buf(4, Y - 1, Z, per, HALF),
            buf(4, Y - 1, Z, per, HALF),
            buf(2, per, HALF, dtype=F32), buf(4, Z - 1, per, HALF), buf(4, Z - 1, per, HALF),
            buf(2, 2 * parts, per, HALF, dtype=F32),
            buf(2, 2, SUB, H, dtype=F32),
            buf(2, SUB, H, dtype=F32),
            buf(Z // 2, X, 2, 2, H, dtype=F32),
            st, st, buf(8, LANE, dtype=F32),
            buf(2, 6, SUB, H, dtype=F32),
            buf(Z, X, Y, 2, 16, LANE, dtype=F32),
            buf(1, Z, X, Y, 16, LANE, dtype=F32),
            buf(X - 1, Z, Y, 16, LANE, dtype=F32),
            buf(Y - 1, Z, 16, LANE, dtype=F32),
            buf(Z - 1, 16, LANE, dtype=F32),
            dma((4, count)), dma((4, count)),
            dma((2, 2 * parts, 3)),
            dma((5,)), dma((5,)),
            dma((Z // 2 * X,)), dma((Z // 2 * X,)),
            dma((count,)), dma((count,)),
            dma((5,)),
            dma((2, 5)),
            dma((2 * parts,)),
        ],
        compiler_params=pltpu.CompilerParams(
            collective_id=1, has_side_effects=True, vmem_limit_bytes=62 << 20
        ),
        name="backward_all",
    )(*given)


def body(tokens, resets, cotangent, weight, *rows):
    _, t, d = tokens.shape
    layers = weight.shape[0]
    steps = t // SUB
    seq, row = lax.axis_size("seq"), lax.axis_size("row")
    H = d // 2
    parts = H // WIDE

    def permuted(v):
        return v.reshape(SUB, steps, -1).transpose(1, 0, 2).reshape(t, -1)

    def restored(v):
        return v.reshape(steps, SUB, d).transpose(1, 0, 2).reshape(1, t, d)

    keep = permuted((1 - resets[0]).astype(F32)[:, None]).reshape(t // LANE, LANE)
    keep = jnp.pad(keep, ((0, 8 - t // LANE), (0, 0)))
    per = rows[0].shape[-1]
    packed = jnp.stack(rows + (jnp.zeros_like(rows[0]),) * 2, axis=1).reshape(2 * 8, per)
    packed = jnp.pad(packed, ((0, 0), (0, LANE - per)))
    local = weight.reshape(layers, per, 3, 2, parts, 2, LANE).transpose(0, 3, 4, 5, 1, 2, 6)
    local = local.reshape(layers, 2, parts, 2, per, HALF)
    out = call_forward(
        seq, row, permuted(tokens[0]), permuted(cotangent[0]), keep, packed, local
    )
    result, sums = out[-2:]
    grad, input_grad, vectors = call_backward(seq, row, t, d, tuple(out[:-2]) + (sums,))
    return (restored(result), restored(input_grad), grad) + tuple(
        jnp.stack([vectors[l * 8 + k, :per] for l in range(layers)]) for k in range(6)
    )


def solution(mesh):
    tokens = P("row", "seq", None)
    rows = P(None, ("seq", "row"))
    weight = P(None, ("seq", "row"), None)
    return jax.shard_map(
        body,
        mesh=mesh,
        in_specs=(tokens, P("row", "seq"), tokens, weight) + (rows,) * 6,
        out_specs=(tokens, tokens, weight) + (rows,) * 6,
        check_vma=False,
    )
```

time: 3050 us -> 596 us (0.20); the launches traced: 3000 us -> 596 us
  local copies, waits for them, and re-layouts: 1170 us -> 31.9 us
  waiting for transfers between devices: 1020 us -> 0 us
  Pallas kernels: 0 us -> 559 us
  blocking collectives: 326 us -> 0 us
  other arithmetic: 323 us -> 4.11 us
  matrix products: 143 us -> 0 us
    reduce_scatter x2 -> x0, waiting for transfers between devices: 869 us -> none  [body(): lax.psum_scatter(weight_term, ('seq', 'row'), scatter_dimension=0, tiled=...]
    slice x249 -> x1, local copies, waits for them, and re-layouts: 583 us -> 0.01 us  [body(): vectors[l * 8 + k, :per]]
    pallas_call x0 -> x2, Pallas kernels: none -> 559 us  [the longest x1 290 us: call_forward(): pl.pallas_call(lambda *refs: forward_all(seq, row, *refs), in_specs=[hbm,...]
    pad x128 -> x2, local copies, waits for them, and re-layouts: 417 us -> 1.2 us  [the longest x1 0.6 us: body(): packed = jnp.pad(packed, ((0, 0), (0, LANE - per)))]
    all_gather x10 -> x0, blocking collectives: 326 us -> none  [the longest x8 244 us: entering(): pieces = jax.tree.map(lambda part: lax.all_gather(part, axis), value)]
    add x111 -> x0, other arithmetic: 165 us -> none  [the longest x40 60.9 us: body(): lax.associative_scan(affine_join, (decay_rate, local_term), reverse=True,...]
    dot_general x6 -> x0, matrix products: 143 us -> none  [the longest x2 50.3 us: body(): jnp.einsum('rte,de->rtd', projected_grad, full_weight, preferred_element_...]
    rev x8 -> x0, local copies, waits for them, and re-layouts: 131 us -> none  [the longest x4 131 us: body(): lax.associative_scan(affine_join, (decay_rate, local_term), reverse=True,...]
  transfers between devices with their start and end apart: 6 -> 0, of which waited for: 4 -> 0; matrix products, arithmetic and copies ran while one was open for 18% -> 0% of each run, Pallas kernels for 0% -> 0%
where the time goes in v3:
time: 596 us
  Pallas kernels  559 us (94%)
  local copies, waits for them, and re-layouts  31.9 us (5%)
    pallas_call x1, Pallas kernels, call_forward(): pl.pallas_call(lambda *refs: forward_all(seq, row, *refs), in_specs=[hbm,...  290 us
    pallas_call x1, Pallas kernels, call_backward(): pl.pallas_call(lambda *refs: backward_all(seq, row, *refs), in_specs=[hbm...  268 us

profile of v3, /device:TPU:0, one launch (start us, length us, event | category | flops | bytes accessed | tf_op | source)
XLA Modules:
  0.0 595.5 jit_solution(12118189774113175183)
XLA Ops:
  0.6 0.7 copy.34
  1.3 0.7 copy.35
  2.0 0.7 copy.36
  2.6 0.7 copy.37
  3.3 0.7 copy.38
  3.9 0.7 copy.39
  4.6 0.6 pad.9.refs_3_
  5.2 0.7 convert_reduce_fusion
  6.2 0.6 pad.8.refs_2_
  6.8 4.9 reshape.64
  11.7 2.6 copy.46
  14.2 2.5 reshape.65.refs_4_
  16.7 6.5 %copy_bitcast_fusion.1 = (bf16[512,2048]{1,0:T(8,128)(2,1)}, bf16[512,2048]{1,0:T(8,128)(2,1)}) fusion(bf16[8,64,2048]{2,1,0:T(8,128)(2,1)} %bitcast.36, bf16[8,64,2048]{2,1,0:T(8,128)(2,1)} %bitcast.37), kind=kLoop, calls=%fused_computation.1 | loop fusion | bytes 8388608 | tf_op jit(solution)/shard_map/reshape | solution.py:1332
  23.3 290.5 %forward_all.1 = (bf16[2,4,2,4,2,2,2,64,384]{8,7,6,5,4,3,2,1,0:T(8,128)(2,1)}, f32[2,8,2048]{2,1,0:T(8,128)}, f32[2,64,8,128]{3,2,1,0:T(8,128)}, f32[2,2,2,64,8,...) custom-call(bf16[512,2048]{1,0:T(8,128)(2,1)} %get-tuple-element.64., ...), custom_call_target="tpu_custom_call" | custom-call | tf_op jit(solution)/shard_map/forward_all/pallas_call | solution.py:676
  313.8 4.1 copy.41
  317.8 268.4 %backward_all.1 = (f32[2,64,6144]{2,1,0:T(8,128)}, bf16[512,2048]{1,0:T(8,128)(2,1)}, f32[16,128]{1,0:T(8,128)}) custom-call(bf16[2,4,2,4,2,2,2,64,384]{8,7,6,5,4,3,2,1,0:T(8,128)(2,1)} %get-tuple-element.31.refs_0_, f32[2,8,2048]{2,1,0:T(8,128)} %get-tuple-element.32.refs_1_, f32[2,64,8,128]{3,2,1,0:T(8,128)} %get-tuple-element.33.refs_2_, ...), custom_call_target="tpu_custom_call" | custom-call | tf_op jit(solution)/shard_map/backward_all/pallas_call | solution.py:1277
  586.2 4.2 copy.42
  590.5 0.6 pad_maximum_fusion.5
  591.0 0.6 pad_maximum_fusion.4
  591.6 0.6 pad_maximum_fusion.3
  592.2 0.6 pad_maximum_fusion.2
  592.7 0.6 pad_maximum_fusion.1
  593.3 0.6 pad_maximum_fusion
  593.9 1.7 copy.48
  (10 shorter events, 0.3 us)
Async XLA Ops:
  586.2 4.2 copy-start.1
  586.2 7.7 %copy-start = (f32[2,64,6144]{2,1,0:T(8,128)S(1)}, f32[2,64,6144]{2,1,0:T(8,128)}, u32[]{:S(2)}) copy-start(f32[2,64,6144]{2,1,0:T(8,128)} %get-tuple-element.76) | copy-start | bytes 9437188

commit v4 on v3

--- a/solution.py
+++ b/solution.py
@@ -154,9 +154,9 @@
     def turn(self, i):
         total = 2 * self.parts
 
-        @pl.when(i + 2 < total)
+        @pl.when(i + 4 < total)
         def _():
-            self.begin(i + 2)
+            self.begin(i + 4)
 
         for stage in range(1, 5):
             g = i - (stage - 1)
@@ -244,7 +244,7 @@
 
 def forward_all(
     seq, row, tok, cot, keep_in, vin, w_own,
-    w_all, vec, keep, stats, f0, g0, cand0, p0, r0, u0, low0, low1, u1, dhr1, dn1, du1, result,
+    w_all, vec, keep, stats, f0, g0, cand0, p0, r0, u0, low0, low1, u1, dhr1, dn1, du1, res1,
     sums, tokbuf, cotbuf, keepc, vall, u, np_, f, g, cand, rpre, low, wbuf, proj, du, resbuf, top_of, ends,
     first, tables, st_own, st_got, st_fin,
     gsnd, grcv, gloc, vsnd, vrcv, wsem, psnd, prcv, csnd, crcv, outs,
@@ -282,9 +282,6 @@
     def lows(b, cols):
         return pair(5 + b, low.at[rows_of(b), cols], low.at[rows_of(b), cols])
 
-    def results(cols):
-        return pair(7, resbuf.at[1 - zl], result.at[:, cols])
-
     def vcopies(stage, arriving):
         axis = gather.axis(stage, 0)
         size = pos.sizes[axis]
@@ -313,12 +310,14 @@
     keeps(zl).start()
     gather.begin(0)
     gather.begin(1)
-    tokens(zl).start()
+    gather.begin(2)
+    gather.begin(3)
     vadvance(1)
     gather.turn(0)
     vadvance(2)
     vadvance(3)
     gather.turn(1)
+    tokens(zl).start()
     vadvance(4)
 
     per = d // (seq * row)
@@ -350,10 +349,7 @@
             v = v * rstd * vec[0, GAIN : GAIN + 1, :] + vec[0, SHIFT : SHIFT + 1, :]
             at_rows = pl.ds(pl.multiple_of(b * t + k * piece * SUB, piece * SUB), piece * SUB)
             low[at_rows, :] = v.astype(BF16)
-            v = tokbuf[b, rows, own].astype(F32)
-            u[b, spot] = v.reshape(piece, SUB, H)
-            v = (v - mu) * rstd * vec[0, GAIN : GAIN + 1, own] + vec[0, SHIFT : SHIFT + 1, own]
-            np_[b, spot] = v.reshape(piece, SUB, H)
+            u[b, spot] = tokbuf[b, rows, own].astype(F32).reshape(piece, SUB, H)
             stats[0, 0, b, spot] = jnp.broadcast_to(mu, (piece * SUB, LANE)).reshape(piece, SUB, LANE)
             stats[0, 1, b, spot] = jnp.broadcast_to(rstd, (piece * SUB, LANE)).reshape(
                 piece, SUB, LANE
@@ -374,16 +370,19 @@
         for h in range(2):
             load(l, m, h).start()
 
-    def gates(l, m, b):
+    def end_load(l, m):
         for h in range(2):
             load(l, m, h).wait()
+
+    def gates(l, m, b):
         w = wbuf[lax.rem(m, 2)].reshape(d, 2 * HALF)
         v = jnp.dot(low[rows_of(b), :], w, preferred_element_type=F32)
         proj[...] = v.reshape(steps, SUB, 2 * HALF)
         cols = lane_tile(m, 2 * LANE)
         wide = pl.ds(pl.multiple_of(zl * H + m * 2 * LANE, 2 * LANE), 2 * LANE)
-        peep, bias, rbias = (
-            jnp.broadcast_to(vec[l, k : k + 1, wide], (SUB, 2 * LANE)) for k in (FPEEP, FBIAS, RBIAS)
+        peep, bias, rbias, gain, shift = (
+            jnp.broadcast_to(vec[l, k : k + 1, wide], (SUB, 2 * LANE))
+            for k in (FPEEP, FBIAS, RBIAS, GAIN, SHIFT)
         )
 
         def both(i, off):
@@ -394,7 +393,10 @@
         def one(i, carry):
             scale, state = carry
             cd = both(i, 0)
-            up, down = both_sigmoids(both(i, LANE) + peep * np_[b, i, :, cols] + bias)
+            n = (u[b, i, :, cols] - lanes(stats[l, 0, b, i], 2 * LANE)) * lanes(
+                stats[l, 1, b, i], 2 * LANE
+            ) * gain + shift
+            up, down = both_sigmoids(both(i, LANE) + peep * n + bias)
             f[b, i, :, cols] = up
             g[b, i, :, cols] = down
             cand[b, i, :, cols] = cd
@@ -407,19 +409,6 @@
         ends[b, 0, :, cols] = scale
         ends[b, 1, :, cols] = state
 
-    def pass_gates(l, b):
-        start_load(l, 0)
-
-        def one(m, _):
-            @pl.when(m + 1 < parts)
-            def _():
-                start_load(l, m + 1)
-
-            gates(l, m, b)
-            return 0
-
-        lax.fori_loop(0, parts, one, 0)
-
     def stash(k, src, dst):
         return pltpu.make_async_copy(src, dst, outs.at[k])
 
@@ -429,30 +418,57 @@
     def turn(i, _):
         gather.turn(i)
 
-        @pl.when((i >= 3) & (i - 3 < parts))
+        @pl.when(i >= 3)
         def _():
-            start_load(0, i - 3)
-
-        @pl.when(i >= 4)
+            @pl.when(i < parts + 1)
+            def _():
+                start_load(0, i - 3)
+
+        @pl.when((i >= 4) & (i < parts + 2))
         def _():
+            end_load(0, i - 4)
             gates(0, i - 4, zl)
 
+        @pl.when(i == parts + 1)
+        def _():
+            tokens(1 - zl).wait_recv()
+            norm0(1 - zl)
+
+        @pl.when(i > parts)
+        def _():
+            last = i == parts + 2
+
+            def job(k, _):
+                m = jnp.where(last, parts - 2 + k // 2, k)
+                b = jnp.where(last & (lax.rem(k, 2) == 0), zl, 1 - zl)
+
+                @pl.when(last & (lax.rem(k, 2) == 0))
+                def _():
+                    end_load(0, m)
+
+                gates(0, m, b)
+
+                @pl.when(jnp.logical_not(last) & (k == 0))
+                def _():
+                    start_load(0, parts - 2)
+
+                return 0
+
+            @pl.when(last)
+            def _():
+                start_load(0, parts - 1)
+
+            lax.fori_loop(0, jnp.where(last, 4, parts - 2), job, 0)
+
         return 0
 
-    lax.fori_loop(2, parts + 4, turn, 0)
-    tokens(1 - zl).wait_recv()
-    cotangents(zl).start()
-    gather.turn(parts + 4)
-    norm0(1 - zl)
+    lax.fori_loop(2, parts + 3, turn, 0)
     keep_u0, keep_low0 = stash(2, u, u0), stash(3, low, low0)
-    keep_u0.start()
-    keep_low0.start()
-    pass_gates(0, 1 - zl)
     gates0 = [stash(4, f, f0), stash(5, g, g0), stash(6, cand, cand0)]
-    for copy in gates0:
+    for copy in [keep_u0, keep_low0] + gates0:
         copy.start()
-    gather.turn(parts + 5)
     chains[0].run(ends, first, False)
+    gather.turn(parts + 3)
     keep_u0.wait()
     keep_low0.wait()
 
@@ -504,7 +520,6 @@
             rstd = to_column(st_fin[b, pl.ds(q + half, 1), :])
             v = u[b, spot].reshape(LANE, H)
             v = (v - mu) * rstd * vec[1, GAIN : GAIN + 1, own] + vec[1, SHIFT : SHIFT + 1, own]
-            np_[b, spot] = v.reshape(LANE // SUB, SUB, H)
             low[pl.ds(pl.multiple_of(b * t + q * LANE, LANE), LANE), own] = v.astype(BF16)
             stats[1, 0, b, spot] = spread_rows(mu)
             stats[1, 1, b, spot] = spread_rows(rstd)
@@ -515,24 +530,47 @@
 
     states0(0)
     local_stats(0)
+    states0(1)
+    keep_p0, keep_r0 = stash(7, np_, p0), stash(8, rpre, r0)
+    keep_p0.start()
+    keep_r0.start()
+    norm1(0)
+    local_stats(1)
+    gather.turn(parts + 4)
+    norm1(1)
+    gather.turn(parts + 5)
     gather.turn(parts + 6)
-    states0(1)
-    local_stats(1)
-    later = [stash(7, np_, p0), stash(8, rpre, r0)]
-    for copy in later:
-        copy.start()
-    for copy in later + gates0:
+    start_load(1, 0)
+    keep_u1 = stash(2, u, u1)
+    keep_u1.start()
+    for copy in gates0 + [keep_r0]:
         copy.wait()
-    norm1(0)
-    norm1(1)
-    for b in range(2):
-        lows(b, other).wait_recv()
-        pass_gates(1, b)
-    keep_low1 = stash(2, low, low1)
+
+    def job1(k, _):
+        b, m = k // parts, lax.rem(k, parts)
+
+        @pl.when(m == 0)
+        def _():
+            lows(b, other).wait_recv()
+
+        @pl.when(k == parts)
+        def _():
+            cotangents(zl).start()
+
+        @pl.when(k + 1 < 2 * parts)
+        def _():
+            start_load(1, lax.rem(k + 1, parts))
+
+        end_load(1, m)
+        gates(1, m, b)
+        return 0
+
+    lax.fori_loop(0, 2 * parts, job1, 0)
+    keep_low1 = stash(3, low, low1)
     keep_low1.start()
     chains[1].run(ends, first, False)
+    keep_p0.wait()
     own_cot.wait()
-    cotangents(1 - zl).wait_recv()
 
     def step_back(b, i, cols, top, peep):
         before, gate, up = np_[b, i, :, cols], rpre[b, i, :, cols], f[b, i, :, cols]
@@ -580,11 +618,17 @@
 
         lax.fori_loop(0, parts, tile, 0)
 
-    turn_round(0)
-    turn_round(1)
-    results(own).start()
-    own_result = stash(9, resbuf.at[zl], result.at[:, own])
-    own_result.start()
+    def blocks(k, _):
+        @pl.when(k == 1)
+        def _():
+            cotangents(1 - zl).wait_recv()
+
+        turn_round(jnp.where(k == 0, zl, 1 - zl))
+        return 0
+
+    lax.fori_loop(0, 2, blocks, 0)
+    keep_res = stash(9, resbuf, res1)
+    keep_res.start()
     chains[2].run(ends, first, True)
 
     def down(b):
@@ -634,27 +678,33 @@
 
         lax.fori_loop(0, parts, tile, 0)
 
+    keep_low1.wait()
+
+    def last(b):
+        yield stash(3, du.at[rows_of(b)], du1.at[rows_of(b)])
+        yield stash(4, cand.at[b], dn1.at[b])
+        yield stash(5, rpre.at[b], dhr1.at[b])
+
     down(0)
+    for copy in last(0):
+        copy.start()
     down(1)
-    last = [
-        stash(3, du, du1), stash(4, cand, dn1), stash(5, rpre, dhr1), stash(6, u, u1),
-    ]
-    for copy in last:
+    for copy in last(0):
+        copy.wait()
+    for copy in last(1):
         copy.start()
-    for copy in last + [keep_low1, own_result]:
-        copy.wait()
-    results(other).wait_recv()
     gather.finish()
     for stage in range(4):
         for copy in vcopies(stage, False):
             copy.wait_send()
+    for copy in list(last(1)) + [keep_u1, keep_res]:
+        copy.wait()
     tokens(zl).wait_send()
     cotangents(zl).wait_send()
     keeps(zl).wait_send()
     for b in range(2):
         statistics(b, st_got).wait_send()
         lows(b, own).wait_send()
-    results(own).wait_send()
 
 
 def call_forward(seq, row, tok, cot, keep, vin, w_own):
@@ -684,7 +734,7 @@
             arr(2, 2, 2, steps, SUB, LANE),
         ]
         + [act] * 6
-        + [half, half, act, act, act, arr(2 * t, 3 * H, dtype=BF16), arr(t, d, dtype=BF16)]
+        + [half, half, act, act, act, arr(2 * t, 3 * H, dtype=BF16), arr(2, t, H, dtype=BF16)]
         + [arr(2, 4, SUB, H)],
         scratch_shapes=[
             pltpu.VMEM((2, t, d), BF16),
@@ -708,8 +758,8 @@
             dma((count,)),
             dma((count,)),
             dma((2, 2)),
-            dma((8,)),
-            dma((8,)),
+            dma((7,)),
+            dma((7,)),
             dma((3, Z // 2 * X)),
             dma((3, Z // 2 * X)),
             dma((10,)),
@@ -910,8 +960,8 @@
 
 def backward_all(
     seq, row, w_all, vec, keep, stats, f0, g0, cand0, p0, r0, u0, low0, low1, u1, dhr1, dn1, du1,
-    sums1,
-    grad, input_grad, vout,
+    res1, sums1,
+    grad, input_grad, result, vout,
     wbuf, du, low, dn, dnsend, dnrecv, u, dhr, stream, proj, top_of,
     keep0, send0, recv0, keep1, send1, recv1, keep2, send2, recv2, keep3, send3, recv3, done,
     ends, first, table, b_own, b_got, b_fin, sums, vbuf, vr0, vr1, vr2, vr3,
@@ -975,6 +1025,12 @@
     def outputs(b, cols):
         return pair(4, dnsend.at[b], input_grad.at[:, cols])
 
+    def results(cols):
+        return pair(5, res1.at[1 - zl], result.at[:, cols])
+
+    own_result = load(5, res1.at[zl], result.at[:, own])
+    own_result.start()
+    results(own).start()
     across = (((1,), (1,)), ((), ()))
 
     def theirs(b, _):
@@ -1253,6 +1309,9 @@
     for b in range(2):
         statistics(b).wait_send()
     own_out.wait()
+    own_result.wait()
+    results(own).wait_send()
+    results(other).wait_recv()
     outputs(1 - zl, own).wait_send()
     outputs(1 - zl, other).wait_recv()
 
@@ -1276,9 +1335,9 @@
 
     return pl.pallas_call(
         lambda *refs: backward_all(seq, row, *refs),
-        in_specs=[hbm, vmem, vmem, vmem] + [hbm] * 12 + [vmem],
-        out_specs=[hbm, hbm, vmem],
-        out_shape=[arr(layers, per, 3 * d), arr(t, d, dtype=BF16), arr(16, LANE)],
+        in_specs=[hbm, vmem, vmem, vmem] + [hbm] * 13 + [vmem],
+        out_specs=[hbm, hbm, hbm, vmem],
+        out_shape=[arr(layers, per, 3 * d)] + [arr(t, d, dtype=BF16)] * 2 + [arr(16, LANE)],
         scratch_shapes=[
             buf(Z // 2, X, Y, 2, per, 3 * H),
             buf(2 * t, 3 * H),
@@ -1306,10 +1365,10 @@
             buf(Z - 1, 16, LANE, dtype=F32),
             dma((4, count)), dma((4, count)),
             dma((2, 2 * parts, 3)),
-            dma((5,)), dma((5,)),
+            dma((6,)), dma((6,)),
             dma((Z // 2 * X,)), dma((Z // 2 * X,)),
             dma((count,)), dma((count,)),
-            dma((5,)),
+            dma((6,)),
             dma((2, 5)),
             dma((2 * parts,)),
         ],
@@ -1344,8 +1403,7 @@
     out = call_forward(
         seq, row, permuted(tokens[0]), permuted(cotangent[0]), keep, packed, local
     )
-    result, sums = out[-2:]
-    grad, input_grad, vectors = call_backward(seq, row, t, d, tuple(out[:-2]) + (sums,))
+    grad, input_grad, result, vectors = call_backward(seq, row, t, d, out)
     return (restored(result), restored(input_grad), grad) + tuple(
         jnp.stack([vectors[l * 8 + k, :per] for l in range(layers)]) for k in range(6)
     )

time: 596 us -> 528 us (0.89)
  Pallas kernels: 559 us -> 492 us
    pallas_call x1, Pallas kernels: 290 us -> 219 us  [call_forward(): pl.pallas_call(lambda *refs: forward_all(seq, row, *refs), in_specs=[hbm,...]
where the time goes in v4:
time: 528 us
  Pallas kernels  492 us (93%)
  local copies, waits for them, and re-layouts  30.3 us (6%)
    pallas_call x1, Pallas kernels, call_backward(): pl.pallas_call(lambda *refs: backward_all(seq, row, *refs), in_specs=[hbm...  274 us
    pallas_call x1, Pallas kernels, call_forward(): pl.pallas_call(lambda *refs: forward_all(seq, row, *refs), in_specs=[hbm,...  219 us

profile of v4, /device:TPU:0, one launch (start us, length us, event | category | flops | bytes accessed | tf_op | source)
XLA Modules:
  0.0 527.5 jit_solution(13081847906110457217)
XLA Ops:
  0.6 0.7 copy.34
  1.3 0.7 copy.35
  2.0 0.7 copy.36
  2.6 0.7 copy.37
  3.3 0.7 copy.38
  3.9 0.7 copy.39
  4.6 0.6 pad.9.refs_3_
  5.2 0.7 convert_reduce_fusion
  6.2 0.6 pad.8.refs_2_
  6.8 4.9 reshape.64
  11.7 2.6 copy.46
  14.2 2.5 reshape.65.refs_4_
  16.7 6.5 %copy_bitcast_fusion.1 = (bf16[512,2048]{1,0:T(8,128)(2,1)}, bf16[512,2048]{1,0:T(8,128)(2,1)}) fusion(bf16[8,64,2048]{2,1,0:T(8,128)(2,1)} %bitcast.36, bf16[8,64,2048]{2,1,0:T(8,128)(2,1)} %bitcast.37), kind=kLoop, calls=%fused_computation.1 | loop fusion | bytes 8388608 | tf_op jit(solution)/shard_map/reshape | solution.py:1391
  23.3 218.9 %forward_all.1 = (bf16[2,4,2,4,2,2,2,64,384]{8,7,6,5,4,3,2,1,0:T(8,128)(2,1)}, f32[2,8,2048]{2,1,0:T(8,128)}, f32[2,64,8,128]{3,2,1,0:T(8,128)}, f32[2,2,2,64,8,...) custom-call(bf16[512,2048]{1,0:T(8,128)(2,1)} %get-tuple-element.66., ...), custom_call_target="tpu_custom_call" | custom-call | tf_op jit(solution)/shard_map/forward_all/pallas_call | solution.py:726
  242.2 273.6 %backward_all.1 = (f32[2,64,6144]{2,1,0:T(8,128)}, bf16[512,2048]{1,0:T(8,128)(2,1)}, bf16[512,2048]{1,0:T(8,128)(2,1)}, f32[16,128]{1,0:T(8,128)}) custom-call(bf16[2,4,2,4,2,2,2,64,384]{8,7,6,5,4,3,2,1,0:T(8,128)(2,1)} %get-tuple-element.31.refs_0_, f32[2,8,2048]{2,1,0:T(8,128)} %get-tuple-element.32.refs_1_, f32[2,64,8,128]{3,2,1,0:T(8,128)} %get-tuple-element.33.refs_2_, ...), custom_call_target="tpu_custom_call" | custom-call | tf_op jit(solution)/shard_map/backward_all/pallas_call | solution.py:1336
  515.7 4.2 copy.41
  519.9 2.5 copy.42
  522.4 0.6 pad_maximum_fusion.5
  523.0 0.6 pad_maximum_fusion.4
  523.6 0.6 pad_maximum_fusion.3
  524.1 0.6 pad_maximum_fusion.2
  524.7 0.6 pad_maximum_fusion.1
  525.3 0.6 pad_maximum_fusion
  525.8 1.7 copy.48
  (12 shorter events, 0.3 us)
Async XLA Ops:
  515.7 4.2 copy-start.1
  519.9 2.5 copy-start.2
  519.9 5.9 %copy-start = (f32[2,64,6144]{2,1,0:T(8,128)S(1)}, f32[2,64,6144]{2,1,0:T(8,128)}, u32[]{:S(2)}) copy-start(f32[2,64,6144]{2,1,0:T(8,128)} %get-tuple-element.78) | copy-start | bytes 9437188

commit v5 on v4

--- a/solution.py
+++ b/solution.py
@@ -776,7 +776,10 @@
 
 
 class Scatter:
-    slots = (2, 4, 4, 4)
+    lag = (0, 1, 3, 5, 7)
+    sends = (2, 4, 4, 4)
+    slots = (2, 6, 6, 6)
+    kept = (1, 3, 3, 3)
 
     def __init__(self, pos, count, low, du, out, keep, send, recv, done, snd, rcv, outs):
         self.pos, self.count, self.low, self.du, self.out = pos, count, low, du, out
@@ -789,12 +792,12 @@
         return ("c", ("x", "y")[h], ("y", "x")[h], "z")[stage]
 
     def copy(self, g, stage, h, k):
-        slot = wrap(g, self.slots[stage])
+        mine, slot = wrap(g, self.sends[stage]), wrap(g, self.slots[stage])
         sem = self.base[stage] + k - 1
         to = self.pos.device(self.pos.moved(self.axis(stage, h), k))
         return remote(
-            self.send[stage].at[slot, k - 1], self.recv[stage].at[slot, k - 1],
-            self.snd.at[slot, sem], self.rcv.at[slot, sem], to,
+            self.send[stage].at[mine, k - 1], self.recv[stage].at[slot, k - 1],
+            self.snd.at[mine, sem], self.rcv.at[slot, sem], to,
         )
 
     def each(self, stage, h):
@@ -806,10 +809,10 @@
                 self.copy(g, stage, h, k).wait_send()
 
         if isinstance(g, int):
-            if g >= self.slots[stage]:
+            if g >= self.sends[stage]:
                 wait()
         else:
-            pl.when(g >= self.slots[stage])(wait)
+            pl.when(g >= self.sends[stage])(wait)
 
     def start(self, g, stage, h):
         for k in self.each(stage, h):
@@ -844,8 +847,7 @@
 
     def stage1(self, g, h):
         pos, axis = self.pos, self.axis(1, h)
-        slot = wrap(g, 4)
-        got = wrap(g, 2)
+        slot, got, mine = wrap(g, 4), wrap(g, 2), wrap(g, 3)
         self.arrive(g, 0, h)
         self.ready(g, 1, h)
         for k in range(pos.sizes[axis]):
@@ -855,7 +857,7 @@
                 where = (z, p) if h == 0 else (z, slice(None), p)
                 v = self.keep[0][where] + self.recv[0][(got, 0) + where].astype(F32)
                 if k == 0:
-                    self.keep[1][got, z] = v
+                    self.keep[1][mine, z] = v
                 else:
                     self.send[1][slot, k - 1, z] = v.astype(BF16)
                 return 0
@@ -865,14 +867,14 @@
 
     def stage2(self, g, h):
         pos, axis = self.pos, self.axis(2, h)
-        slot, mine = wrap(g, 4), wrap(g, 2)
+        slot, got, mine = wrap(g, 4), wrap(g, 6), wrap(g, 3)
         self.arrive(g, 1, h)
         self.ready(g, 2, h)
         for k in range(pos.sizes[axis]):
             p = pos.moved(axis, k)[axis]
             v = self.keep[1][mine, :, p]
             for e in self.each(1, h):
-                v = v + self.recv[1][slot, e - 1, :, p].astype(F32)
+                v = v + self.recv[1][got, e - 1, :, p].astype(F32)
             if k == 0:
                 self.keep[2][mine] = v
             else:
@@ -881,14 +883,14 @@
 
     def stage3(self, g, h):
         pos = self.pos
-        slot, mine = wrap(g, 4), wrap(g, 2)
+        slot, got, mine = wrap(g, 4), wrap(g, 6), wrap(g, 3)
         self.arrive(g, 2, h)
         self.ready(g, 3, h)
         for k in range(pos.Z):
             p = pos.moved("z", k)["z"]
             v = self.keep[2][mine, p]
             for e in self.each(2, h):
-                v = v + self.recv[2][slot, e - 1, p].astype(F32)
+                v = v + self.recv[2][got, e - 1, p].astype(F32)
             if k == 0:
                 self.keep[3][mine] = v
             else:
@@ -899,34 +901,44 @@
         d = self.out.shape[-1] // 3
         at = e * d + half * (d // 2) + q * LANE
         return pltpu.make_async_copy(
-            self.done.at[half, q, :, e * LANE : (e + 1) * LANE],
+            self.done.at[half, wrap(q, 4), :, e * LANE : (e + 1) * LANE],
             self.out.at[l, :, pl.ds(pl.multiple_of(at, LANE), LANE)],
-            self.outs.at[half, q, e],
+            self.outs.at[half, wrap(q, 4), e],
         )
 
     def stage4(self, g, h, l):
         pos = self.pos
-        slot, mine, q = wrap(g, 4), wrap(g, 2), wrap(g, self.count)
+        got, mine, q = wrap(g, 6), wrap(g, 3), wrap(g, self.count)
         self.arrive(g, 3, h)
         own, other = self.keep[3][mine], None
         for k in range(1, pos.Z):
-            v = self.recv[3][slot, k - 1].astype(F32)
+            v = self.recv[3][got, k - 1].astype(F32)
             if k % 2 == 0:
                 own = own + v
             else:
                 other = v if other is None else other + v
-        self.done[pos.zl, q] = own
-        self.done[1 - pos.zl, q] = other
+        if isinstance(q, int):
+            if q >= 4:
+                self.stored(l, q - 4)
+        else:
+            pl.when(q >= 4)(lambda: self.stored(l, q - 4))
+        self.done[pos.zl, wrap(q, 4)] = own
+        self.done[1 - pos.zl, wrap(q, 4)] = other
         for half in (pos.zl, 1 - pos.zl):
             for e in range(3):
                 self.result(l, q, half, e).start()
 
+    def stored(self, l, q):
+        for half in (self.pos.zl, 1 - self.pos.zl):
+            for e in range(3):
+                self.result(l, q, half, e).wait()
+
     def turn(self, run, l, pair, e, enters=True):
         first = run * self.count
 
         def stage(s, f):
-            g = first + 2 * pair + e - s
-            h = (e - s) % 2
+            g = first + 2 * pair + e - self.lag[s]
+            h = (e - self.lag[s]) % 2
             if isinstance(g, int):
                 if first <= g < first + self.count:
                     f(g, h)
@@ -943,28 +955,23 @@
         stage(4, lambda g, h: self.stage4(g, h, l))
 
     def written(self, l):
-        def one(q, _):
-            for half in (self.pos.zl, 1 - self.pos.zl):
-                for e in range(3):
-                    self.result(l, q, half, e).wait()
-            return 0
-
-        lax.fori_loop(0, self.count, one, 0)
+        for q in range(self.count - 4, self.count):
+            self.stored(l, q)
 
     def finish(self, total):
         for stage in range(4):
-            for g in range(total - self.slots[stage], total):
+            for g in range(total - self.sends[stage], total):
                 for k in self.each(stage, g % 2):
                     self.copy(g, stage, g % 2, k).wait_send()
 
 
 def backward_all(
-    seq, row, w_all, vec, keep, stats, f0, g0, cand0, p0, r0, u0, low0, low1, u1, dhr1, dn1, du1,
-    res1, sums1,
+    seq, row, w_all, vec, keep, stats_all, f0, g0, cand0, p0, r0, u0, low0, low1, u1, dhr1, dn1, du1,
+    res1, sums1, tok,
     grad, input_grad, result, vout,
-    wbuf, du, low, dn, dnsend, dnrecv, u, dhr, stream, proj, top_of,
+    stats, wbuf, du, low, dn, dnsend, dnrecv, hsend, hrecv, tokx, u, dhr, stream, proj,
     keep0, send0, recv0, keep1, send1, recv1, keep2, send2, recv2, keep3, send3, recv3, done,
-    ends, first, table, b_own, b_got, b_fin, sums, vbuf, vr0, vr1, vr2, vr3,
+    ends, first, table, b_own, b_got, b_fin, sums, sumsx, vbuf, vr0, vr1, vr2, vr3,
     snd, rcv, gouts, psnd, prcv, csnd, crcv, vsnd, vrcv, ins, ssem, wsem,
 ):
     pos = Place(seq, row)
@@ -1006,7 +1013,8 @@
     get_du, get_low, get_dn = load(0, du1, du), load(1, low1, low), load(2, dn1, dn)
     get_u, get_dhr = load(3, u1, u), load(4, dhr1, dhr)
     begin(weights(1, 1 - zl))
-    begin([get_du, get_low, get_dn, get_u, get_dhr])
+    get_stats = load(6, stats_all.at[1], stats)
+    begin([get_du, get_low, get_dn, get_u, get_dhr, get_stats])
     scatter = Scatter(
         pos, 2 * parts, low, du, grad, (keep0, keep1, keep2, keep3), (send0, send1, send2, send3),
         (recv0, recv1, recv2, recv3), done, snd, rcv, gouts,
@@ -1022,8 +1030,8 @@
     def statistics(b):
         return pair(2 + b, b_own.at[b], b_got.at[b])
 
-    def outputs(b, cols):
-        return pair(4, dnsend.at[b], input_grad.at[:, cols])
+    def carried():
+        return pair(4, hsend, hrecv)
 
     def results(cols):
         return pair(5, res1.at[1 - zl], result.at[:, cols])
@@ -1033,23 +1041,35 @@
     results(own).start()
     across = (((1,), (1,)), ((), ()))
 
-    def theirs(b, _):
-        v = lax.dot_general(
-            du[rows_of(b), :], wbuf[...].reshape(H, H3), across, preferred_element_type=F32
-        )
-        dnsend[b] = v.astype(BF16)
-        partial_sums(b).start()
-        return 0
-
-    def ours(k):
-        n = t2 // parts
-        rows = pl.ds(pl.multiple_of(k * n, n), n)
-        v = lax.dot_general(
+    n = t2 // parts
+    blocks = t // n
+
+    def product(b, k):
+        rows = pl.ds(pl.multiple_of(b * t + k * n, n), n)
+        return lax.dot_general(
             du[rows, :], wbuf[...].reshape(H, H3), across, preferred_element_type=F32
         )
-        blocks = t // n
-        spot = pl.ds(pl.multiple_of(lax.rem(k, blocks) * (n // SUB), n // SUB), n // SUB)
-        dn[k // blocks, spot] += v.reshape(n // SUB, SUB, H)
+
+    def of_block(k):
+        return pl.ds(pl.multiple_of(k * (n // SUB), n // SUB), n // SUB)
+
+    def theirs(q, b, more=None):
+        def one(k, _):
+            v = product(b, k)
+            if more is not None:
+                v = v + more[of_block(k)].reshape(n, H)
+            dnsend[q, pl.ds(pl.multiple_of(k * n, n), n), :] = v.astype(BF16)
+            return 0
+
+        lax.fori_loop(0, blocks, one, 0)
+        partial_sums(q).start()
+
+    def ours(to, b, k, fresh=False):
+        v = product(b, k).reshape(n // SUB, SUB, H)
+        if fresh:
+            dn[to, of_block(k)] = v
+        else:
+            dn[to, of_block(k)] += v
 
     half = t // LANE
 
@@ -1073,8 +1093,8 @@
         statistics(b).start()
 
     def hat(l, b, spot):
-        mu = stats[l, 0, b, spot].reshape(LANE, LANE)[:, :1]
-        rstd = stats[l, 1, b, spot].reshape(LANE, LANE)[:, :1]
+        mu = stats[0, b, spot].reshape(LANE, LANE)[:, :1]
+        rstd = stats[1, b, spot].reshape(LANE, LANE)[:, :1]
         return (u[b, spot].reshape(LANE, H) - mu) * rstd
 
     def norm_back(l, b):
@@ -1084,31 +1104,67 @@
         def one(q, _):
             spot = pl.ds(q * (LANE // SUB), LANE // SUB)
             xhat = hat(l, b, spot)
-            rstd = stats[l, 1, b, spot].reshape(LANE, LANE)[:, :1]
+            rstd = stats[1, b, spot].reshape(LANE, LANE)[:, :1]
             m0 = to_column(b_fin[pl.ds(q, 1), :])
             m1 = to_column(b_fin[pl.ds(q + half, 1), :])
             v = dn[b, spot].reshape(LANE, H) * vec[l, GAIN : GAIN + 1, own]
             v = dhr[b, spot].reshape(LANE, H) + rstd * (v - m0 - xhat * m1)
-            if l == 1:
-                dhr[b, spot] = v.reshape(LANE // SUB, SUB, H)
-            else:
-                dnsend[b, pl.ds(pl.multiple_of(q * LANE, LANE), LANE), :] = v.astype(BF16)
+            dhr[b, spot] = v.reshape(LANE // SUB, SUB, H)
             return 0
 
         lax.fori_loop(0, half, one, 0)
+
+    def norm_last():
+        for q in range(2):
+            partial_sums(q).wait_recv()
+        carried().wait_recv()
+        get_tok.wait()
+        piece = 4
+        n = piece * SUB
+
+        def one(k, _):
+            spot = pl.ds(k * piece, piece)
+            rows = pl.ds(pl.multiple_of(k * n, n), n)
+            mu = stats[0, zl, spot].reshape(n, LANE)[:, :1]
+            rstd = stats[1, zl, spot].reshape(n, LANE)[:, :1]
+            scaled, hats = [], []
+            m0 = m1 = 0.0
+            for q, part in enumerate((zl, 1 - zl)):
+                x = u[zl, spot].reshape(n, H) if q == 0 else tokx[rows, :].astype(F32)
+                xhat = (x - mu) * rstd
+                v = dn[part, spot].reshape(n, H) + dnrecv[q, rows, :].astype(F32)
+                total = sums.at[0] if q == 0 else sumsx
+                total[0] += jnp.sum((v * xhat).reshape(piece, SUB, H), axis=0)
+                total[1] += jnp.sum(v.reshape(piece, SUB, H), axis=0)
+                v = v * vec[0, GAIN : GAIN + 1, own if q == 0 else other]
+                m0 += jnp.sum(v, axis=-1, keepdims=True)
+                m1 += jnp.sum(v * xhat, axis=-1, keepdims=True)
+                scaled.append(v)
+                hats.append(xhat)
+            m0, m1 = m0 * (1.0 / d), m1 * (1.0 / d)
+            for q in range(2):
+                v = rstd * (scaled[q] - m0 - hats[q] * m1)
+                if q == 0:
+                    v = v + dhr[zl, spot].reshape(n, H)
+                else:
+                    v = v + hrecv[rows, :].astype(F32)
+                dnsend[q, rows, :] = v.astype(BF16)
+            return 0
+
+        lax.fori_loop(0, steps // piece, one, 0)
 
     units = 2 * parts
     sources = (f0, g0, cand0, p0, r0)
 
     def fetch(k):
         slot = lax.rem(k, 2)
-        b, m = k // parts, lax.rem(k, parts)
+        b, m = jnp.where(k < parts, 1 - zl, zl), lax.rem(k, parts)
         for j, src in enumerate(sources):
             yield pltpu.make_async_copy(
                 src.at[b, :, :, lane_tile(m, WIDE)], stream.at[slot, j], ssem.at[slot, j]
             )
 
-    def tiles(work):
+    def tiles(work, between=None):
         begin(fetch(0))
 
         def one(k, _):
@@ -1117,10 +1173,12 @@
                 begin(fetch(k + 1))
 
             end(fetch(k))
-            b, m = k // parts, lax.rem(k, parts)
+            b, m = jnp.where(k < parts, 1 - zl, zl), lax.rem(k, parts)
             cols = lane_tile(m, WIDE)
             wide = pl.ds(pl.multiple_of(zl * H + m * WIDE, WIDE), WIDE)
             work(lax.rem(k, 2), b, m, cols, wide)
+            if between is not None:
+                between(k)
             return 0
 
         lax.fori_loop(0, units, one, 0)
@@ -1144,13 +1202,23 @@
 
         def one(k, carry):
             scale, q = carry
-            decay, term = step_back(slot, b, steps - 1 - k, cols, peep)[-2:]
+            i = steps - 1 - k
+            terms = step_back(slot, b, i, cols, peep)
+            gate, top, decay, term = terms[4], terms[5], terms[-2], terms[-1]
+            proj[i, :, :WIDE] = top * (1.0 - gate)
             return scale * decay, decay * q + term
 
         start = jnp.ones((SUB, WIDE), F32), jnp.zeros((SUB, WIDE), F32)
         scale, q = lax.fori_loop(0, steps, one, start, unroll=8)
         ends[b, 0, :, cols] = scale
         ends[b, 1, :, cols] = q
+
+        @pl.when(b != zl)
+        def _():
+            hsend[:, cols] = proj[:, :, :WIDE].reshape(t, WIDE).astype(BF16)
+
+    def send_carried(k):
+        pl.when(k == parts - 1)(lambda: carried().start())
 
     def down_work(slot, b, m, cols, wide):
         fpeep, rpeep, gain, shift = (row_wide(0, k, wide) for k in (FPEEP, RPEEP, GAIN, SHIFT))
@@ -1163,8 +1231,8 @@
             )
             e = direct + q
             dz_f = e * (up * low_f) * (before - cd)
-            n = (u[b, i, :, cols] - lanes(stats[0, 0, b, i], WIDE)) * lanes(
-                stats[0, 1, b, i], WIDE
+            n = (u[b, i, :, cols] - lanes(stats[0, b, i], WIDE)) * lanes(
+                stats[1, b, i], WIDE
             ) * gain + shift
             proj[i, :, :WIDE] = e * low_f
             proj[i, :, WIDE : 2 * WIDE] = dz_f
@@ -1189,76 +1257,119 @@
                 to = pl.ds(pl.multiple_of((2 * m + h) * HALF + k * LANE, LANE), LANE)
                 du[rows_of(b), to] = v.reshape(t, LANE).astype(BF16)
 
-    def layer(run, l):
-        end(weights(l, 1 - zl))
-        lax.fori_loop(0, 2, theirs, 0)
-        begin(weights(l, zl))
-
-        def one(k, _):
-            scatter.turn(run, l, k, 0)
-
-            @pl.when(k == 0)
-            def _():
-                end(weights(l, zl))
-
-            ours(k)
-            scatter.turn(run, l, k, 1)
-            return 0
-
-        lax.fori_loop(0, parts, one, 0)
+    def late(run, l, k):
+        scatter.turn(run, l, parts + k // 2, k % 2, False)
 
     sums[...] = jnp.zeros_like(sums)
+    sumsx[...] = jnp.zeros_like(sumsx)
     sums[1, 2:6] = sums1[0] + sums1[1]
     get_du.wait()
+    end(weights(1, 1 - zl))
+    for b in range(2):
+        theirs(b, b)
+    begin(weights(1, zl))
     get_low.wait()
     get_dn.wait()
-    layer(0, 1)
+
+    def last_layer(k, _):
+        scatter.turn(0, 1, k, 0)
+
+        @pl.when(k == 0)
+        def _():
+            end(weights(1, zl))
+
+        ours(k // blocks, k // blocks, lax.rem(k, blocks))
+        scatter.turn(0, 1, k, 1)
+        return 0
+
+    lax.fori_loop(0, parts, last_layer, 0)
     get_low = load(1, low0, low)
     get_low.start()
     get_u.wait()
     get_dhr.wait()
+    get_stats.wait()
     begin(weights(0, 1 - zl))
     norm_sums(1, 0)
     norm_sums(1, 1)
-    scatter.turn(0, 1, parts, 0, False)
+    late(0, 1, 0)
     norm_back(1, 0)
     norm_back(1, 1)
-    get_u = load(3, u0, u)
-    get_u.start()
-    scatter.turn(0, 1, parts, 1, False)
+    get_u, get_stats = load(3, u0, u), load(6, stats_all.at[0], stats)
+    get_tok = load(7, tok.at[:, other], tokx)
+    begin([get_u, get_stats, get_tok])
+    late(0, 1, 1)
     get_u.wait()
-    tiles(ends_work)
-    scatter.turn(0, 1, parts + 1, 0, False)
+    get_stats.wait()
+    late(0, 1, 2)
+    tiles(ends_work, send_carried)
+    late(0, 1, 3)
     chain.run(ends, first, True)
-    scatter.turn(0, 1, parts + 1, 1, False)
-    tiles(down_work)
+    for k in range(4, 7):
+        late(0, 1, k)
     for b in range(2):
         partial_sums(b).wait_send()
         statistics(b).wait_send()
+    end(weights(0, 1 - zl))
+
+    def between(k):
+        @pl.when(k == parts - 1)
+        def _():
+            theirs(0, 1 - zl)
+            begin(weights(0, zl))
+
+    tiles(down_work, between)
+    end(weights(0, zl))
+    theirs(1, 1 - zl, dn.at[1 - zl])
     scatter.written(1)
     get_low.wait()
-    layer(1, 0)
-    norm_sums(0, 0)
-    norm_sums(0, 1)
-    scatter.turn(1, 0, parts, 0, False)
+
+    def first_layer(k, _):
+        scatter.turn(1, 0, k, 0)
+
+        @pl.when(k < blocks)
+        def _():
+            ours(zl, zl, k)
+
+        @pl.when(k == blocks - 1)
+        def _():
+            begin(weights(0, 1 - zl))
+
+        @pl.when(k == blocks)
+        def _():
+            end(weights(0, 1 - zl))
+
+        @pl.when(k >= blocks)
+        def _():
+            ours(1 - zl, zl, k - blocks, True)
+
+        scatter.turn(1, 0, k, 1)
+        return 0
+
+    lax.fori_loop(0, parts, first_layer, 0)
+    late(1, 0, 0)
+    late(1, 0, 1)
     for b in range(2):
         partial_sums(b).wait_send()
-    norm_back(0, 0)
-    norm_back(0, 1)
-    outputs(1 - zl, own).start()
-    own_out = load(0, dnsend.at[zl], input_grad.at[:, own])
-    own_out.start()
-    scatter.turn(1, 0, parts, 1, False)
+    norm_last()
+    out_own = load(0, dnsend.at[0], input_grad.at[:, own])
+    out_other = load(1, dnsend.at[1], input_grad.at[:, other])
+    begin([out_own, out_other])
+    late(1, 0, 2)
+    late(1, 0, 3)
 
     vbuf[...] = jnp.zeros_like(vbuf)
     per = d // (seq * row)
     total = [jnp.sum(sums[l], axis=1) for l in range(2)]
+    totalx = jnp.sum(sumsx[...], axis=1)
     blank = jnp.zeros((6, LANE - per), F32) if per < LANE else None
     for i in range(H // per):
         spot = (zl * (pos.Z // 2) + i // (2 * pos.Y * pos.X), i // (2 * pos.Y) % pos.X, i // 2 % pos.Y, i % 2)
         for l in range(2):
             piece = total[l][:, i * per : (i + 1) * per]
             vbuf[spot + (slice(l * 8, l * 8 + 6),)] = jnp.concatenate([piece, blank], axis=-1)
+        away = (lax.rem(spot[0] + pos.Z // 2, pos.Z),) + spot[1:]
+        piece = totalx[:, i * per : (i + 1) * per]
+        vbuf[away + (slice(0, 2),)] = jnp.concatenate([piece, blank[:2]], axis=-1)
     every = slice(None)
 
     def vspot(stage, who):
@@ -1291,12 +1402,13 @@
             vbuf[vspot(stage, at)] += vrecv[stage][k - 1]
 
     vstart(0)
-    scatter.turn(1, 0, parts + 1, 0, False)
+    late(1, 0, 4)
     vtake(0)
     vstart(1)
-    scatter.turn(1, 0, parts + 1, 1, False)
+    late(1, 0, 5)
     vtake(1)
     vstart(2)
+    late(1, 0, 6)
     vtake(2)
     vstart(3)
     vtake(3)
@@ -1306,14 +1418,11 @@
             vcopy(stage, k).wait_send()
     scatter.written(0)
     scatter.finish(2 * scatter.count)
-    for b in range(2):
-        statistics(b).wait_send()
-    own_out.wait()
+    carried().wait_send()
+    end([out_own, out_other])
     own_result.wait()
     results(own).wait_send()
     results(other).wait_recv()
-    outputs(1 - zl, own).wait_send()
-    outputs(1 - zl, other).wait_recv()
 
 
 def call_backward(seq, row, t, d, given):
@@ -1325,7 +1434,7 @@
     hbm = pl.BlockSpec(memory_space=pl.ANY)
     dma = pltpu.SemaphoreType.DMA
     big = pltpu.VMEM((2, steps, SUB, H), F32)
-    half = pltpu.VMEM((2, t, H), BF16)
+    half, quarter = pltpu.VMEM((2, t, H), BF16), pltpu.VMEM((t, H), BF16)
     st = pltpu.VMEM((2, 8, LANE), F32)
     count = 1 + 2 * (X - 1) + Z - 1
     chunk = (Z, X, Y, per, HALF)
@@ -1335,45 +1444,46 @@
 
     return pl.pallas_call(
         lambda *refs: backward_all(seq, row, *refs),
-        in_specs=[hbm, vmem, vmem, vmem] + [hbm] * 13 + [vmem],
+        in_specs=[hbm, vmem, vmem] + [hbm] * 14 + [vmem, hbm],
         out_specs=[hbm, hbm, hbm, vmem],
         out_shape=[arr(layers, per, 3 * d)] + [arr(t, d, dtype=BF16)] * 2 + [arr(16, LANE)],
         scratch_shapes=[
+            buf(2, 2, steps, SUB, LANE, dtype=F32),
             buf(Z // 2, X, Y, 2, per, 3 * H),
             buf(2 * t, 3 * H),
             buf(2 * t, d),
-            big, half, half, big, big,
+            big, half, half, quarter, quarter, quarter, big, big,
             buf(2, 5, steps, SUB, WIDE, dtype=F32),
             buf(steps, SUB, 3 * WIDE, dtype=F32),
-            buf(8, LANE, dtype=F32),
             buf(*chunk, dtype=F32), buf(2, 1, *chunk), buf(2, 1, *chunk),
-            buf(2, Z, Y, per, HALF, dtype=F32), buf(4, X - 1, Z, Y, per, HALF),
-            buf(4, X - 1, Z, Y, per, HALF),
-            buf(2, Z, per, HALF, dtype=F32), buf(4, Y - 1, Z, per, HALF),
-            buf(4, Y - 1, Z, per, HALF),
-            buf(2, per, HALF, dtype=F32), buf(4, Z - 1, per, HALF), buf(4, Z - 1, per, HALF),
-            buf(2, 2 * parts, per, HALF, dtype=F32),
+            buf(3, Z, Y, per, HALF, dtype=F32), buf(4, X - 1, Z, Y, per, HALF),
+            buf(6, X - 1, Z, Y, per, HALF),
+            buf(3, Z, per, HALF, dtype=F32), buf(4, Y - 1, Z, per, HALF),
+            buf(6, Y - 1, Z, per, HALF),
+            buf(3, per, HALF, dtype=F32), buf(4, Z - 1, per, HALF), buf(6, Z - 1, per, HALF),
+            buf(2, 4, per, HALF, dtype=F32),
             buf(2, 2, SUB, H, dtype=F32),
             buf(2, SUB, H, dtype=F32),
             buf(Z // 2, X, 2, 2, H, dtype=F32),
             st, st, buf(8, LANE, dtype=F32),
             buf(2, 6, SUB, H, dtype=F32),
+            buf(2, SUB, H, dtype=F32),
             buf(Z, X, Y, 2, 16, LANE, dtype=F32),
             buf(1, Z, X, Y, 16, LANE, dtype=F32),
             buf(X - 1, Z, Y, 16, LANE, dtype=F32),
             buf(Y - 1, Z, 16, LANE, dtype=F32),
             buf(Z - 1, 16, LANE, dtype=F32),
-            dma((4, count)), dma((4, count)),
-            dma((2, 2 * parts, 3)),
+            dma((4, count)), dma((6, count)),
+            dma((2, 4, 3)),
             dma((6,)), dma((6,)),
             dma((Z // 2 * X,)), dma((Z // 2 * X,)),
             dma((count,)), dma((count,)),
-            dma((6,)),
+            dma((8,)),
             dma((2, 5)),
             dma((2 * parts,)),
         ],
         compiler_params=pltpu.CompilerParams(
-            collective_id=1, has_side_effects=True, vmem_limit_bytes=62 << 20
+            collective_id=1, has_side_effects=True, vmem_limit_bytes=63 << 20
         ),
         name="backward_all",
     )(*given)
@@ -1403,7 +1513,7 @@
     out = call_forward(
         seq, row, permuted(tokens[0]), permuted(cotangent[0]), keep, packed, local
     )
-    grad, input_grad, result, vectors = call_backward(seq, row, t, d, out)
+    grad, input_grad, result, vectors = call_backward(seq, row, t, d, tuple(out) + (permuted(tokens[0]),))
     return (restored(result), restored(input_grad), grad) + tuple(
         jnp.stack([vectors[l * 8 + k, :per] for l in range(layers)]) for k in range(6)
     )

time: 528 us -> 479 us (0.907)
  Pallas kernels: 492 us -> 443 us
    pallas_call x1, Pallas kernels: 274 us -> 225 us  [call_backward(): pl.pallas_call(lambda *refs: backward_all(seq, row, *refs), in_specs=[hbm...]
where the time goes in v5:
time: 479 us
  Pallas kernels  443 us (92%)
  local copies, waits for them, and re-layouts  30.3 us (6%)
    pallas_call x1, Pallas kernels, call_backward(): pl.pallas_call(lambda *refs: backward_all(seq, row, *refs), in_specs=[hbm...  225 us
    pallas_call x1, Pallas kernels, call_forward(): pl.pallas_call(lambda *refs: forward_all(seq, row, *refs), in_specs=[hbm,...  219 us

profile of v5, /device:TPU:0, one launch (start us, length us, event | category | flops | bytes accessed | tf_op | source)
XLA Modules:
  0.0 478.5 jit_solution(15842348824875143885)
XLA Ops:
  0.6 0.7 copy.34
  1.3 0.7 copy.35
  2.0 0.7 copy.36
  2.6 0.7 copy.37
  3.3 0.7 copy.38
  3.9 0.7 copy.39
  4.6 0.6 pad.9.refs_3_
  5.2 0.7 convert_reduce_fusion
  6.2 0.6 pad.8.refs_2_
  6.8 4.9 %reshape.65 = bf16[2,64,3,2,4,2,128]{6,5,4,3,2,1,0:T(2,128)(2,1)} reshape(bf16[2,64,6144]{2,1,0:T(8,128)(2,1)} %param.13) | data formatting | bytes 3145728 | tf_op jit(solution)/shard_map/reshape | solution.py:1511
  11.7 2.6 copy.46
  14.2 2.5 reshape.66.refs_4_
  16.7 6.5 %copy_bitcast_fusion.1 = (bf16[512,2048]{1,0:T(8,128)(2,1)}, bf16[512,2048]{1,0:T(8,128)(2,1)}) fusion(bf16[8,64,2048]{2,1,0:T(8,128)(2,1)} %bitcast.36, bf16[8,64,2048]{2,1,0:T(8,128)(2,1)} %bitcast.37), kind=kLoop, calls=%fused_computation.1 | loop fusion | bytes 8388608 | tf_op jit(solution)/shard_map/reshape | solution.py:1501
  23.3 218.9 %forward_all.1 = (bf16[2,4,2,4,2,2,2,64,384]{8,7,6,5,4,3,2,1,0:T(8,128)(2,1)}, f32[2,8,2048]{2,1,0:T(8,128)}, f32[2,64,8,128]{3,2,1,0:T(8,128)}, f32[2,2,2,64,8,...) custom-call(bf16[512,2048]{1,0:T(8,128)(2,1)} %get-tuple-element.66., ...), custom_call_target="tpu_custom_call" | custom-call | tf_op jit(solution)/shard_map/forward_all/pallas_call | solution.py:726
  242.2 224.6 %backward_all.1 = (f32[2,64,6144]{2,1,0:T(8,128)}, bf16[512,2048]{1,0:T(8,128)(2,1)}, bf16[512,2048]{1,0:T(8,128)(2,1)}, f32[16,128]{1,0:T(8,128)}) custom-call(bf16[2,4,2,4,2,2,2,64,384]{8,7,6,5,4,3,2,1,0:T(8,128)(2,1)} %get-tuple-element.31.refs_0_, f32[2,8,2048]{2,1,0:T(8,128)} %get-tuple-element.32.refs_1_, f32[2,64,8,128]{3,2,1,0:T(8,128)} %get-tuple-element.33.refs_2_, ...), custom_call_target="tpu_custom_call" | custom-call | tf_op jit(solution)/shard_map/backward_all/pallas_call | solution.py:1445
  466.8 4.2 copy.41
  471.0 2.5 copy.42
  473.5 0.6 pad_maximum_fusion.5
  474.0 0.6 pad_maximum_fusion.4
  474.6 0.6 pad_maximum_fusion.3
  475.2 0.6 pad_maximum_fusion.2
  475.7 0.6 pad_maximum_fusion.1
  476.3 0.6 pad_maximum_fusion
  476.9 1.7 copy.48
  (12 shorter events, 0.3 us)
Async XLA Ops:
  466.7 4.2 copy-start.1
  471.0 2.5 copy-start.2
  471.0 5.9 %copy-start = (f32[2,64,6144]{2,1,0:T(8,128)S(1)}, f32[2,64,6144]{2,1,0:T(8,128)}, u32[]{:S(2)}) copy-start(f32[2,64,6144]{2,1,0:T(8,128)} %get-tuple-element.78) | copy-start | bytes 9437188

commit v6 on v5

--- a/solution.py
+++ b/solution.py
@@ -154,7 +154,7 @@
     def turn(self, i):
         total = 2 * self.parts
 
-        @pl.when(i + 4 < total)
+        @pl.when(i < 2)
         def _():
             self.begin(i + 4)
 
@@ -243,9 +243,9 @@
 
 
 def forward_all(
-    seq, row, tok, cot, keep_in, vin, w_own,
-    w_all, vec, keep, stats, f0, g0, cand0, p0, r0, u0, low0, low1, u1, dhr1, dn1, du1, res1,
-    sums, tokbuf, cotbuf, keepc, vall, u, np_, f, g, cand, rpre, low, wbuf, proj, du, resbuf, top_of, ends,
+    seq, row, tok, cot, keep_in, vin, weight,
+    w_all, vec, keep, stats, f0, g0, cand0, p0, r0, u0, low0, low1, u1, dhr1, dn1, du1, res1, resx,
+    sums, w_nat, w_own, tokbuf, cotbuf, keepc, vall, u, np_, f, g, cand, rpre, low, wbuf, proj, du, resbuf, top_of, ends,
     first, tables, st_own, st_got, st_fin,
     gsnd, grcv, gloc, vsnd, vrcv, wsem, psnd, prcv, csnd, crcv, outs,
 ):
@@ -259,7 +259,19 @@
     own = pl.ds(pl.multiple_of(zl * H, H), H)
     other = pl.ds(pl.multiple_of((1 - zl) * H, H), H)
     rows_of = lambda b: pl.ds(pl.multiple_of(b * t, t), t)
+    get_weight = pltpu.make_async_copy(weight, w_nat, outs.at[10])
+    get_weight.start()
     pos.barrier(seq)
+    get_weight.wait()
+    for l in range(2):
+        for p in range(2):
+            for m in range(parts):
+                for h in range(2):
+                    for e in range(3):
+                        start = e * d + p * H + (2 * m + h) * LANE
+                        w_own[l, p, m, h, :, e * LANE : (e + 1) * LANE] = w_nat[
+                            l, :, start : start + LANE
+                        ]
 
     gather = Gather(pos, parts, w_own, w_all, gsnd, grcv, gloc)
     chains = [Chain(pos, tables.at[k], csnd.at[k], crcv.at[k]) for k in range(3)]
@@ -281,6 +293,9 @@
 
     def lows(b, cols):
         return pair(5 + b, low.at[rows_of(b), cols], low.at[rows_of(b), cols])
+
+    def results():
+        return pair(7, resbuf.at[1 - zl, pl.ds(0, t // 2)], resx)
 
     def vcopies(stage, arriving):
         axis = gather.axis(stage, 0)
@@ -405,7 +420,7 @@
             return scale * a, a * state + down * cd
 
         start = jnp.ones((SUB, 2 * LANE), F32), jnp.zeros((SUB, 2 * LANE), F32)
-        scale, state = lax.fori_loop(0, steps, one, start, unroll=8)
+        scale, state = lax.fori_loop(0, steps, one, start, unroll=16)
         ends[b, 0, :, cols] = scale
         ends[b, 1, :, cols] = state
 
@@ -432,6 +447,8 @@
         @pl.when(i == parts + 1)
         def _():
             tokens(1 - zl).wait_recv()
+            for k in range(6, 2 * parts):
+                gather.begin(k)
             norm0(1 - zl)
 
         @pl.when(i > parts)
@@ -487,7 +504,7 @@
                 u[b, i, :, cols] = gate * cell + (1.0 - gate) * u[b, i, :, cols]
                 return cell
 
-            lax.fori_loop(0, steps, one, first[b, :, cols], unroll=8)
+            lax.fori_loop(0, steps, one, first[b, :, cols], unroll=16)
             return 0
 
         lax.fori_loop(0, parts, tile, 0)
@@ -538,8 +555,6 @@
     local_stats(1)
     gather.turn(parts + 4)
     norm1(1)
-    gather.turn(parts + 5)
-    gather.turn(parts + 6)
     start_load(1, 0)
     keep_u1 = stash(2, u, u1)
     keep_u1.start()
@@ -556,6 +571,10 @@
         @pl.when(k == parts)
         def _():
             cotangents(zl).start()
+
+        @pl.when((k == 1) | (k == 2))
+        def _():
+            gather.turn(parts + 4 + k)
 
         @pl.when(k + 1 < 2 * parts)
         def _():
@@ -598,7 +617,7 @@
                 proj[i, :, : 2 * LANE] = gate * cell + (1.0 - gate) * u[b, i, :, cols]
                 return cell
 
-            lax.fori_loop(0, steps, one, first[b, :, cols], unroll=8)
+            lax.fori_loop(0, steps, one, first[b, :, cols], unroll=16)
             v = proj[:, :, : 2 * LANE].reshape(t, 2 * LANE)
             resbuf[b, :, cols] = v.astype(BF16)
 
@@ -611,7 +630,7 @@
                 return scale * decay, decay * q + term
 
             start = jnp.ones((SUB, 2 * LANE), F32), jnp.zeros((SUB, 2 * LANE), F32)
-            scale, q = lax.fori_loop(0, steps, back, start, unroll=8)
+            scale, q = lax.fori_loop(0, steps, back, start, unroll=16)
             ends[b, 0, :, cols] = scale
             ends[b, 1, :, cols] = q
             return 0
@@ -627,6 +646,7 @@
         return 0
 
     lax.fori_loop(0, 2, blocks, 0)
+    results().start()
     keep_res = stash(9, resbuf, res1)
     keep_res.start()
     chains[2].run(ends, first, True)
@@ -666,7 +686,7 @@
 
             top_of[...] = cotbuf[b, :, cols].astype(F32).reshape(steps, SUB, 2 * LANE)
             zero = jnp.zeros((SUB, 2 * LANE), F32)
-            carry = lax.fori_loop(0, steps, one, (first[b, :, cols], zero, zero, zero, zero), unroll=4)
+            carry = lax.fori_loop(0, steps, one, (first[b, :, cols], zero, zero, zero, zero), unroll=16)
             for k in range(4):
                 sums[b, k, :, cols] = carry[k + 1]
             for h in range(2):
@@ -699,6 +719,8 @@
             copy.wait_send()
     for copy in list(last(1)) + [keep_u1, keep_res]:
         copy.wait()
+    results().wait_recv()
+    results().wait_send()
     tokens(zl).wait_send()
     cotangents(zl).wait_send()
     keeps(zl).wait_send()
@@ -707,13 +729,14 @@
         lows(b, own).wait_send()
 
 
-def call_forward(seq, row, tok, cot, keep, vin, w_own):
+def call_forward(seq, row, tok, cot, keep, vin, weight):
     t, d = tok.shape
-    layers, _, parts, _, per, _ = w_own.shape
+    layers, per, _ = weight.shape
     Y = row // 2
     X = Y
     Z = seq // X
     H = d // 2
+    parts = H // WIDE
     steps = t // SUB
     act, stat = arr(2, steps, SUB, H), arr(2, steps, SUB, LANE)
     half = arr(2 * t, d, dtype=BF16)
@@ -726,7 +749,7 @@
     return pl.pallas_call(
         lambda *refs: forward_all(seq, row, *refs),
         in_specs=[hbm, hbm, vmem, vmem, hbm],
-        out_specs=[hbm, vmem, vmem, vmem] + [hbm] * 13 + [vmem],
+        out_specs=[hbm, vmem, vmem, vmem] + [hbm] * 14 + [vmem],
         out_shape=[
             arr(layers, parts, 2, Z, X, Y, 2, per, HALF, dtype=BF16),
             arr(2, 8, d),
@@ -734,9 +757,11 @@
             arr(2, 2, 2, steps, SUB, LANE),
         ]
         + [act] * 6
-        + [half, half, act, act, act, arr(2 * t, 3 * H, dtype=BF16), arr(2, t, H, dtype=BF16)]
+        + [half, half, act, act, act, arr(2 * t, 3 * H, dtype=BF16), arr(2, t, H, dtype=BF16), arr(t // 2, H, dtype=BF16)]
         + [arr(2, 4, SUB, H)],
         scratch_shapes=[
+            pltpu.VMEM((layers, per, 3 * d), BF16),
+            pltpu.VMEM((layers, 2, parts, 2, per, HALF), BF16),
             pltpu.VMEM((2, t, d), BF16),
             pltpu.VMEM((2, t, H), BF16),
             pltpu.VMEM((2, 8, LANE), F32),
@@ -758,17 +783,17 @@
             dma((count,)),
             dma((count,)),
             dma((2, 2)),
-            dma((7,)),
-            dma((7,)),
+            dma((8,)),
+            dma((8,)),
             dma((3, Z // 2 * X)),
             dma((3, Z // 2 * X)),
-            dma((10,)),
+            dma((11,)),
         ],
         compiler_params=pltpu.CompilerParams(
             collective_id=0, has_side_effects=True, vmem_limit_bytes=62 << 20
         ),
         name="forward_all",
-    )(tok, cot, keep, vin, w_own)
+    )(tok, cot, keep, vin, weight)
 
 
 def wrap(a, b):
@@ -967,7 +992,7 @@
 
 def backward_all(
     seq, row, w_all, vec, keep, stats_all, f0, g0, cand0, p0, r0, u0, low0, low1, u1, dhr1, dn1, du1,
-    res1, sums1, tok,
+    res1, resx, sums1, tok,
     grad, input_grad, result, vout,
     stats, wbuf, du, low, dn, dnsend, dnrecv, hsend, hrecv, tokx, u, dhr, stream, proj,
     keep0, send0, recv0, keep1, send1, recv1, keep2, send2, recv2, keep3, send3, recv3, done,
@@ -1034,10 +1059,13 @@
         return pair(4, hsend, hrecv)
 
     def results(cols):
-        return pair(5, res1.at[1 - zl], result.at[:, cols])
+        rows = pl.ds(t // 2, t // 2)
+        return pair(5, res1.at[1 - zl, rows], result.at[rows, cols])
 
     own_result = load(5, res1.at[zl], result.at[:, own])
     own_result.start()
+    got_result = load(8, resx, result.at[pl.ds(0, t // 2), other])
+    got_result.start()
     results(own).start()
     across = (((1,), (1,)), ((), ()))
 
@@ -1209,7 +1237,7 @@
             return scale * decay, decay * q + term
 
         start = jnp.ones((SUB, WIDE), F32), jnp.zeros((SUB, WIDE), F32)
-        scale, q = lax.fori_loop(0, steps, one, start, unroll=8)
+        scale, q = lax.fori_loop(0, steps, one, start, unroll=16)
         ends[b, 0, :, cols] = scale
         ends[b, 1, :, cols] = q
 
@@ -1248,7 +1276,7 @@
             )
 
         zero = jnp.zeros((SUB, WIDE), F32)
-        carry = lax.fori_loop(0, steps, one, (first[b, :, cols], zero, zero, zero, zero), unroll=4)
+        carry = lax.fori_loop(0, steps, one, (first[b, :, cols], zero, zero, zero, zero), unroll=16)
         for k in range(4):
             sums[0, 2 + k, :, cols] += carry[k + 1]
         for h in range(2):
@@ -1317,35 +1345,36 @@
             theirs(0, 1 - zl)
             begin(weights(0, zl))
 
+        for e in range(2):
+            pl.when(k == parts + e)(lambda: scatter.turn(1, 0, 0, e))
+
+    scatter.written(1)
+    get_low.wait()
     tiles(down_work, between)
     end(weights(0, zl))
     theirs(1, 1 - zl, dn.at[1 - zl])
-    scatter.written(1)
-    get_low.wait()
 
     def first_layer(k, _):
         scatter.turn(1, 0, k, 0)
 
-        @pl.when(k < blocks)
+        @pl.when(k == 1)
         def _():
-            ours(zl, zl, k)
-
-        @pl.when(k == blocks - 1)
-        def _():
+            ours(zl, zl, 0)
+            ours(zl, zl, 1)
             begin(weights(0, 1 - zl))
 
-        @pl.when(k == blocks)
+        @pl.when(k == 2)
         def _():
             end(weights(0, 1 - zl))
 
-        @pl.when(k >= blocks)
+        @pl.when(k > 1)
         def _():
-            ours(1 - zl, zl, k - blocks, True)
+            ours(1 - zl, zl, k - 2, True)
 
         scatter.turn(1, 0, k, 1)
         return 0
 
-    lax.fori_loop(0, parts, first_layer, 0)
+    lax.fori_loop(1, parts, first_layer, 0)
     late(1, 0, 0)
     late(1, 0, 1)
     for b in range(2):
@@ -1421,6 +1450,7 @@
     carried().wait_send()
     end([out_own, out_other])
     own_result.wait()
+    got_result.wait()
     results(own).wait_send()
     results(other).wait_recv()
 
@@ -1444,7 +1474,7 @@
 
     return pl.pallas_call(
         lambda *refs: backward_all(seq, row, *refs),
-        in_specs=[hbm, vmem, vmem] + [hbm] * 14 + [vmem, hbm],
+        in_specs=[hbm, vmem, vmem] + [hbm] * 15 + [vmem, hbm],
         out_specs=[hbm, hbm, hbm, vmem],
         out_shape=[arr(layers, per, 3 * d)] + [arr(t, d, dtype=BF16)] * 2 + [arr(16, LANE)],
         scratch_shapes=[
@@ -1478,7 +1508,7 @@
             dma((6,)), dma((6,)),
             dma((Z // 2 * X,)), dma((Z // 2 * X,)),
             dma((count,)), dma((count,)),
-            dma((8,)),
+            dma((9,)),
             dma((2, 5)),
             dma((2 * parts,)),
         ],
@@ -1494,8 +1524,6 @@
     layers = weight.shape[0]
     steps = t // SUB
     seq, row = lax.axis_size("seq"), lax.axis_size("row")
-    H = d // 2
-    parts = H // WIDE
 
     def permuted(v):
         return v.reshape(SUB, steps, -1).transpose(1, 0, 2).reshape(t, -1)
@@ -1506,12 +1534,12 @@
     keep = permuted((1 - resets[0]).astype(F32)[:, None]).reshape(t // LANE, LANE)
     keep = jnp.pad(keep, ((0, 8 - t // LANE), (0, 0)))
     per = rows[0].shape[-1]
-    packed = jnp.stack(rows + (jnp.zeros_like(rows[0]),) * 2, axis=1).reshape(2 * 8, per)
-    packed = jnp.pad(packed, ((0, 0), (0, LANE - per)))
-    local = weight.reshape(layers, per, 3, 2, parts, 2, LANE).transpose(0, 3, 4, 5, 1, 2, 6)
-    local = local.reshape(layers, 2, parts, 2, per, HALF)
+    blank = jnp.zeros((), BF16)
+    packed = sum(
+        lax.pad(v, blank, ((k, 7 - k, 7), (0, LANE - per, 0))) for k, v in enumerate(rows)
+    )
     out = call_forward(
-        seq, row, permuted(tokens[0]), permuted(cotangent[0]), keep, packed, local
+        seq, row, permuted(tokens[0]), permuted(cotangent[0]), keep, packed, weight
     )
     grad, input_grad, result, vectors = call_backward(seq, row, t, d, tuple(out) + (permuted(tokens[0]),))
     return (restored(result), restored(input_grad), grad) + tuple(

time: 479 us -> 456 us (0.952)
  Pallas kernels: 443 us -> 431 us
  local copies, waits for them, and re-layouts: 30.3 us -> 19.8 us
    pallas_call x1, Pallas kernels: 225 us -> 214 us  [call_backward(): pl.pallas_call(lambda *refs: backward_all(seq, row, *refs), in_specs=[hbm...]
    reshape x3 -> x0, local copies, waits for them, and re-layouts: 9.95 us -> none  [the longest x2 7.43 us: body(): weight.reshape(layers, per, 3, 2, parts, 2, LANE)]
where the time goes in v6:
time: 456 us
  Pallas kernels  431 us (95%)
  local copies, waits for them, and re-layouts  19.8 us (4%)
  other arithmetic  4.71 us (1%)
    pallas_call x1, Pallas kernels, call_forward(): pl.pallas_call(lambda *refs: forward_all(seq, row, *refs), in_specs=[hbm,...  217 us
    pallas_call x1, Pallas kernels, call_backward(): pl.pallas_call(lambda *refs: backward_all(seq, row, *refs), in_specs=[hbm...  214 us

profile of v6, /device:TPU:0, one launch (start us, length us, event | category | flops | bytes accessed | tf_op | source)
XLA Modules:
  0.0 456.1 jit_solution(4048934365453933486)
XLA Ops:
  0.6 0.7 convert_reduce_fusion
  1.3 0.1 convert_element_type.16
  1.4 0.7 pad.23
  2.1 0.7 pad.24
  2.8 0.7 pad.25
  3.4 0.7 pad.26
  4.1 0.7 pad.27
  4.8 0.7 pad.28
  5.5 0.6 add_add_fusion.refs_3_
  6.1 0.1 copy.26
  6.1 0.1 reshape_reshape.3
  6.2 0.6 pad.22.refs_2_
  6.8 6.5 %copy_bitcast_fusion = (bf16[512,2048]{1,0:T(8,128)(2,1)}, bf16[512,2048]{1,0:T(8,128)(2,1)}) fusion(bf16[8,64,2048]{2,1,0:T(8,128)(2,1)} %bitcast.25, bf16[8,64,2048]{2,1,0:T(8,128)(2,1)} %bitcast.26), kind=kLoop, calls=%fused_computation | loop fusion | bytes 8388608 | tf_op jit(solution)/shard_map/reshape | solution.py:1529
  13.4 216.9 %forward_all.1 = (bf16[2,4,2,4,2,2,2,64,384]{8,7,6,5,4,3,2,1,0:T(8,128)(2,1)}, f32[2,8,2048]{2,1,0:T(8,128)}, f32[2,64,8,128]{3,2,1,0:T(8,128)}, f32[2,2,2,64,8,...) custom-call(bf16[512,2048]{1,0:T(8,128)(2,1)} %get-tuple-element.68., ...), custom_call_target="tpu_custom_call" | custom-call | tf_op jit(solution)/shard_map/forward_all/pallas_call | solution.py:749
  230.3 214.0 %backward_all.1 = (f32[2,64,6144]{2,1,0:T(8,128)}, bf16[512,2048]{1,0:T(8,128)(2,1)}, bf16[512,2048]{1,0:T(8,128)(2,1)}, f32[16,128]{1,0:T(8,128)}) custom-call(bf16[2,4,2,4,2,2,2,64,384]{8,7,6,5,4,3,2,1,0:T(8,128)(2,1)} %get-tuple-element.32.refs_0_, f32[2,8,2048]{2,1,0:T(8,128)} %get-tuple-element.33.refs_1_, f32[2,64,8,128]{3,2,1,0:T(8,128)} %get-tuple-element.34.refs_2_, ...), custom_call_target="tpu_custom_call" | custom-call | tf_op jit(solution)/shard_map/backward_all/pallas_call | solution.py:1475
  444.3 4.2 copy.27
  448.5 2.5 copy.28
  451.0 0.6 pad_maximum_fusion.5
  451.5 0.6 pad_maximum_fusion.4
  452.1 0.6 pad_maximum_fusion.3
  452.7 0.6 pad_maximum_fusion.2
  453.3 0.6 pad_maximum_fusion.1
  453.8 0.6 pad_maximum_fusion
  454.4 1.7 copy.32
  (7 shorter events, 0.0 us)
Async XLA Ops:
  444.3 4.2 copy-start.1
  448.5 2.5 copy-start.2
  448.5 5.9 %copy-start = (f32[2,64,6144]{2,1,0:T(8,128)S(1)}, f32[2,64,6144]{2,1,0:T(8,128)}, u32[]{:S(2)}) copy-start(f32[2,64,6144]{2,1,0:T(8,128)} %get-tuple-element.80) | copy-start | bytes 9437188

commit v7 on v6

--- a/solution.py
+++ b/solution.py
@@ -243,9 +243,9 @@
 
 
 def forward_all(
-    seq, row, tok, cot, keep_in, vin, weight,
-    w_all, vec, keep, stats, f0, g0, cand0, p0, r0, u0, low0, low1, u1, dhr1, dn1, du1, res1, resx,
-    sums, w_nat, w_own, tokbuf, cotbuf, keepc, vall, u, np_, f, g, cand, rpre, low, wbuf, proj, du, resbuf, top_of, ends,
+    seq, row, tok, cot, resets, gain_in, shift_in, fpeep_in, rpeep_in, fbias_in, rbias_in, weight,
+    w_all, vec, keep, stats, f0, g0, cand0, p0, r0, u0, low0, low1, u1, dhr1, dn1, du1, res1, resx, tokx0,
+    sums, nat, w_nat, w_own, tokbuf, cotbuf, keepc, vall, u, np_, f, g, cand, rpre, low, wbuf, proj, du, resbuf, top_of, ends,
     first, tables, st_own, st_got, st_fin,
     gsnd, grcv, gloc, vsnd, vrcv, wsem, psnd, prcv, csnd, crcv, outs,
 ):
@@ -280,10 +280,30 @@
         return remote(src, dst, psnd.at[k], prcv.at[k], partner)
 
     def tokens(b):
-        return pair(0, tok, tokbuf.at[b])
+        return pair(0, tokbuf.at[b], tokbuf.at[b])
 
     def cotangents(b):
-        return pair(1, cot.at[:, other], cotbuf.at[b])
+        return pair(1, du.at[t : 2 * t, d : d + H], cotbuf.at[b])
+
+    def permute(src, store):
+        group = nat.shape[0]
+        for q in range(d // LANE // group):
+            for k in range(group):
+                at_lanes = (q * group + k) * LANE
+                nat[k] = src[:, at_lanes : at_lanes + LANE].astype(F32)
+
+            def one(k, _):
+                rows = [
+                    jnp.concatenate(
+                        [nat[e, pl.ds(2 * k + j, SUB, stride=steps), :] for e in range(group)], axis=-1
+                    )
+                    for j in range(2)
+                ]
+                spot = pl.ds(pl.multiple_of(2 * SUB * k, 2 * SUB), 2 * SUB)
+                store(spot, q, jnp.concatenate(rows, axis=0).astype(BF16))
+                return 0
+
+            lax.fori_loop(0, steps // 2, one, 0, unroll=4)
 
     def keeps(b):
         return pair(2, keepc.at[b], keepc.at[b])
@@ -314,10 +334,21 @@
             for copy in vcopies(stage, False):
                 copy.start()
 
-    own_tokens = pltpu.make_async_copy(tok, tokbuf.at[zl], outs.at[0])
-    own_cot = pltpu.make_async_copy(cot.at[:, own], cotbuf.at[zl], outs.at[1])
-    vall[z, x, y, c] = vin[...]
-    keepc[zl] = keep_in[...]
+    own_tokens = pltpu.make_async_copy(tok, du.at[0:t, 0:d], outs.at[0])
+    own_cot = pltpu.make_async_copy(cot, du.at[t : 2 * t, 0:d], outs.at[1])
+    given = [
+        v[...].astype(F32) for v in (gain_in, shift_in, fpeep_in, rpeep_in, fbias_in, rbias_in)
+    ]
+    per = given[0].shape[-1]
+    blank = jnp.zeros((2, per), F32)
+    given = jnp.concatenate(
+        [v[l : l + 1] for l in range(2) for v in given + [blank] * 2], axis=0
+    )
+    given = jnp.concatenate([given, jnp.zeros((16, LANE - per), F32)], axis=-1)
+    vall[z, x, y, c] = given.astype(BF16)
+    kept = 1.0 - resets[...].astype(F32)
+    kept = jnp.concatenate([kept[:, k * steps : (k + 1) * steps] for k in range(SUB)], axis=0)
+    keepc[zl] = jnp.concatenate([kept, jnp.zeros((SUB, LANE - steps), F32)], axis=-1)
     own_tokens.start()
     own_cot.start()
     for copy in vcopies(0, False):
@@ -328,6 +359,13 @@
     gather.begin(2)
     gather.begin(3)
     vadvance(1)
+    own_tokens.wait()
+    wide = nat.shape[0] * LANE
+
+    def store_tokens(rows, q, v):
+        tokbuf[zl, rows, q * wide : (q + 1) * wide] = v
+
+    permute(du.at[0:t, 0:d], store_tokens)
     gather.turn(0)
     vadvance(2)
     vadvance(3)
@@ -347,9 +385,9 @@
             vec[l, :, q * LANE : (q + 1) * LANE] = value[l * 8 : l * 8 + 8]
     keeps(1 - zl).wait_recv()
     for b in range(2):
-        for q in range(t // LANE):
-            piece = spread_rows(to_column(keepc[b, q : q + 1, :]))
-            keep[b, q * (LANE // SUB) : (q + 1) * (LANE // SUB)] = piece
+        kept = keepc[b]
+        for i in range(steps):
+            keep[b, i] = jnp.broadcast_to(kept[:, i : i + 1], (SUB, LANE))
 
     def norm0(b):
         piece = 8
@@ -427,11 +465,27 @@
     def stash(k, src, dst):
         return pltpu.make_async_copy(src, dst, outs.at[k])
 
-    own_tokens.wait()
     norm0(zl)
+    own_cot.wait()
+
+    def store_cot(rows, q, v):
+        side, at_lanes = q * wide // H, q * wide % H
+
+        @pl.when(zl == side)
+        def _():
+            cotbuf[zl, rows, at_lanes : at_lanes + wide] = v
+
+        @pl.when(zl != side)
+        def _():
+            to = pl.ds(pl.multiple_of(rows.start + t, 2 * SUB), 2 * SUB)
+            du[to, d + at_lanes : d + at_lanes + wide] = v
 
     def turn(i, _):
         gather.turn(i)
+
+        @pl.when(i == 3)
+        def _():
+            permute(du.at[t : 2 * t, 0:d], store_cot)
 
         @pl.when(i >= 3)
         def _():
@@ -480,6 +534,8 @@
         return 0
 
     lax.fori_loop(2, parts + 3, turn, 0)
+    keep_tokx = stash(0, tokbuf.at[zl, :, other], tokx0)
+    keep_tokx.start()
     keep_u0, keep_low0 = stash(2, u, u0), stash(3, low, low0)
     gates0 = [stash(4, f, f0), stash(5, g, g0), stash(6, cand, cand0)]
     for copy in [keep_u0, keep_low0] + gates0:
@@ -589,7 +645,6 @@
     keep_low1.start()
     chains[1].run(ends, first, False)
     keep_p0.wait()
-    own_cot.wait()
 
     def step_back(b, i, cols, top, peep):
         before, gate, up = np_[b, i, :, cols], rpre[b, i, :, cols], f[b, i, :, cols]
@@ -699,6 +754,7 @@
         lax.fori_loop(0, parts, tile, 0)
 
     keep_low1.wait()
+    cotangents(zl).wait_send()
 
     def last(b):
         yield stash(3, du.at[rows_of(b)], du1.at[rows_of(b)])
@@ -717,19 +773,18 @@
     for stage in range(4):
         for copy in vcopies(stage, False):
             copy.wait_send()
-    for copy in list(last(1)) + [keep_u1, keep_res]:
+    for copy in list(last(1)) + [keep_u1, keep_res, keep_tokx]:
         copy.wait()
     results().wait_recv()
     results().wait_send()
     tokens(zl).wait_send()
-    cotangents(zl).wait_send()
     keeps(zl).wait_send()
     for b in range(2):
         statistics(b, st_got).wait_send()
         lows(b, own).wait_send()
 
 
-def call_forward(seq, row, tok, cot, keep, vin, weight):
+def call_forward(seq, row, tok, cot, keep, rows, weight):
     t, d = tok.shape
     layers, per, _ = weight.shape
     Y = row // 2
@@ -748,8 +803,8 @@
     st = pltpu.VMEM((2, 8, LANE), F32)
     return pl.pallas_call(
         lambda *refs: forward_all(seq, row, *refs),
-        in_specs=[hbm, hbm, vmem, vmem, hbm],
-        out_specs=[hbm, vmem, vmem, vmem] + [hbm] * 14 + [vmem],
+        in_specs=[hbm, hbm] + [vmem] * (1 + len(rows)) + [hbm],
+        out_specs=[hbm, vmem, vmem, vmem] + [hbm] * 15 + [vmem],
         out_shape=[
             arr(layers, parts, 2, Z, X, Y, 2, per, HALF, dtype=BF16),
             arr(2, 8, d),
@@ -757,9 +812,10 @@
             arr(2, 2, 2, steps, SUB, LANE),
         ]
         + [act] * 6
-        + [half, half, act, act, act, arr(2 * t, 3 * H, dtype=BF16), arr(2, t, H, dtype=BF16), arr(t // 2, H, dtype=BF16)]
+        + [half, half, act, act, act, arr(2 * t, 3 * H, dtype=BF16), arr(2, t, H, dtype=BF16), arr(t // 2, H, dtype=BF16), arr(t, H, dtype=BF16)]
         + [arr(2, 4, SUB, H)],
         scratch_shapes=[
+            pltpu.VMEM((4, t, LANE), F32),
             pltpu.VMEM((layers, per, 3 * d), BF16),
             pltpu.VMEM((layers, 2, parts, 2, per, HALF), BF16),
             pltpu.VMEM((2, t, d), BF16),
@@ -793,7 +849,7 @@
             collective_id=0, has_side_effects=True, vmem_limit_bytes=62 << 20
         ),
         name="forward_all",
-    )(tok, cot, keep, vin, weight)
+    )(tok, cot, keep, *rows, weight)
 
 
 def wrap(a, b):
@@ -992,8 +1048,8 @@
 
 def backward_all(
     seq, row, w_all, vec, keep, stats_all, f0, g0, cand0, p0, r0, u0, low0, low1, u1, dhr1, dn1, du1,
-    res1, resx, sums1, tok,
-    grad, input_grad, result, vout,
+    res1, resx, tok, sums1,
+    grad, input_grad, result, vo0, vo1, vo2, vo3, vo4, vo5,
     stats, wbuf, du, low, dn, dnsend, dnrecv, hsend, hrecv, tokx, u, dhr, stream, proj,
     keep0, send0, recv0, keep1, send1, recv1, keep2, send2, recv2, keep3, send3, recv3, done,
     ends, first, table, b_own, b_got, b_fin, sums, sumsx, vbuf, vr0, vr1, vr2, vr3,
@@ -1011,7 +1067,6 @@
     own = pl.ds(pl.multiple_of(zl * H, H), H)
     other = pl.ds(pl.multiple_of((1 - zl) * H, H), H)
     rows_of = lambda b: pl.ds(pl.multiple_of(b * t, t), t)
-    pos.barrier(seq)
 
     def load(k, src, dst):
         return pltpu.make_async_copy(src, dst, ins.at[k])
@@ -1037,9 +1092,10 @@
 
     get_du, get_low, get_dn = load(0, du1, du), load(1, low1, low), load(2, dn1, dn)
     get_u, get_dhr = load(3, u1, u), load(4, dhr1, dhr)
+    get_stats = load(6, stats_all.at[1], stats)
+    get_du.start()
     begin(weights(1, 1 - zl))
-    get_stats = load(6, stats_all.at[1], stats)
-    begin([get_du, get_low, get_dn, get_u, get_dhr, get_stats])
+    pos.barrier(seq)
     scatter = Scatter(
         pos, 2 * parts, low, du, grad, (keep0, keep1, keep2, keep3), (send0, send1, send2, send3),
         (recv0, recv1, recv2, recv3), done, snd, rcv, gouts,
@@ -1293,9 +1349,11 @@
     sums[1, 2:6] = sums1[0] + sums1[1]
     get_du.wait()
     end(weights(1, 1 - zl))
+    begin([get_low, get_dn])
     for b in range(2):
         theirs(b, b)
     begin(weights(1, zl))
+    begin([get_u, get_dhr, get_stats])
     get_low.wait()
     get_dn.wait()
 
@@ -1323,7 +1381,7 @@
     norm_back(1, 0)
     norm_back(1, 1)
     get_u, get_stats = load(3, u0, u), load(6, stats_all.at[0], stats)
-    get_tok = load(7, tok.at[:, other], tokx)
+    get_tok = load(7, tok, tokx)
     begin([get_u, get_stats, get_tok])
     late(0, 1, 1)
     get_u.wait()
@@ -1441,7 +1499,9 @@
     vtake(2)
     vstart(3)
     vtake(3)
-    vout[...] = vbuf[z, x, y, c]
+    mine = vbuf[z, x, y, c]
+    for k, out in enumerate((vo0, vo1, vo2, vo3, vo4, vo5)):
+        out[...] = jnp.concatenate([mine[l * 8 + k : l * 8 + k + 1, :per] for l in range(2)], axis=0)
     for stage in range(4):
         for k in pos.others("cxyz"[stage]):
             vcopy(stage, k).wait_send()
@@ -1474,9 +1534,9 @@
 
     return pl.pallas_call(
         lambda *refs: backward_all(seq, row, *refs),
-        in_specs=[hbm, vmem, vmem] + [hbm] * 15 + [vmem, hbm],
-        out_specs=[hbm, hbm, hbm, vmem],
-        out_shape=[arr(layers, per, 3 * d)] + [arr(t, d, dtype=BF16)] * 2 + [arr(16, LANE)],
+        in_specs=[hbm, vmem, vmem] + [hbm] * 16 + [vmem],
+        out_specs=[hbm, hbm, hbm] + [vmem] * 6,
+        out_shape=[arr(layers, per, 3 * d)] + [arr(t, d, dtype=BF16)] * 2 + [arr(layers, per)] * 6,
         scratch_shapes=[
             buf(2, 2, steps, SUB, LANE, dtype=F32),
             buf(Z // 2, X, Y, 2, per, 3 * H),
@@ -1525,26 +1585,14 @@
     steps = t // SUB
     seq, row = lax.axis_size("seq"), lax.axis_size("row")
 
-    def permuted(v):
-        return v.reshape(SUB, steps, -1).transpose(1, 0, 2).reshape(t, -1)
-
     def restored(v):
         return v.reshape(steps, SUB, d).transpose(1, 0, 2).reshape(1, t, d)
 
-    keep = permuted((1 - resets[0]).astype(F32)[:, None]).reshape(t // LANE, LANE)
-    keep = jnp.pad(keep, ((0, 8 - t // LANE), (0, 0)))
-    per = rows[0].shape[-1]
-    blank = jnp.zeros((), BF16)
-    packed = sum(
-        lax.pad(v, blank, ((k, 7 - k, 7), (0, LANE - per, 0))) for k, v in enumerate(rows)
+    out = call_forward(
+        seq, row, tokens[0], cotangent[0], resets, rows, weight
     )
-    out = call_forward(
-        seq, row, permuted(tokens[0]), permuted(cotangent[0]), keep, packed, weight
-    )
-    grad, input_grad, result, vectors = call_backward(seq, row, t, d, tuple(out) + (permuted(tokens[0]),))
-    return (restored(result), restored(input_grad), grad) + tuple(
-        jnp.stack([vectors[l * 8 + k, :per] for l in range(layers)]) for k in range(6)
-    )
+    grad, input_grad, result, *vectors = call_backward(seq, row, t, d, out)
+    return (restored(result), restored(input_grad), grad) + tuple(vectors)
 
 
 def solution(mesh):

time: 456 us -> 444 us (0.974)
  local copies, waits for them, and re-layouts: 19.8 us -> 11.8 us
  other arithmetic: 4.71 us -> 0 us
    reshape x1 -> x0, local copies, waits for them, and re-layouts: 6.53 us -> none  [permuted(): return v.reshape(SUB, steps, -1).transpose(1, 0, 2).reshape(t, -1)]
    pad x7 -> x0, local copies, waits for them, and re-layouts: 4.64 us -> none  [the longest x6 4.04 us: body(): lax.pad(v, blank, ((k, 7 - k, 7), (0, LANE - per, 0)))]
where the time goes in v7:
time: 444 us
  Pallas kernels  431 us (97%)
  local copies, waits for them, and re-layouts  11.8 us (3%)
    pallas_call x1, Pallas kernels, call_forward(): pl.pallas_call(lambda *refs: forward_all(seq, row, *refs), in_specs=[hbm,...  218 us
    pallas_call x1, Pallas kernels, call_backward(): pl.pallas_call(lambda *refs: backward_all(seq, row, *refs), in_specs=[hbm...  213 us

profile of v7, /device:TPU:0, one launch (start us, length us, event | category | flops | bytes accessed | tf_op | source)
XLA Modules:
  0.0 443.8 jit_solution(8657195395100781475)
XLA Ops:
  0.6 218.0 %forward_all.1 = (bf16[2,4,2,4,2,2,2,64,384]{8,7,6,5,4,3,2,1,0:T(8,128)(2,1)}, f32[2,8,2048]{2,1,0:T(8,128)}, f32[2,64,8,128]{3,2,1,0:T(8,128)}, f32[2,2,2,64,8,...) custom-call(bf16[512,2048]{1,0:T(8,128)(2,1)} %bitcast.14, ...), custom_call_target="tpu_custom_call" | custom-call | tf_op jit(solution)/shard_map/forward_all/pallas_call | solution.py:804
  218.7 213.3 %backward_all.1 = (f32[2,64,6144]{2,1,0:T(8,128)}, bf16[512,2048]{1,0:T(8,128)(2,1)}, bf16[512,2048]{1,0:T(8,128)(2,1)}, f32[2,64]{1,0:T(2,128)}, f32[2,64]{1,0:...) custom-call(bf16[2,4,2,4,2,2,2,64,384]{8,7,6,5,4,3,2,1,0:T(8,128)(2,1)} %get-tuple-element.38.r, ...), custom_call_target="tpu_custom_call" | custom-call | tf_op jit(solution)/shard_map/backward_all/pallas_call | solution.py:1535
  432.0 0.0 copy-start.1
  432.0 0.0 copy-start
  432.0 4.2 copy.19
  436.2 0.0 copy-done.1
  436.2 2.5 copy.20
  438.7 0.0 copy-start.7
  438.7 0.0 copy-start.3
  438.7 0.0 copy-start.2
  438.7 0.0 copy-done
  438.7 1.7 copy.28
  440.4 0.0 copy-done.7
  440.4 0.6 copy.29
  441.0 0.0 copy-done.6
  441.0 0.6 copy.30
  441.5 0.0 copy-done.5
  441.5 0.6 copy.31
  442.1 0.0 copy-done.4
  442.1 0.6 copy.32
  442.7 0.0 copy-done.3
  442.7 0.6 copy.33
  443.2 0.0 copy-done.2
  443.2 0.6 copy.34
  (3 shorter events, 0.0 us)
Async XLA Ops:
  432.0 4.2 copy-start.1
  432.0 6.7 %copy-start = (f32[2,64,6144]{2,1,0:T(8,128)S(1)}, f32[2,64,6144]{2,1,0:T(8,128)}, u32[]{:S(2)}) copy-start(f32[2,64,6144]{2,1,0:T(8,128)} %get-tuple-element.78) | copy-start | bytes 9437188
  438.7 1.7 copy-start.7
  438.7 2.3 copy-start.6
  438.7 2.8 copy-start.5
  438.7 3.4 copy-start.4
  438.7 4.0 copy-start.3
  438.7 4.5 %copy-start.2 = (f32[2,64]{1,0:T(2,128)S(1)}, f32[2,64]{1,0:T(2,128)}, u32[]{:S(2)}) copy-start(f32[2,64]{1,0:T(2,128)} %get-tuple-element.84) | copy-start | bytes 1540

commit v8 on v7

--- a/solution.py
+++ b/solution.py
@@ -1122,7 +1122,6 @@
     own_result.start()
     got_result = load(8, resx, result.at[pl.ds(0, t // 2), other])
     got_result.start()
-    results(own).start()
     across = (((1,), (1,)), ((), ()))
 
     n = t2 // parts
@@ -1380,6 +1379,7 @@
     late(0, 1, 0)
     norm_back(1, 0)
     norm_back(1, 1)
+    results(own).start()
     get_u, get_stats = load(3, u0, u), load(6, stats_all.at[0], stats)
     get_tok = load(7, tok, tokx)
     begin([get_u, get_stats, get_tok])
@@ -1390,8 +1390,6 @@
     tiles(ends_work, send_carried)
     late(0, 1, 3)
     chain.run(ends, first, True)
-    for k in range(4, 7):
-        late(0, 1, k)
     for b in range(2):
         partial_sums(b).wait_send()
         statistics(b).wait_send()
@@ -1403,12 +1401,14 @@
             theirs(0, 1 - zl)
             begin(weights(0, zl))
 
+        for e in range(3):
+            pl.when(k == e)(lambda: late(0, 1, 4 + e))
         for e in range(2):
             pl.when(k == parts + e)(lambda: scatter.turn(1, 0, 0, e))
 
-    scatter.written(1)
     get_low.wait()
     tiles(down_work, between)
+    scatter.written(1)
     end(weights(0, zl))
     theirs(1, 1 - zl, dn.at[1 - zl])
 

time: 444 us -> 440 us (level)
  no operation moved by 1% of the time
where the time goes in v8:
time: 440 us
  Pallas kernels  427 us (97%)
  local copies, waits for them, and re-layouts  11.8 us (3%)
    pallas_call x1, Pallas kernels, call_forward(): pl.pallas_call(lambda *refs: forward_all(seq, row, *refs), in_specs=[hbm,...  218 us
    pallas_call x1, Pallas kernels, call_backward(): pl.pallas_call(lambda *refs: backward_all(seq, row, *refs), in_specs=[hbm...  209 us

profile of v8, /device:TPU:0, one launch (start us, length us, event | category | flops | bytes accessed | tf_op | source)
XLA Modules:
  0.0 439.7 jit_solution(4980513294657470076)
XLA Ops:
  0.6 218.0 %forward_all.1 = (bf16[2,4,2,4,2,2,2,64,384]{8,7,6,5,4,3,2,1,0:T(8,128)(2,1)}, f32[2,8,2048]{2,1,0:T(8,128)}, f32[2,64,8,128]{3,2,1,0:T(8,128)}, f32[2,2,2,64,8,...) custom-call(bf16[512,2048]{1,0:T(8,128)(2,1)} %bitcast.14, ...), custom_call_target="tpu_custom_call" | custom-call | tf_op jit(solution)/shard_map/forward_all/pallas_call | solution.py:804
  218.7 209.2 %backward_all.1 = (f32[2,64,6144]{2,1,0:T(8,128)}, bf16[512,2048]{1,0:T(8,128)(2,1)}, bf16[512,2048]{1,0:T(8,128)(2,1)}, f32[2,64]{1,0:T(2,128)}, f32[2,64]{1,0:...) custom-call(bf16[2,4,2,4,2,2,2,64,384]{8,7,6,5,4,3,2,1,0:T(8,128)(2,1)} %get-tuple-element.38.r, ...), custom_call_target="tpu_custom_call" | custom-call | tf_op jit(solution)/shard_map/backward_all/pallas_call | solution.py:1535
  427.9 0.0 copy-start.1
  427.9 0.0 copy-start
  427.9 4.2 copy.19
  432.1 0.0 copy-done.1
  432.1 2.5 copy.20
  434.6 0.0 copy-start.7
  434.6 0.0 copy-start.3
  434.6 0.0 copy-start.2
  434.6 0.0 copy-done
  434.6 1.7 copy.28
  436.3 0.0 copy-done.7
  436.3 0.6 copy.29
  436.9 0.0 copy-done.6
  436.9 0.6 copy.30
  437.4 0.0 copy-done.5
  437.4 0.6 copy.31
  438.0 0.0 copy-done.4
  438.0 0.6 copy.32
  438.6 0.0 copy-done.3
  438.6 0.6 copy.33
  439.1 0.0 copy-done.2
  439.1 0.6 copy.34
  (3 shorter events, 0.0 us)
Async XLA Ops:
  427.9 4.2 copy-start.1
  427.9 6.7 %copy-start = (f32[2,64,6144]{2,1,0:T(8,128)S(1)}, f32[2,64,6144]{2,1,0:T(8,128)}, u32[]{:S(2)}) copy-start(f32[2,64,6144]{2,1,0:T(8,128)} %get-tuple-element.78) | copy-start | bytes 9437188
  434.6 1.7 copy-start.7
  434.6 2.3 copy-start.6
  434.6 2.8 copy-start.5
  434.6 3.4 copy-start.4
  434.6 4.0 copy-start.3
  434.6 4.5 %copy-start.2 = (f32[2,64]{1,0:T(2,128)S(1)}, f32[2,64]{1,0:T(2,128)}, u32[]{:S(2)}) copy-start(f32[2,64]{1,0:T(2,128)} %get-tuple-element.84) | copy-start | bytes 1540

commit v9 on v8

--- a/solution.py
+++ b/solution.py
@@ -1302,6 +1302,8 @@
 
     def send_carried(k):
         pl.when(k == parts - 1)(lambda: carried().start())
+        pl.when(k == 1)(lambda: late(0, 1, 2))
+        pl.when(k == parts + 1)(lambda: late(0, 1, 3))
 
     def down_work(slot, b, m, cols, wide):
         fpeep, rpeep, gain, shift = (row_wide(0, k, wide) for k in (FPEEP, RPEEP, GAIN, SHIFT))
@@ -1386,9 +1388,7 @@
     late(0, 1, 1)
     get_u.wait()
     get_stats.wait()
-    late(0, 1, 2)
     tiles(ends_work, send_carried)
-    late(0, 1, 3)
     chain.run(ends, first, True)
     for b in range(2):
         partial_sums(b).wait_send()

time: 440 us -> 440 us (level)
  no operation moved by 1% of the time
where the time goes in v9:
time: 440 us
  Pallas kernels  427 us (97%)
  local copies, waits for them, and re-layouts  11.8 us (3%)
    pallas_call x1, Pallas kernels, call_forward(): pl.pallas_call(lambda *refs: forward_all(seq, row, *refs), in_specs=[hbm,...  218 us
    pallas_call x1, Pallas kernels, call_backward(): pl.pallas_call(lambda *refs: backward_all(seq, row, *refs), in_specs=[hbm...  209 us

profile of v9, /device:TPU:0, one launch (start us, length us, event | category | flops | bytes accessed | tf_op | source)
XLA Modules:
  0.0 439.7 jit_solution(13428875554999432063)
XLA Ops:
  0.6 218.0 %forward_all.1 = (bf16[2,4,2,4,2,2,2,64,384]{8,7,6,5,4,3,2,1,0:T(8,128)(2,1)}, f32[2,8,2048]{2,1,0:T(8,128)}, f32[2,64,8,128]{3,2,1,0:T(8,128)}, f32[2,2,2,64,8,...) custom-call(bf16[512,2048]{1,0:T(8,128)(2,1)} %bitcast.14, ...), custom_call_target="tpu_custom_call" | custom-call | tf_op jit(solution)/shard_map/forward_all/pallas_call | solution.py:804
  218.7 209.2 %backward_all.1 = (f32[2,64,6144]{2,1,0:T(8,128)}, bf16[512,2048]{1,0:T(8,128)(2,1)}, bf16[512,2048]{1,0:T(8,128)(2,1)}, f32[2,64]{1,0:T(2,128)}, f32[2,64]{1,0:...) custom-call(bf16[2,4,2,4,2,2,2,64,384]{8,7,6,5,4,3,2,1,0:T(8,128)(2,1)} %get-tuple-element.38.r, ...), custom_call_target="tpu_custom_call" | custom-call | tf_op jit(solution)/shard_map/backward_all/pallas_call | solution.py:1535
  427.9 0.0 copy-start.1
  427.9 0.0 copy-start
  427.9 4.2 copy.19
  432.1 0.0 copy-done.1
  432.1 2.5 copy.20
  434.6 0.0 copy-start.7
  434.6 0.0 copy-start.3
  434.6 0.0 copy-start.2
  434.6 0.0 copy-done
  434.6 1.7 copy.28
  436.3 0.0 copy-done.7
  436.3 0.6 copy.29
  436.8 0.0 copy-done.6
  436.8 0.6 copy.30
  437.4 0.0 copy-done.5
  437.4 0.6 copy.31
  438.0 0.0 copy-done.4
  438.0 0.6 copy.32
  438.5 0.0 copy-done.3
  438.5 0.6 copy.33
  439.1 0.0 copy-done.2
  439.1 0.6 copy.34
  (3 shorter events, 0.0 us)
Async XLA Ops:
  427.9 4.2 copy-start.1
  427.9 6.7 %copy-start = (f32[2,64,6144]{2,1,0:T(8,128)S(1)}, f32[2,64,6144]{2,1,0:T(8,128)}, u32[]{:S(2)}) copy-start(f32[2,64,6144]{2,1,0:T(8,128)} %get-tuple-element.78) | copy-start | bytes 9437188
  434.6 1.7 copy-start.7
  434.6 2.3 copy-start.6
  434.6 2.8 copy-start.5
  434.6 3.4 copy-start.4
  434.6 4.0 copy-start.3
  434.6 4.5 %copy-start.2 = (f32[2,64]{1,0:T(2,128)S(1)}, f32[2,64]{1,0:T(2,128)}, u32[]{:S(2)}) copy-start(f32[2,64]{1,0:T(2,128)} %get-tuple-element.84) | copy-start | bytes 1540
